TPU v7x, 32 devices: a whole 2x2x4 slice. The times are simulated.
32 devices in a mesh: rows: 4 (over z), cols: 2 (over y), dp: 4 (over x, core).
Axes of the slice: x: 2, y: 2, z: 4, core: 2. Of those that a mesh axis runs over, the one named last changes fastest.
Arguments:
- features: bfloat16 [4, 32, 512, 256], P('dp', 'rows', 'cols'), may hold values from -340 to 340, as said below
- upstream: bfloat16 [4, 32, 512, 256], P('dp', 'rows', 'cols'), may hold values from -6 to 6
- conv_weight: bfloat16 [3, 3, 32, 256], replicated, may hold values from -0.375 to 0.375
- norm_gain: float32 [256], replicated, may hold values from 0.25 to 1.75
- norm_bias: float32 [256], replicated, may hold values from -3 to 3
Outputs:
- input_grad: bfloat16 [4, 32, 512, 256], P('dp', 'rows', 'cols')
- weight_grad: float32 [3, 3, 32, 256], replicated
- gain_grad: float32 [256], replicated
- bias_grad: float32 [256], replicated
Inputs may be any that keep to these rules, and one draw needn't show every extreme that they name: `features`: finite feature values.
All inputs are finite; a program needn't handle non-finite values.
Results may differ from a plain program's by a relative error of at most 0.0031.
Values may be sent and summed in bfloat16 or wider, within the bound.
No kernel may reach another device: no remote copies, remote signals or barrier semaphores. Data moves between devices by JAX's collectives and lax.ppermute only.
A program may use at most 128 MiB of HBM per device.

v0:
```python
import functools
import math

import jax
import jax.numpy as jnp
from jax import lax
from jax.experimental import pallas as pl
from jax.experimental.pallas import tpu as pltpu
from jax.sharding import PartitionSpec as P

C = 256
CHANNEL_GROUPS = 8
GS = 32
DILATION_RATE = 6
ITERS = 5
EPSILON = 1e-05

F32 = jnp.float32
BF16 = jnp.bfloat16
VMEM_SPEC = pl.BlockSpec(memory_space=pltpu.VMEM)


def run(body, out_shapes, operands, scratch=(), flops=0, after=()):
    many = isinstance(out_shapes, (tuple, list))
    count = len(operands)

    def kernel(*refs):
        body(*refs[:count], *refs[count + len(after) :])

    return pl.pallas_call(
        kernel,
        out_shape=out_shapes,
        in_specs=[VMEM_SPEC] * count + [pl.BlockSpec(memory_space=pl.ANY)] * len(after),
        out_specs=[VMEM_SPEC] * len(out_shapes) if many else VMEM_SPEC,
        scratch_shapes=list(scratch),
        compiler_params=pltpu.CompilerParams(vmem_limit_bytes=8 * 2**20),
        cost_estimate=pl.CostEstimate(flops=flops, bytes_accessed=2**20, transcendentals=0),
    )(*operands, *after)


TOKEN = jax.ShapeDtypeStruct((8, 128), F32)


def leave(token_ref):
    token_ref[...] = jnp.zeros(token_ref.shape, F32)


def same_group():
    rows = lax.broadcasted_iota(jnp.int32, (C, C), 0)
    columns = lax.broadcasted_iota(jnp.int32, (C, C), 1)
    return (rows >> 5) == (columns >> 5)


def fold(full, same):
    kept = jnp.where(same, full, 0.0)
    total = kept[0:GS]
    for g in range(1, CHANNEL_GROUPS):
        total = total + kept[g * GS : (g + 1) * GS]
    return total


def spread(packed, same):
    return jnp.where(same, jnp.concatenate([packed] * CHANNEL_GROUPS, axis=0), 0)


def split(value):
    high = value.astype(BF16)
    low = (value - high.astype(F32)).astype(BF16)
    return high, low


def spread_split(packed, same):
    high, low = split(spread(packed, same))
    return high, low


def dot(a, b):
    return jnp.dot(a, b, preferred_element_type=F32)


def times(left, right):
    rows = left.shape[0]
    left_high, left_low = split(left)
    right_high, right_low = right
    both = dot(jnp.concatenate([left_high, left_low], axis=0), right_high)
    return both[:rows] + both[rows:] + dot(left_high, right_low)


def unit():
    rows = lax.broadcasted_iota(jnp.int32, (GS, C), 0)
    columns = lax.broadcasted_iota(jnp.int32, (GS, C), 1)
    return jnp.where(rows == (columns & (GS - 1)), 1.0, 0.0)


def group_total(row, same):
    wide = jnp.broadcast_to(row, (8, C))
    return jnp.dot(wide, jnp.where(same, 1.0, 0.0), precision=lax.Precision.HIGHEST)


def stats_kernel(x_ref, out_ref):
    rows = x_ref.shape[0]
    cells = rows * x_ref.shape[1]
    same = same_group()

    def add_up(r, total):
        return total + jnp.sum(x_ref[r].astype(F32), axis=0, keepdims=True)

    mean = lax.fori_loop(0, rows, add_up, jnp.zeros((1, C), F32)) / cells

    def products(r, total):
        high, low = split(x_ref[r].astype(F32) - mean)
        return total + lax.dot_general(
            high,
            jnp.concatenate([high, low], axis=1),
            (((0,), (0,)), ((), ())),
            preferred_element_type=F32,
        )

    total = lax.fori_loop(0, rows, products, jnp.zeros((C, 2 * C), F32))
    cross = total[:, C:]
    out_ref[0:GS] = fold(total[:, :C] + cross + cross.T, same) / cells
    out_ref[GS : 2 * GS] = fold(jnp.broadcast_to(mean, (C, C)).T, same)
    out_ref[2 * GS : 2 * GS + 8] = jnp.broadcast_to(mean, (8, C))


def merge_kernel(a_ref, b_ref, out_ref):
    a, b = a_ref[...], b_ref[...]
    half = 0.5 * (a + b)
    gap = b - a
    wide = jnp.concatenate([gap[2 * GS :]] * (GS // 8), axis=0)
    out_ref[0:GS] = half[0:GS] + 0.25 * gap[GS : 2 * GS] * wide
    out_ref[GS:] = half[GS:]


def add_kernel(a_ref, b_ref, out_ref):
    out_ref[...] = a_ref[...] + b_ref[...]


def shift_band(moved_ref, bands_ref, e, middle, left, right):
    d, pad, width = DILATION_RATE, 16, middle.shape[0]
    bands_ref[pad : pad + width] = middle.astype(F32)
    bands_ref[pad - 8 : pad] = left.astype(F32)
    bands_ref[pad + width : pad + width + 8] = right.astype(F32)
    moved_ref[0, e] = bands_ref[pad + d : pad + d + width].astype(BF16)
    moved_ref[1, e] = middle
    moved_ref[2, e] = bands_ref[pad - d : pad - d + width].astype(BF16)


def tap_rows(moved_ref, weight_ref, taps):
    bands = [moved_ref[b, band] for a, band in taps for b in range(3)]
    taps = [a for a, _ in taps]
    weights = [weight_ref[3 * a + b] for a in taps for b in range(3)]
    return dot(jnp.concatenate(bands, axis=1), jnp.concatenate(weights, axis=0))


def pack_kernel(up_ref, left_ref, right_ref, odd_ref, first_ref, second_ref):
    rows, width = up_ref.shape[0], up_ref.shape[1]
    d = DILATION_RATE
    odd = odd_ref[0:1] > 0.5
    for r in range(d):
        for begin, size, ref in ((0, width, up_ref), (width, 8, left_ref), (width + 8, 8, right_ref)):
            top, bottom = ref[r].astype(F32), ref[rows - d + r].astype(F32)
            first_ref[r, begin : begin + size] = jnp.where(odd, top, bottom).astype(BF16)
            second_ref[r, begin : begin + size] = jnp.where(odd, bottom, top).astype(BF16)


def bands_kernel(up_ref, left_ref, right_ref, w_ref, moved_ref, weight_ref, token_ref, bands_ref):
    rows = up_ref.shape[0]
    same = same_group()
    for tap in range(9):
        tile = jnp.concatenate([w_ref[tap].astype(F32)] * CHANNEL_GROUPS, axis=0)
        weight_ref[tap] = jnp.where(same, tile, 0.0).T.astype(BF16)

    def inner(r, carry):
        shift_band(moved_ref, bands_ref, r, up_ref[r], left_ref[r], right_ref[r])
        return carry

    lax.fori_loop(0, rows, inner, 0)
    leave(token_ref)


def near_kernel(moved_ref, weight_ref, out_ref, token_ref):
    rows = out_ref.shape[0]
    d = DILATION_RATE
    for first, last, taps in ((0, rows - d, {0: d, 1: 0}), (rows - d, d, {1: 0}), (d, rows, {1: 0, 2: -d})):

        def row(r, carry, taps=taps):
            out_ref[r] = tap_rows(moved_ref, weight_ref, [(a, r + step) for a, step in taps.items()])
            return carry

        lax.fori_loop(first, last, row, 0)
    leave(token_ref)


def far_kernel(even_ref, odd_ref, first_ref, second_ref, weight_ref, near_ref, moved_ref, out_ref, token_ref, bands_ref):
    rows, width = out_ref.shape[0], out_ref.shape[1]
    d = DILATION_RATE

    def outer(r, carry):
        first, second = first_ref[r], second_ref[r]
        for begin, place in ((0, odd_ref), (d, even_ref)):
            halo = jnp.where(place[0:1] > 0.5, first.astype(F32), second.astype(F32)).astype(BF16)
            shift_band(
                moved_ref, bands_ref, begin + r, halo[0:width], halo[width : width + 8], halo[width + 8 :]
            )
        return carry

    lax.fori_loop(0, d, outer, 0)
    back = 2 * d - rows
    for first, last, taps in ((0, rows - d, {2: 0}), (rows - d, d, {0: back, 2: 0}), (d, rows, {0: back})):

        def row(r, carry, taps=taps):
            far = tap_rows(moved_ref, weight_ref, [(a, r + step) for a, step in taps.items()])
            out_ref[r] = near_ref[r] + far
            return carry

        lax.fori_loop(first, last, row, 0)
    leave(token_ref)


def act_kernel(x_ref, stats_ref, gain_ref, bias_ref, turned_ref, white_ref, slope_ref, kept_ref, mean_ref):
    rows, width = x_ref.shape[0], x_ref.shape[1]
    same = same_group()
    eye = unit()
    gain, bias = gain_ref[0:1], bias_ref[0:1]
    mean = stats_ref[2 * GS : 2 * GS + 1]
    cov = stats_ref[0:GS] + EPSILON * eye
    trace = group_total(jnp.sum(cov * eye, axis=0, keepdims=True), same)[0:1]
    normed = cov / trace
    normed_wide = spread_split(normed, same)
    iterate = 1.5 * eye - 0.5 * normed
    for k in range(ITERS - 1):
        wide = spread_split(iterate, same)
        square = times(iterate, wide)
        scaled = times(iterate, normed_wide)
        scaled_wide = spread_split(scaled, same)
        cube_scaled = times(square, scaled_wide)
        kept_ref[k, 0] = iterate
        kept_ref[k, 1] = square
        kept_ref[k, 2] = scaled
        iterate = 1.5 * iterate - 0.5 * cube_scaled
    whitener = iterate * lax.rsqrt(trace)
    mean_wide = jnp.broadcast_to(mean, (8, C))
    kept_ref[ITERS - 1, 0] = whitener
    kept_ref[ITERS - 1, 1] = normed
    kept_ref[ITERS - 1, 2] = jnp.broadcast_to(trace, (GS, C))
    mean_ref[...] = mean_wide
    white_high, white_low = spread_split(whitener, same)
    rounded = white_high.astype(F32) + white_low.astype(F32)
    offset = jnp.dot(mean_wide, rounded, precision=lax.Precision.HIGHEST)[0:1]

    for r in range(rows):
        x = x_ref[r]
        white = dot(x, white_high) + dot(x, white_low) - offset
        pre = gain * white + bias
        gate = 0.5 * jnp.tanh(0.5 * pre) + 0.5
        act = pre * gate
        turned_ref[:, r * width : (r + 1) * width] = act.T.astype(BF16)
        white_ref[r] = white
        slope_ref[r] = gate + act * (1.0 - gate)


def tap_kernel(turned_ref, near_ref, far_ref, out_ref):
    rows, width = near_ref.shape[1], near_ref.shape[2]
    d = DILATION_RATE
    gap = rows - d
    same = same_group()

    def pair(b, first, count, ref, band):
        turned = turned_ref[:, first * width : (first + count) * width]
        return dot(turned, ref[b, band : band + count].reshape(count * width, C))

    def column(b, carry):
        out_ref[b] = fold(pair(b, 0, gap, near_ref, d) + pair(b, gap, d, far_ref, d), same)
        out_ref[3 + b] = fold(pair(b, 0, rows, near_ref, 0), same)
        out_ref[6 + b] = fold(pair(b, 0, d, far_ref, 0) + pair(b, d, gap, near_ref, 0), same)
        return carry

    lax.fori_loop(0, 3, column, 0)


def grad_kernel(x_ref, grad_ref, white_ref, slope_ref, kept_ref, mean_ref, gain_ref, back_ref, sums_ref):
    rows = x_ref.shape[0]
    same = same_group()
    gain = gain_ref[0:1]
    mean = mean_ref[0:1]
    white_high, white_low = spread_split(kept_ref[ITERS - 1, 0], same)

    def row(r, carry):
        gain_sum, bias_sum, products = carry
        pre_grad = grad_ref[r] * slope_ref[r]
        gain_sum = gain_sum + jnp.sum(pre_grad * white_ref[r], axis=0, keepdims=True)
        bias_sum = bias_sum + jnp.sum(pre_grad, axis=0, keepdims=True)
        high, low = split(pre_grad * gain)
        back_ref[r] = dot(high, white_high) + dot(low, white_high) + dot(high, white_low)
        products = products + lax.dot_general(
            x_ref[r], jnp.concatenate([high, low], axis=1), (((0,), (0,)), ((), ())), preferred_element_type=F32
        )
        return gain_sum, bias_sum, products

    nothing = jnp.zeros((1, C), F32)
    gain_sum, bias_sum, products = lax.fori_loop(0, rows, row, (nothing, nothing, jnp.zeros((C, 2 * C), F32)))
    mean_column = jnp.broadcast_to(mean, (C, C)).T
    full = products[:, :C] + products[:, C:] - mean_column * (gain * bias_sum)
    sums_ref[0:GS] = fold(full + full.T, same)
    line = lax.broadcasted_iota(jnp.int32, (8, C), 0)
    sums_ref[GS : GS + 8] = jnp.where(line == 0, gain_sum, jnp.where(line == 1, bias_sum, 0.0))


def prepare_kernel(kept_ref, wide_ref, cube_ref, token_ref):
    same = same_group()

    def put(place, packed):
        high, low = spread_split(packed, same)
        wide_ref[place, 0] = high
        wide_ref[place, 1] = low

    for k in range(ITERS - 1):
        iterate, square, scaled = kept_ref[k, 0], kept_ref[k, 1], kept_ref[k, 2]
        put(2 * k, scaled)
        put(2 * k + 1, times(iterate, (wide_ref[2 * k, 0], wide_ref[2 * k, 1])))
        cube_ref[k] = times(square, spread_split(iterate, same))
    put(2 * ITERS - 2, kept_ref[ITERS - 1, 1])
    leave(token_ref)


def final_kernel(cell_count, x_ref, back_ref, sums_ref, kept_ref, mean_ref, wide_ref, cube_ref, gain_ref, out_ref, vector_ref):
    rows = x_ref.shape[0]
    same = same_group()
    eye = unit()
    last = ITERS - 1
    whitener, normed = kept_ref[last, 0], kept_ref[last, 1]
    trace = kept_ref[last, 2, 0:1]
    mean = mean_ref[...]
    paired = sums_ref[0:GS]
    step = paired * lax.rsqrt(trace)
    wide = lambda place: (wide_ref[place, 0], wide_ref[place, 1])
    cubes = jnp.concatenate([cube_ref[k] for k in range(ITERS - 1)], axis=0)
    direct = times(cubes, spread_split(step, same))
    change = -0.5 * step
    for k in range(ITERS - 1):
        moved = direct[k * GS : (k + 1) * GS] + times(change, wide(2 * k + 1))
        moved = moved + times(kept_ref[k, 0], spread_split(times(change, wide(2 * k)), same))
        moved = moved + times(kept_ref[k, 1], spread_split(times(change, wide(2 * ITERS - 2)), same))
        change = 1.5 * change - 0.5 * moved
    inner = jnp.sum(change * normed + 0.5 * paired * whitener, axis=0, keepdims=True)
    symmetric = (change - eye * group_total(inner, same)[0:1]) / trace
    high, low = spread_split(symmetric * (1.0 / cell_count), same)
    rounded = high.astype(F32) + low.astype(F32)
    bias_sum = sums_ref[GS + 1 : GS + 2]
    weighted = jnp.broadcast_to(gain_ref[0:1] * bias_sum * (1.0 / cell_count), (8, C))
    constant = jnp.dot(mean, rounded, precision=lax.Precision.HIGHEST)
    constant = constant + jnp.dot(weighted, spread(whitener, same), precision=lax.Precision.HIGHEST)
    constant = constant[0:1]

    def row(r, carry):
        x = x_ref[r]
        out_ref[r] = (dot(x, high) + dot(x, low) + back_ref[r] - constant).astype(BF16)
        return carry

    lax.fori_loop(0, rows, row, 0)
    vector_ref[...] = sums_ref[GS:] * (1.0 / math.sqrt(cell_count))


def stages(axes):
    for axis in axes:
        size = lax.axis_size(axis)
        stride = 1
        while stride < size:
            yield axis, [(i, i ^ stride) for i in range(size)]
            stride *= 2


def add(part, other, after=()):
    return run(add_kernel, jax.ShapeDtypeStruct(part.shape, F32), (part, other), after=after)


def swap(earlier, later, axis):
    size = lax.axis_size(axis)
    got = []
    for begin, part in ((0, earlier), (1, later)):
        pairs = [(i, i + 1) for i in range(begin, size - 1, 2)]
        pairs = pairs + [(j, i) for i, j in pairs]
        got.append(lax.ppermute(part, axis, pairs) if pairs else jnp.zeros_like(part))
    return got


def shards(features, upstream, conv_weight, norm_gain, norm_bias):
    mos_n, rows, width, _ = features.shape
    axes = ("dp", "cols", "rows")
    cell_count = mos_n * rows * width
    for axis in axes:
        cell_count *= lax.axis_size(axis)
    stage_pairs = list(stages(axes))
    count = len(stage_pairs)
    d = DILATION_RATE
    x = features.reshape(rows, width, C)
    up = upstream.reshape(rows, width, C)
    gain = jnp.broadcast_to(norm_gain[None], (8, C))
    bias = jnp.broadcast_to(norm_bias[None], (8, C))
    shape = jax.ShapeDtypeStruct
    cells = (rows, width, C)

    stats = run(stats_kernel, shape((2 * GS + 8, C), F32), (x,), flops=10**9)
    odd = lax.axis_index("cols") % 2 == 1
    first, second = up[:, :8], up[:, -8:]
    first, second = swap(jnp.where(odd, first, second), jnp.where(odd, second, first), "cols")
    left, right = jnp.where(odd, first, second), jnp.where(odd, second, first)
    odd_line = jnp.broadcast_to((lax.axis_index("rows") % 2 == 1).astype(F32), (8, C))
    even_line = 1.0 - odd_line
    halo = shape((d, width + 16, C), BF16)
    first, second = swap(*run(pack_kernel, (halo, halo), (up, left, right, odd_line), after=(stats,)), "rows")
    scratch = (pltpu.VMEM((width + 32, C), F32),)
    for number, (axis, pairs) in enumerate(stage_pairs):
        other = lax.ppermute(stats, axis, pairs)
        token = ()
        if number == 1:
            near_bands, weights, *token = run(
                bands_kernel,
                (shape((3,) + cells, BF16), shape((9, C, C), BF16), TOKEN),
                (up, left, right, conv_weight.reshape(9, GS, C)),
                scratch=scratch,
                flops=10**9,
                after=(stats,),
            )
        if number == 2:
            near_grad, *token = run(
                near_kernel, (shape(cells, F32), TOKEN), (near_bands, weights), flops=10**9, after=(stats,)
            )
        if number == count - 1:
            far_bands, act_grad, *token = run(
                far_kernel,
                (shape((3, 2 * d, width, C), BF16), shape(cells, F32), TOKEN),
                (even_line, odd_line, first, second, weights, near_grad),
                scratch=scratch,
                flops=2 * 10**9,
                after=(stats,),
            )
        stats = run(merge_kernel, shape(stats.shape, F32), (stats, other), after=token)

    turned, white, slope, kept, mean = run(
        act_kernel,
        (
            shape((C, rows * width), BF16),
            shape(cells, F32),
            shape(cells, F32),
            shape((ITERS, 3, GS, C), F32),
            shape((8, C), F32),
        ),
        (x, stats, gain, bias),
        flops=2 * 10**9,
    )
    taps = run(tap_kernel, shape((9, GS, C), F32), (turned, near_bands, far_bands), flops=3 * 10**9)

    tap_axis, tap_pairs = stage_pairs[0]
    later = lax.axis_index(tap_axis) % 2
    halves = taps.reshape(2, -1, C)
    half = lax.dynamic_index_in_dim(halves, later, 0, False)
    half = add(half, lax.ppermute(lax.dynamic_index_in_dim(halves, 1 - later, 0, False), tap_axis, tap_pairs))

    back, sums = run(
        grad_kernel,
        (shape(cells, F32), shape((GS + 8, C), F32)),
        (x, act_grad, white, slope, kept, mean, gain),
        flops=2 * 10**9,
        after=(half,),
    )
    row_stages = [stage for stage in stage_pairs[1:] if stage[0] == "rows"]
    tap_stages = row_stages + [stage for stage in stage_pairs[1:] if stage[0] != "rows"]
    half = add(half, lax.ppermute(half, *tap_stages[0]), after=(sums,))
    for number, stage in enumerate(stage_pairs):
        other = lax.ppermute(sums, *stage)
        token = ()
        if number == 1:
            wide, cubes, *token = run(
                prepare_kernel,
                (shape((2 * ITERS - 1, 2, C, C), BF16), shape((ITERS - 1, GS, C), F32), TOKEN),
                (kept,),
                flops=10**9,
                after=(sums,),
            )
        sums = add(sums, other, after=token)
        if 2 <= number < count:
            last = number == count - 1
            half = add(half, lax.ppermute(half, *tap_stages[number - 1]), after=() if last else (sums,))
    input_grad, vectors = run(
        functools.partial(final_kernel, cell_count),
        (shape(cells, BF16), shape((8, C), F32)),
        (x, back, sums, kept, mean, wide, cubes, gain),
        flops=10**9,
        after=(half,),
    )
    half = half * (1.0 / math.sqrt(cell_count))
    other = lax.ppermute(half, tap_axis, tap_pairs)
    taps = jnp.where(later == 0, jnp.stack([half, other]), jnp.stack([other, half]))
    return (
        input_grad.reshape(features.shape),
        taps.reshape(3, 3, GS, C),
        vectors[0],
        vectors[1],
    )


def solution(mesh):
    placed = (P("dp", "rows", "cols", None), P("dp", "rows", "cols", None), P(), P(), P())
    return jax.shard_map(
        shards,
        mesh=mesh,
        in_specs=placed,
        out_specs=(P("dp", "rows", "cols", None), P(), P(), P()),
        check_vma=False,
    )
```

profile of v0, /device:TPU:0, one launch (start us, length us, event | category | flops | bytes accessed | tf_op | source)
XLA Modules:
  0.0 90.8 jit_solution(13916810486718164315)
XLA Ops:
  0.6 0.8 slice_select_fusion
  1.4 3.0 %collective-permute-start = (bf16[8,8,256]{2,1,0:T(8,128)(2,1)S(1)}, bf16[8,8,256]{2,1,0:T(8,128)(2,1)S(1)}, u32[]{:S(2)}, u32[]{:S(2)}) collective-permute-start(bf16[8,8,256]{2,1,0:T(8,128)(2,1)S(1)} %slice_select_fusion), channel_id=1, source_target_pairs={{0,4},{4,0},{1,5},{5,1},{2,6},{6,2},{3,7},{7,3},{8,12},{12,8},{9,1... | collective-permute-start | bytes 98312 | tf_op jit(solution)/shard_map/ppermute | solution.py:384
  4.4 1.2 %copy-done = bf16[1,8,256,256]{3,2,1,0:T(8,128)(2,1)S(1)} copy-done((bf16[1,8,256,256]{3,2,1,0:T(8,128)(2,1)S(1)}, bf16[1,8,256,256]{3,2,1,0:T(8,128)(2,1)}, u32[]{:S(2)}) %copy-start) | copy-done | bytes 1048600
  5.6 3.0 %shard_map.84.refs_4_.refs_0_ = f32[72,256]{1,0:T(8,128)S(1)} custom-call(bf16[8,256,256]{2,1,0:T(8,128)(2,1)S(1)} %bitcast.15), custom_call_target="tpu_custom_call" | custom-call | flops 1000000000 | bytes 1048576 | tf_op jit(solution)/shard_map/pallas_call | solution.py:30
  8.7 1.6 %shard_map.85 = (bf16[6,272,256]{2,1,0:T(8,128)(2,1)}, bf16[6,272,256]{2,1,0:T(8,128)(2,1)}) custom-call(bf16[8,256,256]{2,1,0:T(8,128)(2,1)S(1)} %bitcast.20, bf16[8,8,256]{2,1,0:T(8,128)(2,1)S(1)} %get-tuple-element.53.refs_1_, bf16[8,8,256]{2,1,0:T(8,128)(2,1)S(1)} %get-tuple-element.52.refs_2_, f32[8,256]{1,0:T(8,128)S(1)} %broadcast_in_dim.8.refs_3_.refs_1_, ...), custom_call_target="tpu_custom_call" | custom-call | bytes 1048576 | tf_op jit(solution)/shard_map/pallas_call | solution.py:30
  10.2 1.6 %collective-permute-start.1 = (bf16[6,272,256]{2,1,0:T(8,128)(2,1)}, bf16[6,272,256]{2,1,0:T(8,128)(2,1)S(1)}, u32[]{:S(2)}, u32[]{:S(2)}) collective-permute-start(bf16[6,272,256]{2,1,0:T(8,128)(2,1)} %get-tuple-element.26), channel_id=1, source_target_pairs={{0,8},{16,24},{8,0},{24,16},{1,9},{17,25},{9,1},{25,17},{2,10},{18... | collective-permute-start | bytes 2506760 | tf_op jit(solution)/shard_map/ppermute | solution.py:384
  11.8 1.6 %collective-permute-start.2 = (bf16[6,272,256]{2,1,0:T(8,128)(2,1)}, bf16[6,272,256]{2,1,0:T(8,128)(2,1)}, u32[]{:S(2)}, u32[]{:S(2)}) collective-permute-start(bf16[6,272,256]{2,1,0:T(8,128)(2,1)} %get-tuple-element.27), channel_id=1, source_target_pairs={{8,16},{16,8},{9,17},{17,9},{10,18},{18,10},{11,19},{19,11},{12,20... | collective-permute-start | bytes 2506760 | tf_op jit(solution)/shard_map/ppermute | solution.py:384
  13.4 1.3 %collective-permute-done.3.refs_1_ = f32[72,256]{1,0:T(8,128)S(1)} collective-permute-done((f32[72,256]{1,0:T(8,128)S(1)}, f32[72,256]{1,0:T(8,128)S(1)}, u32[]{:S(2)}, u32[]{:S(2)}) %collective-permute-start.3) | collective-permute-done | bytes 73760 | tf_op jit(solution)/shard_map/ppermute | solution.py:415
  14.7 1.6 %collective-permute-start.4 = (f32[72,256]{1,0:T(8,128)S(1)}, f32[72,256]{1,0:T(8,128)S(1)}, u32[]{:S(2)}, u32[]{:S(2)}) collective-permute-start(f32[72,256]{1,0:T(8,128)S(1)} %shard_map.86.refs_4_.refs_0_), channel_id=1, source_target_pairs={{0,2},{1,3},{2,0},{3,1},{4,6},{5,7},{6,4},{7,5},{8,10},{9,11},{10,... | collective-permute-start | bytes 221192 | tf_op jit(solution)/shard_map/ppermute | solution.py:415
  16.2 0.8 shard_map.87
  17.0 2.1 %collective-permute-done.4.refs_1_ = f32[72,256]{1,0:T(8,128)S(1)} collective-permute-done((f32[72,256]{1,0:T(8,128)S(1)}, f32[72,256]{1,0:T(8,128)S(1)}, u32[]{:S(2)}, u32[]{:S(2)}) %collective-permute-start.4) | collective-permute-done | bytes 73760 | tf_op jit(solution)/shard_map/ppermute | solution.py:415
  19.1 0.6 collective-permute-start.5
  19.7 2.6 %shard_map.89 = (f32[8,256,256]{2,1,0:T(8,128)S(1)}, f32[8,128]{1,0:T(8,128)S(1)}) custom-call(bf16[3,8,256,256]{3,2,1,0:T(8,128)(2,1)S(1)} %get-tuple-element.29.refs_0_.refs_1_, bf16[9,256,256]{2,1,0:T(8,128)(2,1)S(1)} %get-tuple-element.28.refs_1_.refs_4_, f32[72,256]{1,0:T(8,128)S(1)} %shard_map.88.refs_2_.refs_0_), custom_call_target="tpu_custom_call" | custom-call | flops 1000000000 | bytes 1048576 | tf_op jit(solution)/shard_map/pallas_call | solution.py:30
  22.3 1.3 %copy-done.15 = f32[8,256,256]{2,1,0:T(8,128)} copy-done((f32[8,256,256]{2,1,0:T(8,128)}, f32[8,256,256]{2,1,0:T(8,128)S(1)}, u32[]{:S(2)}) %copy-start.15) | copy-done | bytes 2097176
  23.7 3.6 %collective-permute-start.6 = (f32[72,256]{1,0:T(8,128)S(1)}, f32[72,256]{1,0:T(8,128)S(1)}, u32[]{:S(2)}, u32[]{:S(2)}) collective-permute-start(f32[72,256]{1,0:T(8,128)S(1)} %shard_map.90.refs_0_), channel_id=1, source_target_pairs={{0,8},{8,0},{16,24},{24,16},{1,9},{9,1},{17,25},{25,17},{2,10},{10... | collective-permute-start | bytes 221192 | tf_op jit(solution)/shard_map/ppermute | solution.py:415
  27.3 4.8 %collective-permute-done.6.refs_1_ = f32[72,256]{1,0:T(8,128)S(1)} collective-permute-done((f32[72,256]{1,0:T(8,128)S(1)}, f32[72,256]{1,0:T(8,128)S(1)}, u32[]{:S(2)}, u32[]{:S(2)}) %collective-permute-start.6) | collective-permute-done | bytes 73760 | tf_op jit(solution)/shard_map/ppermute | solution.py:415
  32.1 2.7 %collective-permute-start.7 = (f32[72,256]{1,0:T(8,128)S(1)}, f32[72,256]{1,0:T(8,128)S(1)}, u32[]{:S(2)}, u32[]{:S(2)}) collective-permute-start(f32[72,256]{1,0:T(8,128)S(1)} %shard_map.91.refs_6_.refs_0_), channel_id=1, source_target_pairs={{0,16},{8,24},{16,0},{24,8},{1,17},{9,25},{17,1},{25,9},{2,18},{10... | collective-permute-start | bytes 221192 | tf_op jit(solution)/shard_map/ppermute | solution.py:415
  34.8 1.6 %copy-done.16 = f32[8,256,256]{2,1,0:T(8,128)S(1)} copy-done((f32[8,256,256]{2,1,0:T(8,128)S(1)}, f32[8,256,256]{2,1,0:T(8,128)}, u32[]{:S(2)}) %copy-start.16) | copy-done | bytes 2097176
  36.4 4.8 %shard_map.92 = (bf16[3,12,256,256]{3,2,1,0:T(8,128)(2,1)S(1)}, f32[8,256,256]{2,1,0:T(8,128)S(1)}, f32[8,128]{1,0:T(8,128)S(1)}) custom-call(f32[8,256]{1,0:T(8,128)S(1)} %sub.10.refs_0_, f32[8,256]{1,0:T(8,128)S(1)} %broadcast_in_dim.8.refs_3_.refs_1_, bf16[6,272,256]{2,1,0:T(8,128)(2,1)S(1)} %collective-permute-done.1.refs_2_, ...), custom_call_target="tpu_custom_call" | custom-call | flops 2000000000 | bytes 1048576 | tf_op jit(solution)/shard_map/pallas_call | solution.py:30
  41.2 3.3 %shard_map.94 = (bf16[256,2048]{1,0:T(8,128)(2,1)S(1)}, f32[8,256,256]{2,1,0:T(8,128)S(1)}, f32[8,256,256]{2,1,0:T(8,128)S(1)}, f32[5,3,32,256]{3,2,1,0:T(8,128)S(1)}, f32[8,256]{1,0:T(8,128)S(1)}) custom-call(bf16[8,256,256]{2,1,0:T(8,128)(2,1)S(1)} %bitcast.16, f32[72,256]{1,0:T(8,128)S(1)} %shard_map.93.refs_1_, ...), custom_call_target="tpu_custom_call" | custom-call | flops 2000000000 | bytes 1048576 | tf_op jit(solution)/shard_map/pallas_call | solution.py:30
  44.6 3.0 %shard_map.95 = f32[9,32,256]{2,1,0:T(8,128)S(1)} custom-call(bf16[256,2048]{1,0:T(8,128)(2,1)S(1)} %get-tuple-element.39.refs_0_, bf16[3,8,256,256]{3,2,1,0:T(8,128)(2,1)S(1)} %copy-done.3, bf16[3,12,256,256]{3,2,1,0:T(8,128)(2,1)S(1)} %get-tuple-element.40.refs_2_), custom_call_target="tpu_custom_call" | custom-call | flops 3000000000 | bytes 1048576 | tf_op jit(solution)/shard_map/pallas_call | solution.py:30
  47.6 1.4 %collective-permute-done.8.refs_1_ = f32[144,256]{1,0:T(8,128)S(1)} collective-permute-done((f32[144,256]{1,0:T(8,128)S(1)}, f32[144,256]{1,0:T(8,128)S(1)}, u32[]{:S(2)}, u32[]{:S(2)}) %collective-permute-start.8) | collective-permute-done | bytes 147488 | tf_op jit(solution)/shard_map/ppermute | solution.py:459
  49.0 1.7 %collective-permute-start.14 = (f32[144,256]{1,0:T(8,128)S(1)}, f32[144,256]{1,0:T(8,128)S(1)}, u32[]{:S(2)}, u32[]{:S(2)}) collective-permute-start(f32[144,256]{1,0:T(8,128)S(1)} %shard_map.96.refs_7_.refs_0_), channel_id=1, source_target_pairs={{0,8},{8,0},{16,24},{24,16},{1,9},{9,1},{17,25},{25,17},{2,10},{10... | collective-permute-start | bytes 442376 | tf_op jit(solution)/shard_map/ppermute | solution.py:470
  50.7 3.5 %shard_map.97 = (f32[8,256,256]{2,1,0:T(8,128)S(1)}, f32[40,256]{1,0:T(8,128)S(1)}) custom-call(bf16[8,256,256]{2,1,0:T(8,128)(2,1)S(1)} %bitcast.17, f32[8,256,256]{2,1,0:T(8,128)S(1)} %get-tuple-element.33.refs_1_, f32[8,256,256]{2,1,0:T(8,128)S(1)} %get-tuple-element.35.refs_2_, f32[8,256,256]{2,1,0:T(8,128)S(1)} %get-tuple-element.36.refs_3_, ...), custom_call_target="tpu_custom_call" | custom-call | flops 2000000000 | bytes 1048576 | tf_op jit(solution)/shard_map/pallas_call | solution.py:30
  54.3 0.7 collective-permute-done.14.refs_1_
  55.0 1.7 %collective-permute-start.15 = (f32[144,256]{1,0:T(8,128)S(1)}, f32[144,256]{1,0:T(8,128)S(1)}, u32[]{:S(2)}, u32[]{:S(2)}) collective-permute-start(f32[144,256]{1,0:T(8,128)S(1)} %shard_map.104.refs_0_), channel_id=1, source_target_pairs={{0,16},{8,24},{16,0},{24,8},{1,17},{9,25},{17,1},{25,9},{2,18},{10... | collective-permute-start | bytes 442376 | tf_op jit(solution)/shard_map/ppermute | solution.py:485
  56.7 1.5 %collective-permute-start.10 = (f32[40,256]{1,0:T(8,128)S(1)}, f32[40,256]{1,0:T(8,128)S(1)}, u32[]{:S(2)}, u32[]{:S(2)}) collective-permute-start(f32[40,256]{1,0:T(8,128)S(1)} %shard_map.98.refs_1_.refs_0_), channel_id=1, source_target_pairs={{0,2},{1,3},{2,0},{3,1},{4,6},{5,7},{6,4},{7,5},{8,10},{9,11},{10,... | collective-permute-start | bytes 122888 | tf_op jit(solution)/shard_map/ppermute | solution.py:472
  58.2 0.8 shard_map.99
  59.0 1.7 %collective-permute-done.10.refs_1_ = f32[40,256]{1,0:T(8,128)S(1)} collective-permute-done((f32[40,256]{1,0:T(8,128)S(1)}, f32[40,256]{1,0:T(8,128)S(1)}, u32[]{:S(2)}, u32[]{:S(2)}) %collective-permute-start.10) | collective-permute-done | bytes 40992 | tf_op jit(solution)/shard_map/ppermute | solution.py:472
  60.8 0.5 collective-permute-start.11
  61.3 3.5 %collective-permute-done.11.refs_1_ = f32[40,256]{1,0:T(8,128)S(1)} collective-permute-done((f32[40,256]{1,0:T(8,128)S(1)}, f32[40,256]{1,0:T(8,128)S(1)}, u32[]{:S(2)}, u32[]{:S(2)}) %collective-permute-start.11) | collective-permute-done | bytes 40992 | tf_op jit(solution)/shard_map/ppermute | solution.py:472
  64.8 1.5 %collective-permute-start.16 = (f32[144,256]{1,0:T(8,128)S(1)}, f32[144,256]{1,0:T(8,128)S(1)}, u32[]{:S(2)}, u32[]{:S(2)}) collective-permute-start(f32[144,256]{1,0:T(8,128)S(1)} %shard_map.105.refs_0_), channel_id=1, source_target_pairs={{0,2},{1,3},{2,0},{3,1},{4,6},{5,7},{6,4},{7,5},{8,10},{9,11},{10,... | collective-permute-start | bytes 442376 | tf_op jit(solution)/shard_map/ppermute | solution.py:485
  66.4 0.3 collective-permute-start.12
  66.7 3.7 %collective-permute-done.12.refs_1_ = f32[40,256]{1,0:T(8,128)S(1)} collective-permute-done((f32[40,256]{1,0:T(8,128)S(1)}, f32[40,256]{1,0:T(8,128)S(1)}, u32[]{:S(2)}, u32[]{:S(2)}) %collective-permute-start.12) | collective-permute-done | bytes 40992 | tf_op jit(solution)/shard_map/ppermute | solution.py:472
  70.4 0.6 shard_map.102.refs_0_.refs_2_
  71.0 0.6 collective-permute-start.17
  71.6 1.3 %collective-permute-start.13 = (f32[40,256]{1,0:T(8,128)}, f32[40,256]{1,0:T(8,128)}, u32[]{:S(2)}, u32[]{:S(2)}) collective-permute-start(f32[40,256]{1,0:T(8,128)} %shard_map.102.refs_0_.refs_2_), channel_id=1, source_target_pairs={{0,16},{8,24},{16,0},{24,8},{1,17},{9,25},{17,1},{25,9},{2,18},{10... | collective-permute-start | bytes 122888 | tf_op jit(solution)/shard_map/ppermute | solution.py:472
  72.9 4.1 %collective-permute-done.13.refs_1_ = f32[40,256]{1,0:T(8,128)} collective-permute-done((f32[40,256]{1,0:T(8,128)}, f32[40,256]{1,0:T(8,128)}, u32[]{:S(2)}, u32[]{:S(2)}) %collective-permute-start.13) | collective-permute-done | bytes 40992 | tf_op jit(solution)/shard_map/ppermute | solution.py:472
  77.0 0.8 shard_map.103.refs_2_
  77.8 0.9 %shard_map.107.refs_8_ = f32[144,256]{1,0:T(8,128)S(1)} custom-call(f32[144,256]{1,0:T(8,128)S(1)} %shard_map.106.refs_0_, f32[144,256]{1,0:T(8,128)} %collective-permute-done.17.refs_1_), custom_call_target="tpu_custom_call" | custom-call | bytes 1048576 | tf_op jit(solution)/shard_map/pallas_call | solution.py:30
  78.9 1.6 %copy-done.5 = f32[8,256,256]{2,1,0:T(8,128)S(1)} copy-done((f32[8,256,256]{2,1,0:T(8,128)S(1)}, f32[8,256,256]{2,1,0:T(8,128)}, u32[]{:S(2)}) %copy-start.5) | copy-done | bytes 2097176
  80.4 1.0 %copy-done.7 = f32[5,3,32,256]{3,2,1,0:T(8,128)S(1)} copy-done((f32[5,3,32,256]{3,2,1,0:T(8,128)S(1)}, f32[5,3,32,256]{3,2,1,0:T(8,128)}, u32[]{:S(2)}) %copy-start.7) | copy-done | bytes 491544
  81.5 0.9 copy-done.10
  82.4 0.7 copy-done.12
  83.1 0.7 copy-done.14
  83.8 5.7 %shard_map.108 = (bf16[8,256,256]{2,1,0:T(8,128)(2,1)}, f32[8,256]{1,0:T(8,128)S(1)}) custom-call(bf16[8,256,256]{2,1,0:T(8,128)(2,1)S(1)} %bitcast.18, f32[8,256,256]{2,1,0:T(8,128)S(1)} %copy-done.5, f32[40,256]{1,0:T(8,128)S(1)} %shard_map.103.refs_2_, f32[5,3,32,256]{3,2,1,0:T(8,128)S(1)} %copy-done.7, f32[8,256]{1,0:T(8,128)S(1)} %copy-done.14, ...), custom_call_target="tpu_custom_call" | custom-call | flops 1000000000 | bytes 1048576 | tf_op jit(solution)/shard_map/pallas_call | solution.py:30
  89.5 0.6 fusion.1
  90.1 0.7 maximum_select_fusion
  (65 shorter events, 0.6 us)
Async XLA Ops:
  1.4 7.2 %collective-permute-start = (bf16[8,8,256]{2,1,0:T(8,128)(2,1)S(1)}, bf16[8,8,256]{2,1,0:T(8,128)(2,1)S(1)}, u32[]{:S(2)}, u32[]{:S(2)}) collective-permute-start(bf16[8,8,256]{2,1,0:T(8,128)(2,1)S(1)} %slice_select_fusion), channel_id=1, source_target_pairs={{0,4},{4,0},{1,5},{5,1},{2,6},{6,2},{3,7},{7,3},{8,12},{12,8},{9,1... | collective-permute-start | bytes 98312 | tf_op jit(solution)/shard_map/ppermute | solution.py:384
  4.4 1.2 %copy-start = (bf16[1,8,256,256]{3,2,1,0:T(8,128)(2,1)S(1)}, bf16[1,8,256,256]{3,2,1,0:T(8,128)(2,1)}, u32[]{:S(2)}) copy-start(bf16[1,8,256,256]{3,2,1,0:T(8,128)(2,1)} %param.5) | copy-start | bytes 3145732
  5.6 3.1 %copy-start.8 = (bf16[1,8,256,256]{3,2,1,0:T(8,128)(2,1)S(1)}, bf16[1,8,256,256]{3,2,1,0:T(8,128)(2,1)}, u32[]{:S(2)}) copy-start(bf16[1,8,256,256]{3,2,1,0:T(8,128)(2,1)} %param.6) | copy-start | bytes 3145732
  5.6 10.6 %copy-start.17 = (bf16[3,3,32,256]{3,2,1,0:T(8,128)(2,1)S(1)}, bf16[3,3,32,256]{3,2,1,0:T(8,128)(2,1)}, u32[]{:S(2)}) copy-start(bf16[3,3,32,256]{3,2,1,0:T(8,128)(2,1)} %param.7) | copy-start | bytes 442372
  10.2 24.5 %collective-permute-start.1 = (bf16[6,272,256]{2,1,0:T(8,128)(2,1)}, bf16[6,272,256]{2,1,0:T(8,128)(2,1)S(1)}, u32[]{:S(2)}, u32[]{:S(2)}) collective-permute-start(bf16[6,272,256]{2,1,0:T(8,128)(2,1)} %get-tuple-element.26), channel_id=1, source_target_pairs={{0,8},{16,24},{8,0},{24,16},{1,9},{17,25},{9,1},{25,17},{2,10},{18... | collective-permute-start | bytes 2506760 | tf_op jit(solution)/shard_map/ppermute | solution.py:384
  11.8 22.9 %collective-permute-start.2 = (bf16[6,272,256]{2,1,0:T(8,128)(2,1)}, bf16[6,272,256]{2,1,0:T(8,128)(2,1)}, u32[]{:S(2)}, u32[]{:S(2)}) collective-permute-start(bf16[6,272,256]{2,1,0:T(8,128)(2,1)} %get-tuple-element.27), channel_id=1, source_target_pairs={{8,16},{16,8},{9,17},{17,9},{10,18},{18,10},{11,19},{19,11},{12,20... | collective-permute-start | bytes 2506760 | tf_op jit(solution)/shard_map/ppermute | solution.py:384
  13.4 1.3 %collective-permute-start.3 = (f32[72,256]{1,0:T(8,128)S(1)}, f32[72,256]{1,0:T(8,128)S(1)}, u32[]{:S(2)}, u32[]{:S(2)}) collective-permute-start(f32[72,256]{1,0:T(8,128)S(1)} %shard_map.84.refs_4_.refs_0_), channel_id=1, source_target_pairs={{0,1},{1,0},{2,3},{3,2},{4,5},{5,4},{6,7},{7,6},{8,9},{9,8},{10,11... | collective-permute-start | bytes 221192 | tf_op jit(solution)/shard_map/ppermute | solution.py:415
  14.7 4.4 %collective-permute-start.4 = (f32[72,256]{1,0:T(8,128)S(1)}, f32[72,256]{1,0:T(8,128)S(1)}, u32[]{:S(2)}, u32[]{:S(2)}) collective-permute-start(f32[72,256]{1,0:T(8,128)S(1)} %shard_map.86.refs_4_.refs_0_), channel_id=1, source_target_pairs={{0,2},{1,3},{2,0},{3,1},{4,6},{5,7},{6,4},{7,5},{8,10},{9,11},{10,... | collective-permute-start | bytes 221192 | tf_op jit(solution)/shard_map/ppermute | solution.py:415
  17.0 5.3 %copy-start.2 = (bf16[3,8,256,256]{3,2,1,0:T(8,128)(2,1)}, bf16[3,8,256,256]{3,2,1,0:T(8,128)(2,1)S(1)}, u32[]{:S(2)}) copy-start(bf16[3,8,256,256]{3,2,1,0:T(8,128)(2,1)S(1)} %get-tuple-element.29.refs_0_.refs_1_) | copy-start | bytes 9437188
  19.1 4.5 %collective-permute-start.5 = (f32[72,256]{1,0:T(8,128)S(1)}, f32[72,256]{1,0:T(8,128)S(1)}, u32[]{:S(2)}, u32[]{:S(2)}) collective-permute-start(f32[72,256]{1,0:T(8,128)S(1)} %shard_map.88.refs_2_.refs_0_), channel_id=1, source_target_pairs={{0,4},{4,0},{1,5},{5,1},{2,6},{6,2},{3,7},{7,3},{8,12},{12,8},{9,1... | collective-permute-start | bytes 221192 | tf_op jit(solution)/shard_map/ppermute | solution.py:415
  22.3 1.3 %copy-start.15 = (f32[8,256,256]{2,1,0:T(8,128)}, f32[8,256,256]{2,1,0:T(8,128)S(1)}, u32[]{:S(2)}) copy-start(f32[8,256,256]{2,1,0:T(8,128)S(1)} %get-tuple-element.31.refs_5_) | copy-start | bytes 6291460
  23.7 8.4 %collective-permute-start.6 = (f32[72,256]{1,0:T(8,128)S(1)}, f32[72,256]{1,0:T(8,128)S(1)}, u32[]{:S(2)}, u32[]{:S(2)}) collective-permute-start(f32[72,256]{1,0:T(8,128)S(1)} %shard_map.90.refs_0_), channel_id=1, source_target_pairs={{0,8},{8,0},{16,24},{24,16},{1,9},{9,1},{17,25},{25,17},{2,10},{10... | collective-permute-start | bytes 221192 | tf_op jit(solution)/shard_map/ppermute | solution.py:415
  32.1 9.0 %collective-permute-start.7 = (f32[72,256]{1,0:T(8,128)S(1)}, f32[72,256]{1,0:T(8,128)S(1)}, u32[]{:S(2)}, u32[]{:S(2)}) collective-permute-start(f32[72,256]{1,0:T(8,128)S(1)} %shard_map.91.refs_6_.refs_0_), channel_id=1, source_target_pairs={{0,16},{8,24},{16,0},{24,8},{1,17},{9,25},{17,1},{25,9},{2,18},{10... | collective-permute-start | bytes 221192 | tf_op jit(solution)/shard_map/ppermute | solution.py:415
  34.8 1.6 %copy-start.16 = (f32[8,256,256]{2,1,0:T(8,128)S(1)}, f32[8,256,256]{2,1,0:T(8,128)}, u32[]{:S(2)}) copy-start(f32[8,256,256]{2,1,0:T(8,128)} %copy-done.15) | copy-start | bytes 6291460
  36.4 4.8 %copy-start.18 = (f32[256]{0:T(256)S(1)}, f32[256]{0:T(256)}, u32[]{:S(2)}) copy-start(f32[256]{0:T(256)} %param.8) | copy-start | bytes 3076
  36.4 4.8 %copy-start.19 = (f32[256]{0:T(256)S(1)}, f32[256]{0:T(256)}, u32[]{:S(2)}) copy-start(f32[256]{0:T(256)} %param.9) | copy-start | bytes 3076
  36.4 4.9 %copy-start.1 = (bf16[1,8,256,256]{3,2,1,0:T(8,128)(2,1)S(1)}, bf16[1,8,256,256]{3,2,1,0:T(8,128)(2,1)}, u32[]{:S(2)}) copy-start(bf16[1,8,256,256]{3,2,1,0:T(8,128)(2,1)} %param.5) | copy-start | bytes 3145732
  41.2 9.5 %copy-start.11 = (f32[8,256]{1,0:T(8,128)}, f32[8,256]{1,0:T(8,128)S(1)}, u32[]{:S(2)}) copy-start(f32[8,256]{1,0:T(8,128)S(1)} %broadcast_in_dim.20.refs_2_.refs_6_.refs_7_) | copy-start | bytes 24580
  41.2 3.3 %copy-start.3 = (bf16[3,8,256,256]{3,2,1,0:T(8,128)(2,1)S(1)}, bf16[3,8,256,256]{3,2,1,0:T(8,128)(2,1)}, u32[]{:S(2)}) copy-start(bf16[3,8,256,256]{3,2,1,0:T(8,128)(2,1)} %copy-done.2) | copy-start | bytes 9437188
  44.5 6.2 %copy-start.13 = (f32[8,256]{1,0:T(8,128)}, f32[8,256]{1,0:T(8,128)S(1)}, u32[]{:S(2)}) copy-start(f32[8,256]{1,0:T(8,128)S(1)} %get-tuple-element.38.refs_5_.refs_4_) | copy-start | bytes 24580
  44.5 13.7 %copy-start.6 = (f32[5,3,32,256]{3,2,1,0:T(8,128)}, f32[5,3,32,256]{3,2,1,0:T(8,128)S(1)}, u32[]{:S(2)}) copy-start(f32[5,3,32,256]{3,2,1,0:T(8,128)S(1)} %get-tuple-element.37.refs_4_.refs_0_.refs_3_) | copy-start | bytes 1474564
  47.6 1.4 %collective-permute-start.8 = (f32[144,256]{1,0:T(8,128)S(1)}, f32[144,256]{1,0:T(8,128)S(1)}, u32[]{:S(2)}, u32[]{:S(2)}) collective-permute-start(f32[144,256]{1,0:T(8,128)S(1)} %get-tuple-element.48), channel_id=1, source_target_pairs={{0,1},{1,0},{2,3},{3,2},{4,5},{5,4},{6,7},{7,6},{8,9},{9,8},{10,11... | collective-permute-start | bytes 442376 | tf_op jit(solution)/shard_map/ppermute | solution.py:459
  49.0 6.0 %collective-permute-start.14 = (f32[144,256]{1,0:T(8,128)S(1)}, f32[144,256]{1,0:T(8,128)S(1)}, u32[]{:S(2)}, u32[]{:S(2)}) collective-permute-start(f32[144,256]{1,0:T(8,128)S(1)} %shard_map.96.refs_7_.refs_0_), channel_id=1, source_target_pairs={{0,8},{8,0},{16,24},{24,16},{1,9},{9,1},{17,25},{25,17},{2,10},{10... | collective-permute-start | bytes 442376 | tf_op jit(solution)/shard_map/ppermute | solution.py:470
  54.2 4.8 %copy-start.4 = (f32[8,256,256]{2,1,0:T(8,128)}, f32[8,256,256]{2,1,0:T(8,128)S(1)}, u32[]{:S(2)}) copy-start(f32[8,256,256]{2,1,0:T(8,128)S(1)} %get-tuple-element.41.refs_1_) | copy-start | bytes 6291460
  54.2 2.5 %collective-permute-start.9 = (f32[40,256]{1,0:T(8,128)S(1)}, f32[40,256]{1,0:T(8,128)S(1)}, u32[]{:S(2)}, u32[]{:S(2)}) collective-permute-start(f32[40,256]{1,0:T(8,128)S(1)} %get-tuple-element.42.refs_0_.refs_2_), channel_id=1, source_target_pairs={{0,1},{1,0},{2,3},{3,2},{4,5},{5,4},{6,7},{7,6},{8,9},{9,8},{10,11... | collective-permute-start | bytes 122888 | tf_op jit(solution)/shard_map/ppermute | solution.py:472
  55.0 9.8 %collective-permute-start.15 = (f32[144,256]{1,0:T(8,128)S(1)}, f32[144,256]{1,0:T(8,128)S(1)}, u32[]{:S(2)}, u32[]{:S(2)}) collective-permute-start(f32[144,256]{1,0:T(8,128)S(1)} %shard_map.104.refs_0_), channel_id=1, source_target_pairs={{0,16},{8,24},{16,0},{24,8},{1,17},{9,25},{17,1},{25,9},{2,18},{10... | collective-permute-start | bytes 442376 | tf_op jit(solution)/shard_map/ppermute | solution.py:485
  56.7 4.1 %collective-permute-start.10 = (f32[40,256]{1,0:T(8,128)S(1)}, f32[40,256]{1,0:T(8,128)S(1)}, u32[]{:S(2)}, u32[]{:S(2)}) collective-permute-start(f32[40,256]{1,0:T(8,128)S(1)} %shard_map.98.refs_1_.refs_0_), channel_id=1, source_target_pairs={{0,2},{1,3},{2,0},{3,1},{4,6},{5,7},{6,4},{7,5},{8,10},{9,11},{10,... | collective-permute-start | bytes 122888 | tf_op jit(solution)/shard_map/ppermute | solution.py:472
  59.0 12.0 %copy-start.9 = (f32[4,32,256]{2,1,0:T(8,128)}, f32[4,32,256]{2,1,0:T(8,128)S(1)}, u32[]{:S(2)}) copy-start(f32[4,32,256]{2,1,0:T(8,128)S(1)} %get-tuple-element.45.refs_6_) | copy-start | bytes 393220
  60.8 4.0 %collective-permute-start.11 = (f32[40,256]{1,0:T(8,128)S(1)}, f32[40,256]{1,0:T(8,128)S(1)}, u32[]{:S(2)}, u32[]{:S(2)}) collective-permute-start(f32[40,256]{1,0:T(8,128)S(1)} %shard_map.100.refs_0_), channel_id=1, source_target_pairs={{0,4},{4,0},{1,5},{5,1},{2,6},{6,2},{3,7},{7,3},{8,12},{12,8},{9,1... | collective-permute-start | bytes 122888 | tf_op jit(solution)/shard_map/ppermute | solution.py:472
  64.8 6.2 %collective-permute-start.16 = (f32[144,256]{1,0:T(8,128)S(1)}, f32[144,256]{1,0:T(8,128)S(1)}, u32[]{:S(2)}, u32[]{:S(2)}) collective-permute-start(f32[144,256]{1,0:T(8,128)S(1)} %shard_map.105.refs_0_), channel_id=1, source_target_pairs={{0,2},{1,3},{2,0},{3,1},{4,6},{5,7},{6,4},{7,5},{8,10},{9,11},{10,... | collective-permute-start | bytes 442376 | tf_op jit(solution)/shard_map/ppermute | solution.py:485
  66.4 4.0 %collective-permute-start.12 = (f32[40,256]{1,0:T(8,128)S(1)}, f32[40,256]{1,0:T(8,128)S(1)}, u32[]{:S(2)}, u32[]{:S(2)}) collective-permute-start(f32[40,256]{1,0:T(8,128)S(1)} %shard_map.101.refs_0_.refs_2_), channel_id=1, source_target_pairs={{0,8},{8,0},{16,24},{24,16},{1,9},{9,1},{17,25},{25,17},{2,10},{10... | collective-permute-start | bytes 122888 | tf_op jit(solution)/shard_map/ppermute | solution.py:472
  71.0 6.8 %collective-permute-start.17 = (f32[144,256]{1,0:T(8,128)S(1)}, f32[144,256]{1,0:T(8,128)}, u32[]{:S(2)}, u32[]{:S(2)}) collective-permute-start(f32[144,256]{1,0:T(8,128)S(1)} %shard_map.106.refs_0_), channel_id=1, source_target_pairs={{0,4},{4,0},{1,5},{5,1},{2,6},{6,2},{3,7},{7,3},{8,12},{12,8},{9,1... | collective-permute-start | bytes 442376 | tf_op jit(solution)/shard_map/ppermute | solution.py:485
  71.6 5.4 %collective-permute-start.13 = (f32[40,256]{1,0:T(8,128)}, f32[40,256]{1,0:T(8,128)}, u32[]{:S(2)}, u32[]{:S(2)}) collective-permute-start(f32[40,256]{1,0:T(8,128)} %shard_map.102.refs_0_.refs_2_), channel_id=1, source_target_pairs={{0,16},{8,24},{16,0},{24,8},{1,17},{9,25},{17,1},{25,9},{2,18},{10... | collective-permute-start | bytes 122888 | tf_op jit(solution)/shard_map/ppermute | solution.py:472
  78.8 11.3 %collective-permute-start.18 = (f32[144,256]{1,0:T(8,128)S(1)}, f32[144,256]{1,0:T(8,128)S(1)}, u32[]{:S(2)}, u32[]{:S(2)}) collective-permute-start(f32[144,256]{1,0:T(8,128)S(1)} %get-tuple-element.51), channel_id=1, source_target_pairs={{0,1},{1,0},{2,3},{3,2},{4,5},{5,4},{6,7},{7,6},{8,9},{9,8},{10,11... | collective-permute-start | bytes 442376 | tf_op jit(solution)/shard_map/ppermute | solution.py:494
  78.8 1.6 %copy-start.5 = (f32[8,256,256]{2,1,0:T(8,128)S(1)}, f32[8,256,256]{2,1,0:T(8,128)}, u32[]{:S(2)}) copy-start(f32[8,256,256]{2,1,0:T(8,128)} %copy-done.4) | copy-start | bytes 6291460
  80.4 1.0 %copy-start.7 = (f32[5,3,32,256]{3,2,1,0:T(8,128)S(1)}, f32[5,3,32,256]{3,2,1,0:T(8,128)}, u32[]{:S(2)}) copy-start(f32[5,3,32,256]{3,2,1,0:T(8,128)} %copy-done.6) | copy-start | bytes 1474564
  81.5 0.9 copy-start.10
  82.4 0.7 copy-start.12
  83.1 0.7 copy-start.14
where the time goes:
time: 91.4 us; the launch traced here: 90.8 us
  Pallas kernels  31.5 us (34%)
  starting transfers between devices  23.9 us (26%)
  waiting for transfers between devices  23.2 us (25%)
  local copies, waits for them, and re-layouts  9.72 us (11%)
  other arithmetic  1.55 us (2%)
  between operations  1.02 us (1%)
    pallas_call x25, Pallas kernels, run(): pl.pallas_call(kernel, out_shape=out_shapes, in_specs=[VMEM_SPEC] * count...  31.5 us
    ppermute x5, waiting for transfers between devices, shards(): other = lax.ppermute(sums, *stage)  13 us
    unnamed x40, local copies, waits for them, and re-layouts  9.11 us
    ppermute x5, starting transfers between devices, shards(): other = lax.ppermute(stats, axis, pairs)  8.39 us
    ppermute x5, waiting for transfers between devices, shards(): other = lax.ppermute(stats, axis, pairs)  8.13 us
    ppermute x3, starting transfers between devices, swap(): lax.ppermute(part, axis, pairs)  6.12 us
    ppermute x3, starting transfers between devices, shards(): lax.ppermute(half, *tap_stages[number - 1])  3.8 us
    ppermute x5, starting transfers between devices, shards(): other = lax.ppermute(sums, *stage)  3.75 us
  transfers between devices with their start and end apart: 19, of which 9 were waited for; matrix products, arithmetic and copies ran while one was open for 1% of the time, Pallas kernels for 25%

commit v1 on v0

--- a/solution.py
+++ b/solution.py
@@ -18,9 +18,10 @@
 F32 = jnp.float32
 BF16 = jnp.bfloat16
 VMEM_SPEC = pl.BlockSpec(memory_space=pltpu.VMEM)
-
-
-def run(body, out_shapes, operands, scratch=(), flops=0, after=()):
+NO_COST = pl.CostEstimate(flops=0, bytes_accessed=0, transcendentals=0)
+
+
+def run(body, out_shapes, operands, scratch=(), after=()):
     many = isinstance(out_shapes, (tuple, list))
     count = len(operands)
 
@@ -34,7 +35,7 @@
         out_specs=[VMEM_SPEC] * len(out_shapes) if many else VMEM_SPEC,
         scratch_shapes=list(scratch),
         compiler_params=pltpu.CompilerParams(vmem_limit_bytes=8 * 2**20),
-        cost_estimate=pl.CostEstimate(flops=flops, bytes_accessed=2**20, transcendentals=0),
+        cost_estimate=NO_COST,
     )(*operands, *after)
 
 
@@ -153,7 +154,7 @@
     return dot(jnp.concatenate(bands, axis=1), jnp.concatenate(weights, axis=0))
 
 
-def pack_kernel(up_ref, left_ref, right_ref, odd_ref, first_ref, second_ref):
+def pack_kernel(up_ref, left_ref, right_ref, odd_ref, first_ref, second_ref, token_ref):
     rows, width = up_ref.shape[0], up_ref.shape[1]
     d = DILATION_RATE
     odd = odd_ref[0:1] > 0.5
@@ -162,6 +163,7 @@
             top, bottom = ref[r].astype(F32), ref[rows - d + r].astype(F32)
             first_ref[r, begin : begin + size] = jnp.where(odd, top, bottom).astype(BF16)
             second_ref[r, begin : begin + size] = jnp.where(odd, bottom, top).astype(BF16)
+    leave(token_ref)
 
 
 def bands_kernel(up_ref, left_ref, right_ref, w_ref, moved_ref, weight_ref, token_ref, bands_ref):
@@ -307,7 +309,7 @@
     sums_ref[GS : GS + 8] = jnp.where(line == 0, gain_sum, jnp.where(line == 1, bias_sum, 0.0))
 
 
-def prepare_kernel(kept_ref, wide_ref, cube_ref, token_ref):
+def prepare_kernel(kept_ref, mean_ref, gain_ref, wide_ref, lines_ref, token_ref):
     same = same_group()
 
     def put(place, packed):
@@ -319,46 +321,58 @@
         iterate, square, scaled = kept_ref[k, 0], kept_ref[k, 1], kept_ref[k, 2]
         put(2 * k, scaled)
         put(2 * k + 1, times(iterate, (wide_ref[2 * k, 0], wide_ref[2 * k, 1])))
-        cube_ref[k] = times(square, spread_split(iterate, same))
+        lines_ref[0, k] = iterate
+        lines_ref[1, k] = square
+        lines_ref[2, k] = times(square, spread_split(iterate, same))
     put(2 * ITERS - 2, kept_ref[ITERS - 1, 1])
+    for k in range(3):
+        lines_ref[3, k] = kept_ref[ITERS - 1, k]
+    lines_ref[3, 3, 0:8] = mean_ref[...]
+    lines_ref[3, 3, 8:16] = gain_ref[...]
+    lines_ref[3, 3, 16:] = jnp.zeros((GS - 16, C), F32)
     leave(token_ref)
 
 
-def final_kernel(cell_count, x_ref, back_ref, sums_ref, kept_ref, mean_ref, wide_ref, cube_ref, gain_ref, out_ref, vector_ref):
-    rows = x_ref.shape[0]
+def final_kernel(cell_count, x_ref, back_ref, sums_ref, wide_ref, lines_ref, after_ref, out_ref, vector_ref, high_ref, low_ref, constant_ref):
+    del after_ref
+
+    @pl.when(pl.program_id(0) == 0)
+    def _():
+        derivative(cell_count, sums_ref, wide_ref, lines_ref, vector_ref, high_ref, low_ref, constant_ref)
+
+    x = x_ref[0]
+    moved = dot(x, high_ref[...]) + dot(x, low_ref[...])
+    out_ref[0] = (moved + back_ref[0] - constant_ref[0:1]).astype(BF16)
+
+
+def derivative(cell_count, sums_ref, wide_ref, lines_ref, vector_ref, high_ref, low_ref, constant_ref):
     same = same_group()
     eye = unit()
-    last = ITERS - 1
-    whitener, normed = kept_ref[last, 0], kept_ref[last, 1]
-    trace = kept_ref[last, 2, 0:1]
-    mean = mean_ref[...]
+    whitener, normed = lines_ref[3, 0], lines_ref[3, 1]
+    trace = lines_ref[3, 2, 0:1]
+    mean, gain = lines_ref[3, 3, 0:8], lines_ref[3, 3, 8:16]
     paired = sums_ref[0:GS]
     step = paired * lax.rsqrt(trace)
     wide = lambda place: (wide_ref[place, 0], wide_ref[place, 1])
-    cubes = jnp.concatenate([cube_ref[k] for k in range(ITERS - 1)], axis=0)
-    direct = times(cubes, spread_split(step, same))
+    direct = times(lines_ref[2].reshape((ITERS - 1) * GS, C), spread_split(step, same))
     change = -0.5 * step
     for k in range(ITERS - 1):
         moved = direct[k * GS : (k + 1) * GS] + times(change, wide(2 * k + 1))
-        moved = moved + times(kept_ref[k, 0], spread_split(times(change, wide(2 * k)), same))
-        moved = moved + times(kept_ref[k, 1], spread_split(times(change, wide(2 * ITERS - 2)), same))
+        moved = moved + times(lines_ref[0, k], spread_split(times(change, wide(2 * k)), same))
+        moved = moved + times(lines_ref[1, k], spread_split(times(change, wide(2 * ITERS - 2)), same))
         change = 1.5 * change - 0.5 * moved
     inner = jnp.sum(change * normed + 0.5 * paired * whitener, axis=0, keepdims=True)
     symmetric = (change - eye * group_total(inner, same)[0:1]) / trace
     high, low = spread_split(symmetric * (1.0 / cell_count), same)
+    high_ref[...] = high
+    low_ref[...] = low
     rounded = high.astype(F32) + low.astype(F32)
     bias_sum = sums_ref[GS + 1 : GS + 2]
-    weighted = jnp.broadcast_to(gain_ref[0:1] * bias_sum * (1.0 / cell_count), (8, C))
-    constant = jnp.dot(mean, rounded, precision=lax.Precision.HIGHEST)
-    constant = constant + jnp.dot(weighted, spread(whitener, same), precision=lax.Precision.HIGHEST)
-    constant = constant[0:1]
-
-    def row(r, carry):
-        x = x_ref[r]
-        out_ref[r] = (dot(x, high) + dot(x, low) + back_ref[r] - constant).astype(BF16)
-        return carry
-
-    lax.fori_loop(0, rows, row, 0)
+    weighted = gain * bias_sum * (1.0 / cell_count)
+    both = jnp.concatenate([mean, weighted], axis=1)
+    constant_ref[...] = jnp.dot(
+        both, jnp.concatenate([rounded, spread(whitener, same)], axis=0), precision=lax.Precision.HIGHEST
+    )
     vector_ref[...] = sums_ref[GS:] * (1.0 / math.sqrt(cell_count))
 
 
@@ -372,6 +386,8 @@
 
 
 def add(part, other, after=()):
+    if not after:
+        return part + other
     return run(add_kernel, jax.ShapeDtypeStruct(part.shape, F32), (part, other), after=after)
 
 
@@ -401,7 +417,6 @@
     shape = jax.ShapeDtypeStruct
     cells = (rows, width, C)
 
-    stats = run(stats_kernel, shape((2 * GS + 8, C), F32), (x,), flops=10**9)
     odd = lax.axis_index("cols") % 2 == 1
     first, second = up[:, :8], up[:, -8:]
     first, second = swap(jnp.where(odd, first, second), jnp.where(odd, second, first), "cols")
@@ -409,23 +424,24 @@
     odd_line = jnp.broadcast_to((lax.axis_index("rows") % 2 == 1).astype(F32), (8, C))
     even_line = 1.0 - odd_line
     halo = shape((d, width + 16, C), BF16)
-    first, second = swap(*run(pack_kernel, (halo, halo), (up, left, right, odd_line), after=(stats,)), "rows")
+    first, second, token = run(pack_kernel, (halo, halo, TOKEN), (up, left, right, odd_line))
+    first, second = swap(first, second, "rows")
+    stats = run(stats_kernel, shape((2 * GS + 8, C), F32), (x,), after=(token,))
     scratch = (pltpu.VMEM((width + 32, C), F32),)
     for number, (axis, pairs) in enumerate(stage_pairs):
         other = lax.ppermute(stats, axis, pairs)
         token = ()
-        if number == 1:
+        if number == count - 3:
             near_bands, weights, *token = run(
                 bands_kernel,
                 (shape((3,) + cells, BF16), shape((9, C, C), BF16), TOKEN),
                 (up, left, right, conv_weight.reshape(9, GS, C)),
                 scratch=scratch,
-                flops=10**9,
                 after=(stats,),
             )
-        if number == 2:
+        if number == count - 2:
             near_grad, *token = run(
-                near_kernel, (shape(cells, F32), TOKEN), (near_bands, weights), flops=10**9, after=(stats,)
+                near_kernel, (shape(cells, F32), TOKEN), (near_bands, weights), after=(stats,)
             )
         if number == count - 1:
             far_bands, act_grad, *token = run(
@@ -433,7 +449,6 @@
                 (shape((3, 2 * d, width, C), BF16), shape(cells, F32), TOKEN),
                 (even_line, odd_line, first, second, weights, near_grad),
                 scratch=scratch,
-                flops=2 * 10**9,
                 after=(stats,),
             )
         stats = run(merge_kernel, shape(stats.shape, F32), (stats, other), after=token)
@@ -448,9 +463,8 @@
             shape((8, C), F32),
         ),
         (x, stats, gain, bias),
-        flops=2 * 10**9,
     )
-    taps = run(tap_kernel, shape((9, GS, C), F32), (turned, near_bands, far_bands), flops=3 * 10**9)
+    taps = run(tap_kernel, shape((9, GS, C), F32), (turned, near_bands, far_bands))
 
     tap_axis, tap_pairs = stage_pairs[0]
     later = lax.axis_index(tap_axis) % 2
@@ -462,7 +476,6 @@
         grad_kernel,
         (shape(cells, F32), shape((GS + 8, C), F32)),
         (x, act_grad, white, slope, kept, mean, gain),
-        flops=2 * 10**9,
         after=(half,),
     )
     row_stages = [stage for stage in stage_pairs[1:] if stage[0] == "rows"]
@@ -471,25 +484,28 @@
     for number, stage in enumerate(stage_pairs):
         other = lax.ppermute(sums, *stage)
         token = ()
-        if number == 1:
-            wide, cubes, *token = run(
+        if number == count - 1:
+            wide, lines, *token = run(
                 prepare_kernel,
-                (shape((2 * ITERS - 1, 2, C, C), BF16), shape((ITERS - 1, GS, C), F32), TOKEN),
-                (kept,),
-                flops=10**9,
+                (shape((2 * ITERS - 1, 2, C, C), BF16), shape((4, ITERS - 1, GS, C), F32), TOKEN),
+                (kept, mean, gain),
                 after=(sums,),
             )
         sums = add(sums, other, after=token)
         if 2 <= number < count:
             last = number == count - 1
             half = add(half, lax.ppermute(half, *tap_stages[number - 1]), after=() if last else (sums,))
-    input_grad, vectors = run(
+    block = pl.BlockSpec((1, width, C), lambda r: (r, 0, 0))
+    input_grad, vectors = pl.pallas_call(
         functools.partial(final_kernel, cell_count),
-        (shape(cells, BF16), shape((8, C), F32)),
-        (x, back, sums, kept, mean, wide, cubes, gain),
-        flops=10**9,
-        after=(half,),
-    )
+        grid=(rows,),
+        out_shape=(shape(cells, BF16), shape((8, C), F32)),
+        in_specs=[block, block] + [VMEM_SPEC] * 3 + [pl.BlockSpec(memory_space=pl.ANY)],
+        out_specs=[block, VMEM_SPEC],
+        scratch_shapes=[pltpu.VMEM((C, C), BF16), pltpu.VMEM((C, C), BF16), pltpu.VMEM((8, C), F32)],
+        compiler_params=pltpu.CompilerParams(vmem_limit_bytes=8 * 2**20),
+        cost_estimate=NO_COST,
+    )(x, back, sums, wide, lines, half)
     half = half * (1.0 / math.sqrt(cell_count))
     other = lax.ppermute(half, tap_axis, tap_pairs)
     taps = jnp.where(later == 0, jnp.stack([half, other]), jnp.stack([other, half]))

time: 91.4 us -> 92.4 us (1.011)
  waiting for transfers between devices: 23.2 us -> 20 us
  local copies, waits for them, and re-layouts: 9.72 us -> 12.9 us
  starting transfers between devices: 23.9 us -> 25.9 us
  Pallas kernels: 31.5 us -> 30.4 us
    pallas_call x25 -> x18, Pallas kernels: 31.5 us -> 23.6 us  [run(): pl.pallas_call(kernel, out_shape=out_shapes, in_specs=[VMEM_SPEC] * count...]
    pallas_call x0 -> x1, Pallas kernels: none -> 6.86 us  [shards(): pl.pallas_call(functools.partial(final_kernel, cell_count), grid=(rows,),...]
    unnamed x40 -> x38, local copies, waits for them, and re-layouts: 9.11 us -> 12.3 us
    ppermute x5, waiting for transfers between devices: 13 us -> 10.6 us  [shards(): other = lax.ppermute(sums, *stage)]
    ppermute x5, waiting for transfers between devices: 8.13 us -> 6.14 us  [shards(): other = lax.ppermute(stats, axis, pairs)]
    ppermute x5, starting transfers between devices: 3.75 us -> 5.71 us  [shards(): other = lax.ppermute(sums, *stage)]
    ppermute x3, waiting for transfers between devices: 0.01 us -> 1.9 us  [swap(): lax.ppermute(part, axis, pairs)]
    ppermute x5, starting transfers between devices: 8.39 us -> 6.85 us  [shards(): other = lax.ppermute(stats, axis, pairs)]
  transfers between devices with their start and end apart: 19 -> 19, of which waited for: 9 -> 10; matrix products, arithmetic and copies ran while one was open for 1% -> 1% of each run, Pallas kernels for 25% -> 25%
where the time goes in v1:
time: 92.4 us; the launch traced here: 92 us
  Pallas kernels  30.4 us (33%)
  starting transfers between devices  25.9 us (28%)
  waiting for transfers between devices  20 us (22%)
  local copies, waits for them, and re-layouts  12.9 us (14%)
  other arithmetic  1.7 us (2%)
  between operations  1.04 us (1%)
    pallas_call x18, Pallas kernels, run(): pl.pallas_call(kernel, out_shape=out_shapes, in_specs=[VMEM_SPEC] * count...  23.6 us
    unnamed x38, local copies, waits for them, and re-layouts  12.3 us
    ppermute x5, waiting for transfers between devices, shards(): other = lax.ppermute(sums, *stage)  10.6 us
    pallas_call x1, Pallas kernels, shards(): pl.pallas_call(functools.partial(final_kernel, cell_count), grid=(rows,),...  6.86 us
    ppermute x5, starting transfers between devices, shards(): other = lax.ppermute(stats, axis, pairs)  6.85 us
    ppermute x3, starting transfers between devices, swap(): lax.ppermute(part, axis, pairs)  6.62 us
    ppermute x5, waiting for transfers between devices, shards(): other = lax.ppermute(stats, axis, pairs)  6.14 us
    ppermute x5, starting transfers between devices, shards(): other = lax.ppermute(sums, *stage)  5.71 us
  transfers between devices with their start and end apart: 19, of which 10 were waited for; matrix products, arithmetic and copies ran while one was open for 1% of the time, Pallas kernels for 25%

profile of v1, /device:TPU:0, one launch (start us, length us, event | category | flops | bytes accessed | tf_op | source)
XLA Modules:
  0.0 92.0 jit_solution(2714966332344937789)
XLA Ops:
  0.7 0.9 slice_select_fusion
  1.5 3.0 %collective-permute-start = (bf16[8,8,256]{2,1,0:T(8,128)(2,1)S(1)}, bf16[8,8,256]{2,1,0:T(8,128)(2,1)S(1)}, u32[]{:S(2)}, u32[]{:S(2)}) collective-permute-start(bf16[8,8,256]{2,1,0:T(8,128)(2,1)S(1)} %slice_select_fusion), channel_id=1, source_target_pairs={{0,4},{4,0},{1,5},{5,1},{2,6},{6,2},{3,7},{7,3},{8,12},{12,8},{9,1... | collective-permute-start | bytes 98312 | tf_op jit(solution)/shard_map/ppermute | solution.py:400
  4.5 1.9 %collective-permute-done = bf16[8,8,256]{2,1,0:T(8,128)(2,1)S(1)} collective-permute-done((bf16[8,8,256]{2,1,0:T(8,128)(2,1)S(1)}, bf16[8,8,256]{2,1,0:T(8,128)(2,1)S(1)}, u32[]{:S(2)}, u32[]{:S(2)}) %collective-permute-start) | collective-permute-done | bytes 32800 | tf_op jit(solution)/shard_map/ppermute | solution.py:400
  6.4 1.2 %copy-done.3 = bf16[1,8,256,256]{3,2,1,0:T(8,128)(2,1)S(1)} copy-done((bf16[1,8,256,256]{3,2,1,0:T(8,128)(2,1)S(1)}, bf16[1,8,256,256]{3,2,1,0:T(8,128)(2,1)}, u32[]{:S(2)}) %copy-start.3) | copy-done | bytes 1048600
  7.6 1.6 %shard_map.84 = (bf16[6,272,256]{2,1,0:T(8,128)(2,1)}, bf16[6,272,256]{2,1,0:T(8,128)(2,1)}, f32[8,128]{1,0:T(8,128)S(1)}) custom-call(bf16[8,256,256]{2,1,0:T(8,128)(2,1)S(1)} %bitcast.20, bf16[8,8,256]{2,1,0:T(8,128)(2,1)S(1)} %get-tuple-element.53.refs_1_, bf16[8,8,256]{2,1,0:T(8,128)(2,1)S(1)} %get-tuple-element.52.refs_2_, ...), custom_call_target="tpu_custom_call" | custom-call | tf_op jit(solution)/shard_map/pallas_call | solution.py:31
  9.2 2.1 %collective-permute-start.1 = (bf16[6,272,256]{2,1,0:T(8,128)(2,1)}, bf16[6,272,256]{2,1,0:T(8,128)(2,1)S(1)}, u32[]{:S(2)}, u32[]{:S(2)}) collective-permute-start(bf16[6,272,256]{2,1,0:T(8,128)(2,1)} %get-tuple-element.27), channel_id=1, source_target_pairs={{0,8},{16,24},{8,0},{24,16},{1,9},{17,25},{9,1},{25,17},{2,10},{18... | collective-permute-start | bytes 2506760 | tf_op jit(solution)/shard_map/ppermute | solution.py:400
  11.3 1.6 %collective-permute-start.2 = (bf16[6,272,256]{2,1,0:T(8,128)(2,1)}, bf16[6,272,256]{2,1,0:T(8,128)(2,1)}, u32[]{:S(2)}, u32[]{:S(2)}) collective-permute-start(bf16[6,272,256]{2,1,0:T(8,128)(2,1)} %get-tuple-element.28), channel_id=1, source_target_pairs={{8,16},{16,8},{9,17},{17,9},{10,18},{18,10},{11,19},{19,11},{12,20... | collective-permute-start | bytes 2506760 | tf_op jit(solution)/shard_map/ppermute | solution.py:400
  12.8 3.0 %shard_map.85.refs_0_ = f32[72,256]{1,0:T(8,128)S(1)} custom-call(bf16[8,256,256]{2,1,0:T(8,128)(2,1)S(1)} %bitcast.15, f32[8,128]{1,0:T(8,128)S(1)} %get-tuple-element.29.refs_1_), custom_call_target="tpu_custom_call" | custom-call | tf_op jit(solution)/shard_map/pallas_call | solution.py:31
  15.8 0.1 collective-permute-start.3
  15.9 1.3 %collective-permute-done.3.refs_1_ = f32[72,256]{1,0:T(8,128)S(1)} collective-permute-done((f32[72,256]{1,0:T(8,128)S(1)}, f32[72,256]{1,0:T(8,128)S(1)}, u32[]{:S(2)}, u32[]{:S(2)}) %collective-permute-start.3) | collective-permute-done | bytes 73760 | tf_op jit(solution)/shard_map/ppermute | solution.py:432
  17.2 1.6 %collective-permute-start.4 = (f32[72,256]{1,0:T(8,128)S(1)}, f32[72,256]{1,0:T(8,128)S(1)}, u32[]{:S(2)}, u32[]{:S(2)}) collective-permute-start(f32[72,256]{1,0:T(8,128)S(1)} %shard_map.86.refs_0_), channel_id=1, source_target_pairs={{0,2},{1,3},{2,0},{3,1},{4,6},{5,7},{6,4},{7,5},{8,10},{9,11},{10,... | collective-permute-start | bytes 221192 | tf_op jit(solution)/shard_map/ppermute | solution.py:432
  18.7 2.9 %collective-permute-done.4.refs_1_ = f32[72,256]{1,0:T(8,128)S(1)} collective-permute-done((f32[72,256]{1,0:T(8,128)S(1)}, f32[72,256]{1,0:T(8,128)S(1)}, u32[]{:S(2)}, u32[]{:S(2)}) %collective-permute-start.4) | collective-permute-done | bytes 73760 | tf_op jit(solution)/shard_map/ppermute | solution.py:432
  21.6 1.6 %collective-permute-start.5 = (f32[72,256]{1,0:T(8,128)S(1)}, f32[72,256]{1,0:T(8,128)S(1)}, u32[]{:S(2)}, u32[]{:S(2)}) collective-permute-start(f32[72,256]{1,0:T(8,128)S(1)} %shard_map.87.refs_4_.refs_0_), channel_id=1, source_target_pairs={{0,4},{4,0},{1,5},{5,1},{2,6},{6,2},{3,7},{7,3},{8,12},{12,8},{9,1... | collective-permute-start | bytes 221192 | tf_op jit(solution)/shard_map/ppermute | solution.py:432
  23.2 0.8 shard_map.88
  24.0 2.0 %collective-permute-done.5.refs_1_ = f32[72,256]{1,0:T(8,128)S(1)} collective-permute-done((f32[72,256]{1,0:T(8,128)S(1)}, f32[72,256]{1,0:T(8,128)S(1)}, u32[]{:S(2)}, u32[]{:S(2)}) %collective-permute-start.5) | collective-permute-done | bytes 73760 | tf_op jit(solution)/shard_map/ppermute | solution.py:432
  26.1 3.6 %collective-permute-start.6 = (f32[72,256]{1,0:T(8,128)S(1)}, f32[72,256]{1,0:T(8,128)S(1)}, u32[]{:S(2)}, u32[]{:S(2)}) collective-permute-start(f32[72,256]{1,0:T(8,128)S(1)} %shard_map.89.refs_2_.refs_0_), channel_id=1, source_target_pairs={{0,8},{8,0},{16,24},{24,16},{1,9},{9,1},{17,25},{25,17},{2,10},{10... | collective-permute-start | bytes 221192 | tf_op jit(solution)/shard_map/ppermute | solution.py:432
  29.6 2.6 %shard_map.90 = (f32[8,256,256]{2,1,0:T(8,128)S(1)}, f32[8,128]{1,0:T(8,128)S(1)}) custom-call(bf16[3,8,256,256]{3,2,1,0:T(8,128)(2,1)S(1)} %get-tuple-element.31.refs_0_.refs_1_, bf16[9,256,256]{2,1,0:T(8,128)(2,1)S(1)} %get-tuple-element.30.refs_1_.refs_4_, f32[72,256]{1,0:T(8,128)S(1)} %shard_map.89.refs_2_.refs_0_), custom_call_target="tpu_custom_call" | custom-call | tf_op jit(solution)/shard_map/pallas_call | solution.py:31
  32.2 1.3 %copy-done.5 = f32[8,256,256]{2,1,0:T(8,128)} copy-done((f32[8,256,256]{2,1,0:T(8,128)}, f32[8,256,256]{2,1,0:T(8,128)S(1)}, u32[]{:S(2)}) %copy-start.5) | copy-done | bytes 2097176
  33.7 1.6 %copy-done.6 = f32[8,256,256]{2,1,0:T(8,128)S(1)} copy-done((f32[8,256,256]{2,1,0:T(8,128)S(1)}, f32[8,256,256]{2,1,0:T(8,128)}, u32[]{:S(2)}) %copy-start.6) | copy-done | bytes 2097176
  35.3 4.9 %shard_map.92 = (bf16[3,12,256,256]{3,2,1,0:T(8,128)(2,1)S(1)}, f32[8,256,256]{2,1,0:T(8,128)S(1)}, f32[8,128]{1,0:T(8,128)S(1)}) custom-call(f32[8,256]{1,0:T(8,128)S(1)} %sub.10.refs_0_, f32[8,256]{1,0:T(8,128)S(1)} %broadcast_in_dim.8.refs_3_.refs_1_, bf16[6,272,256]{2,1,0:T(8,128)(2,1)S(1)} %collective-permute-done.1.refs_2_, ...), custom_call_target="tpu_custom_call" | custom-call | tf_op jit(solution)/shard_map/pallas_call | solution.py:31
  40.2 1.3 %copy-done.7 = f32[8,256,256]{2,1,0:T(8,128)} copy-done((f32[8,256,256]{2,1,0:T(8,128)}, f32[8,256,256]{2,1,0:T(8,128)S(1)}, u32[]{:S(2)}) %copy-start.7) | copy-done | bytes 2097176
  41.6 3.3 %shard_map.94 = (bf16[256,2048]{1,0:T(8,128)(2,1)S(1)}, f32[8,256,256]{2,1,0:T(8,128)S(1)}, f32[8,256,256]{2,1,0:T(8,128)S(1)}, f32[5,3,32,256]{3,2,1,0:T(8,128)S(1)}, f32[8,256]{1,0:T(8,128)S(1)}) custom-call(bf16[8,256,256]{2,1,0:T(8,128)(2,1)S(1)} %bitcast.16, f32[72,256]{1,0:T(8,128)S(1)} %shard_map.93.refs_1_, ...), custom_call_target="tpu_custom_call" | custom-call | tf_op jit(solution)/shard_map/pallas_call | solution.py:31
  44.9 3.0 %shard_map.95 = f32[9,32,256]{2,1,0:T(8,128)S(1)} custom-call(bf16[256,2048]{1,0:T(8,128)(2,1)S(1)} %get-tuple-element.41.refs_0_, bf16[3,8,256,256]{3,2,1,0:T(8,128)(2,1)S(1)} %copy-done.2, bf16[3,12,256,256]{3,2,1,0:T(8,128)(2,1)S(1)} %get-tuple-element.42.refs_2_), custom_call_target="tpu_custom_call" | custom-call | tf_op jit(solution)/shard_map/pallas_call | solution.py:31
  48.1 1.4 %collective-permute-done.8 = f32[144,256]{1,0:T(8,128)S(1)} collective-permute-done((f32[144,256]{1,0:T(8,128)S(1)}, f32[144,256]{1,0:T(8,128)S(1)}, u32[]{:S(2)}, u32[]{:S(2)}) %collective-permute-start.8) | collective-permute-done | bytes 147488 | tf_op jit(solution)/shard_map/ppermute | solution.py:473
  49.4 1.5 %collective-permute-start.14 = (f32[144,256]{1,0:T(8,128)S(1)}, f32[144,256]{1,0:T(8,128)S(1)}, u32[]{:S(2)}, u32[]{:S(2)}) collective-permute-start(f32[144,256]{1,0:T(8,128)S(1)} %bitcast_add_fusion.refs_7_.refs_0_), channel_id=1, source_target_pairs={{0,8},{8,0},{16,24},{24,16},{1,9},{9,1},{17,25},{25,17},{2,10},{10... | collective-permute-start | bytes 442376 | tf_op jit(solution)/shard_map/ppermute | solution.py:483
  50.9 1.6 %copy-done.8 = f32[8,256,256]{2,1,0:T(8,128)S(1)} copy-done((f32[8,256,256]{2,1,0:T(8,128)S(1)}, f32[8,256,256]{2,1,0:T(8,128)}, u32[]{:S(2)}) %copy-start.8) | copy-done | bytes 2097176
  52.5 1.6 %copy-done.10 = f32[8,256,256]{2,1,0:T(8,128)S(1)} copy-done((f32[8,256,256]{2,1,0:T(8,128)S(1)}, f32[8,256,256]{2,1,0:T(8,128)}, u32[]{:S(2)}) %copy-start.10) | copy-done | bytes 2097176
  54.1 1.6 %copy-done.12 = f32[8,256,256]{2,1,0:T(8,128)S(1)} copy-done((f32[8,256,256]{2,1,0:T(8,128)S(1)}, f32[8,256,256]{2,1,0:T(8,128)}, u32[]{:S(2)}) %copy-start.12) | copy-done | bytes 2097176
  55.7 1.0 %copy-done.14 = f32[5,3,32,256]{3,2,1,0:T(8,128)S(1)} copy-done((f32[5,3,32,256]{3,2,1,0:T(8,128)S(1)}, f32[5,3,32,256]{3,2,1,0:T(8,128)}, u32[]{:S(2)}) %copy-start.14) | copy-done | bytes 491544
  56.7 3.6 %shard_map.96 = (f32[8,256,256]{2,1,0:T(8,128)S(1)}, f32[40,256]{1,0:T(8,128)S(1)}) custom-call(bf16[8,256,256]{2,1,0:T(8,128)(2,1)S(1)} %bitcast.17, f32[8,256,256]{2,1,0:T(8,128)S(1)} %copy-done.8, f32[8,256,256]{2,1,0:T(8,128)S(1)} %copy-done.10, f32[8,256,256]{2,1,0:T(8,128)S(1)} %copy-done.12, f32[5,3,32,256]{3,2,1,0:T(8,128)S(1)} %copy-done.14, ...), custom_call_target="tpu_custom_call" | custom-call | tf_op jit(solution)/shard_map/pallas_call | solution.py:31
  60.4 1.9 %collective-permute-start.15 = (f32[144,256]{1,0:T(8,128)S(1)}, f32[144,256]{1,0:T(8,128)S(1)}, u32[]{:S(2)}, u32[]{:S(2)}) collective-permute-start(f32[144,256]{1,0:T(8,128)S(1)} %shard_map.99.refs_0_), channel_id=1, source_target_pairs={{0,16},{8,24},{16,0},{24,8},{1,17},{9,25},{17,1},{25,9},{2,18},{10... | collective-permute-start | bytes 442376 | tf_op jit(solution)/shard_map/ppermute | solution.py:497
  62.3 1.2 %collective-permute-done.9 = f32[40,256]{1,0:T(8,128)S(1)} collective-permute-done((f32[40,256]{1,0:T(8,128)S(1)}, f32[40,256]{1,0:T(8,128)S(1)}, u32[]{:S(2)}, u32[]{:S(2)}) %collective-permute-start.9) | collective-permute-done | bytes 40992 | tf_op jit(solution)/shard_map/ppermute | solution.py:485
  63.5 1.5 %collective-permute-start.10 = (f32[40,256]{1,0:T(8,128)S(1)}, f32[40,256]{1,0:T(8,128)S(1)}, u32[]{:S(2)}, u32[]{:S(2)}) collective-permute-start(f32[40,256]{1,0:T(8,128)S(1)} %add.42), channel_id=1, source_target_pairs={{0,2},{1,3},{2,0},{3,1},{4,6},{5,7},{6,4},{7,5},{8,10},{9,11},{10,... | collective-permute-start | bytes 122888 | tf_op jit(solution)/shard_map/ppermute | solution.py:485
  65.0 2.5 %collective-permute-done.10 = f32[40,256]{1,0:T(8,128)S(1)} collective-permute-done((f32[40,256]{1,0:T(8,128)S(1)}, f32[40,256]{1,0:T(8,128)S(1)}, u32[]{:S(2)}, u32[]{:S(2)}) %collective-permute-start.10) | collective-permute-done | bytes 40992 | tf_op jit(solution)/shard_map/ppermute | solution.py:485
  67.5 1.5 %collective-permute-start.11 = (f32[40,256]{1,0:T(8,128)S(1)}, f32[40,256]{1,0:T(8,128)S(1)}, u32[]{:S(2)}, u32[]{:S(2)}) collective-permute-start(f32[40,256]{1,0:T(8,128)S(1)} %add.43), channel_id=1, source_target_pairs={{0,4},{4,0},{1,5},{5,1},{2,6},{6,2},{3,7},{7,3},{8,12},{12,8},{9,1... | collective-permute-start | bytes 122888 | tf_op jit(solution)/shard_map/ppermute | solution.py:485
  69.1 2.5 %collective-permute-done.11 = f32[40,256]{1,0:T(8,128)S(1)} collective-permute-done((f32[40,256]{1,0:T(8,128)S(1)}, f32[40,256]{1,0:T(8,128)S(1)}, u32[]{:S(2)}, u32[]{:S(2)}) %collective-permute-start.11) | collective-permute-done | bytes 40992 | tf_op jit(solution)/shard_map/ppermute | solution.py:485
  71.6 1.6 %collective-permute-start.16 = (f32[144,256]{1,0:T(8,128)S(1)}, f32[144,256]{1,0:T(8,128)S(1)}, u32[]{:S(2)}, u32[]{:S(2)}) collective-permute-start(f32[144,256]{1,0:T(8,128)S(1)} %shard_map.100.refs_0_), channel_id=1, source_target_pairs={{0,2},{1,3},{2,0},{3,1},{4,6},{5,7},{6,4},{7,5},{8,10},{9,11},{10,... | collective-permute-start | bytes 442376 | tf_op jit(solution)/shard_map/ppermute | solution.py:497
  73.1 1.6 %collective-permute-start.12 = (f32[40,256]{1,0:T(8,128)S(1)}, f32[40,256]{1,0:T(8,128)S(1)}, u32[]{:S(2)}, u32[]{:S(2)}) collective-permute-start(f32[40,256]{1,0:T(8,128)S(1)} %add.44.refs_2_), channel_id=1, source_target_pairs={{0,8},{8,0},{16,24},{24,16},{1,9},{9,1},{17,25},{25,17},{2,10},{10... | collective-permute-start | bytes 122888 | tf_op jit(solution)/shard_map/ppermute | solution.py:485
  74.8 2.4 %collective-permute-done.12 = f32[40,256]{1,0:T(8,128)S(1)} collective-permute-done((f32[40,256]{1,0:T(8,128)S(1)}, f32[40,256]{1,0:T(8,128)S(1)}, u32[]{:S(2)}, u32[]{:S(2)}) %collective-permute-start.12) | collective-permute-done | bytes 40992 | tf_op jit(solution)/shard_map/ppermute | solution.py:485
  77.2 1.6 %collective-permute-start.17 = (f32[144,256]{1,0:T(8,128)S(1)}, f32[144,256]{1,0:T(8,128)S(1)}, u32[]{:S(2)}, u32[]{:S(2)}) collective-permute-start(f32[144,256]{1,0:T(8,128)S(1)} %shard_map.101), channel_id=1, source_target_pairs={{0,4},{4,0},{1,5},{5,1},{2,6},{6,2},{3,7},{7,3},{8,12},{12,8},{9,1... | collective-permute-start | bytes 442376 | tf_op jit(solution)/shard_map/ppermute | solution.py:497
  78.8 1.1 %collective-permute-start.13 = (f32[40,256]{1,0:T(8,128)S(1)}, f32[40,256]{1,0:T(8,128)S(1)}, u32[]{:S(2)}, u32[]{:S(2)}) collective-permute-start(f32[40,256]{1,0:T(8,128)S(1)} %add.45.refs_3_.refs_0_.refs_2_), channel_id=1, source_target_pairs={{0,16},{8,24},{16,0},{24,8},{1,17},{9,25},{17,1},{25,9},{2,18},{10... | collective-permute-start | bytes 122888 | tf_op jit(solution)/shard_map/ppermute | solution.py:485
  79.8 1.0 %copy-done.15 = f32[5,3,32,256]{3,2,1,0:T(8,128)S(1)} copy-done((f32[5,3,32,256]{3,2,1,0:T(8,128)S(1)}, f32[5,3,32,256]{3,2,1,0:T(8,128)}, u32[]{:S(2)}) %copy-start.15) | copy-done | bytes 491544
  80.9 0.8 shard_map.97
  81.7 2.0 %collective-permute-done.13.refs_1_ = f32[40,256]{1,0:T(8,128)S(1)} collective-permute-done((f32[40,256]{1,0:T(8,128)S(1)}, f32[40,256]{1,0:T(8,128)S(1)}, u32[]{:S(2)}, u32[]{:S(2)}) %collective-permute-start.13) | collective-permute-done | bytes 40992 | tf_op jit(solution)/shard_map/ppermute | solution.py:485
  83.7 0.1 collective-permute-start.18
  83.8 6.9 %shard_map.102 = (bf16[8,256,256]{2,1,0:T(8,128)(2,1)}, f32[8,256]{1,0:T(8,128)S(1)}) custom-call(bf16[8,256,256]{2,1,0:T(8,128)(2,1)S(1)} %bitcast.18, f32[8,256,256]{2,1,0:T(8,128)S(1)} %get-tuple-element.43.back_ref, f32[40,256]{1,0:T(8,128)S(1)} %shard_map.98.sums_ref, bf16[9,2,256,256]{3,2,1,0:T(8,128)(2,1)S(1)} %get-tuple-element.46.wide_ref, ...), custom_call_target="tpu_custom_call" | custom-call | tf_op jit(solution)/shard_map/pallas_call | solution.py:499
  90.7 0.6 fusion.1
  91.2 0.7 maximum_select_fusion
  (63 shorter events, 0.5 us)
Async XLA Ops:
  0.6 12.2 %copy-start = (bf16[1,8,256,256]{3,2,1,0:T(8,128)(2,1)S(1)}, bf16[1,8,256,256]{3,2,1,0:T(8,128)(2,1)}, u32[]{:S(2)}) copy-start(bf16[1,8,256,256]{3,2,1,0:T(8,128)(2,1)} %param.5) | copy-start | bytes 3145732
  1.5 4.9 %collective-permute-start = (bf16[8,8,256]{2,1,0:T(8,128)(2,1)S(1)}, bf16[8,8,256]{2,1,0:T(8,128)(2,1)S(1)}, u32[]{:S(2)}, u32[]{:S(2)}) collective-permute-start(bf16[8,8,256]{2,1,0:T(8,128)(2,1)S(1)} %slice_select_fusion), channel_id=1, source_target_pairs={{0,4},{4,0},{1,5},{5,1},{2,6},{6,2},{3,7},{7,3},{8,12},{12,8},{9,1... | collective-permute-start | bytes 98312 | tf_op jit(solution)/shard_map/ppermute | solution.py:400
  6.4 1.2 %copy-start.3 = (bf16[1,8,256,256]{3,2,1,0:T(8,128)(2,1)S(1)}, bf16[1,8,256,256]{3,2,1,0:T(8,128)(2,1)}, u32[]{:S(2)}) copy-start(bf16[1,8,256,256]{3,2,1,0:T(8,128)(2,1)} %param.6) | copy-start | bytes 3145732
  7.6 15.6 %copy-start.4 = (bf16[1,8,256,256]{3,2,1,0:T(8,128)(2,1)S(1)}, bf16[1,8,256,256]{3,2,1,0:T(8,128)(2,1)}, u32[]{:S(2)}) copy-start(bf16[1,8,256,256]{3,2,1,0:T(8,128)(2,1)} %param.6) | copy-start | bytes 3145732
  7.6 15.6 %copy-start.16 = (bf16[3,3,32,256]{3,2,1,0:T(8,128)(2,1)S(1)}, bf16[3,3,32,256]{3,2,1,0:T(8,128)(2,1)}, u32[]{:S(2)}) copy-start(bf16[3,3,32,256]{3,2,1,0:T(8,128)(2,1)} %param.7) | copy-start | bytes 442372
  9.2 24.5 %collective-permute-start.1 = (bf16[6,272,256]{2,1,0:T(8,128)(2,1)}, bf16[6,272,256]{2,1,0:T(8,128)(2,1)S(1)}, u32[]{:S(2)}, u32[]{:S(2)}) collective-permute-start(bf16[6,272,256]{2,1,0:T(8,128)(2,1)} %get-tuple-element.27), channel_id=1, source_target_pairs={{0,8},{16,24},{8,0},{24,16},{1,9},{17,25},{9,1},{25,17},{2,10},{18... | collective-permute-start | bytes 2506760 | tf_op jit(solution)/shard_map/ppermute | solution.py:400
  11.3 22.4 %collective-permute-start.2 = (bf16[6,272,256]{2,1,0:T(8,128)(2,1)}, bf16[6,272,256]{2,1,0:T(8,128)(2,1)}, u32[]{:S(2)}, u32[]{:S(2)}) collective-permute-start(bf16[6,272,256]{2,1,0:T(8,128)(2,1)} %get-tuple-element.28), channel_id=1, source_target_pairs={{8,16},{16,8},{9,17},{17,9},{10,18},{18,10},{11,19},{19,11},{12,20... | collective-permute-start | bytes 2506760 | tf_op jit(solution)/shard_map/ppermute | solution.py:400
  15.8 1.3 %collective-permute-start.3 = (f32[72,256]{1,0:T(8,128)S(1)}, f32[72,256]{1,0:T(8,128)S(1)}, u32[]{:S(2)}, u32[]{:S(2)}) collective-permute-start(f32[72,256]{1,0:T(8,128)S(1)} %shard_map.85.refs_0_), channel_id=1, source_target_pairs={{0,1},{1,0},{2,3},{3,2},{4,5},{5,4},{6,7},{7,6},{8,9},{9,8},{10,11... | collective-permute-start | bytes 221192 | tf_op jit(solution)/shard_map/ppermute | solution.py:432
  17.2 4.4 %collective-permute-start.4 = (f32[72,256]{1,0:T(8,128)S(1)}, f32[72,256]{1,0:T(8,128)S(1)}, u32[]{:S(2)}, u32[]{:S(2)}) collective-permute-start(f32[72,256]{1,0:T(8,128)S(1)} %shard_map.86.refs_0_), channel_id=1, source_target_pairs={{0,2},{1,3},{2,0},{3,1},{4,6},{5,7},{6,4},{7,5},{8,10},{9,11},{10,... | collective-permute-start | bytes 221192 | tf_op jit(solution)/shard_map/ppermute | solution.py:432
  21.6 4.4 %collective-permute-start.5 = (f32[72,256]{1,0:T(8,128)S(1)}, f32[72,256]{1,0:T(8,128)S(1)}, u32[]{:S(2)}, u32[]{:S(2)}) collective-permute-start(f32[72,256]{1,0:T(8,128)S(1)} %shard_map.87.refs_4_.refs_0_), channel_id=1, source_target_pairs={{0,4},{4,0},{1,5},{5,1},{2,6},{6,2},{3,7},{7,3},{8,12},{12,8},{9,1... | collective-permute-start | bytes 221192 | tf_op jit(solution)/shard_map/ppermute | solution.py:432
  24.0 8.2 %copy-start.1 = (bf16[3,8,256,256]{3,2,1,0:T(8,128)(2,1)}, bf16[3,8,256,256]{3,2,1,0:T(8,128)(2,1)S(1)}, u32[]{:S(2)}) copy-start(bf16[3,8,256,256]{3,2,1,0:T(8,128)(2,1)S(1)} %get-tuple-element.31.refs_0_.refs_1_) | copy-start | bytes 9437188
  26.1 7.5 %collective-permute-start.6 = (f32[72,256]{1,0:T(8,128)S(1)}, f32[72,256]{1,0:T(8,128)S(1)}, u32[]{:S(2)}, u32[]{:S(2)}) collective-permute-start(f32[72,256]{1,0:T(8,128)S(1)} %shard_map.89.refs_2_.refs_0_), channel_id=1, source_target_pairs={{0,8},{8,0},{16,24},{24,16},{1,9},{9,1},{17,25},{25,17},{2,10},{10... | collective-permute-start | bytes 221192 | tf_op jit(solution)/shard_map/ppermute | solution.py:432
  32.2 1.3 %copy-start.5 = (f32[8,256,256]{2,1,0:T(8,128)}, f32[8,256,256]{2,1,0:T(8,128)S(1)}, u32[]{:S(2)}) copy-start(f32[8,256,256]{2,1,0:T(8,128)S(1)} %get-tuple-element.33.refs_5_) | copy-start | bytes 6291460
  33.6 7.9 %collective-permute-start.7 = (f32[72,256]{1,0:T(8,128)S(1)}, f32[72,256]{1,0:T(8,128)S(1)}, u32[]{:S(2)}, u32[]{:S(2)}) collective-permute-start(f32[72,256]{1,0:T(8,128)S(1)} %shard_map.91.refs_6_.refs_0_), channel_id=1, source_target_pairs={{0,16},{8,24},{16,0},{24,8},{1,17},{9,25},{17,1},{25,9},{2,18},{10... | collective-permute-start | bytes 221192 | tf_op jit(solution)/shard_map/ppermute | solution.py:432
  33.7 1.6 %copy-start.6 = (f32[8,256,256]{2,1,0:T(8,128)S(1)}, f32[8,256,256]{2,1,0:T(8,128)}, u32[]{:S(2)}) copy-start(f32[8,256,256]{2,1,0:T(8,128)} %copy-done.5) | copy-start | bytes 6291460
  35.3 6.2 %copy-start.17 = (f32[256]{0:T(256)S(1)}, f32[256]{0:T(256)}, u32[]{:S(2)}) copy-start(f32[256]{0:T(256)} %param.8) | copy-start | bytes 3076
  35.3 6.2 %copy-start.18 = (f32[256]{0:T(256)S(1)}, f32[256]{0:T(256)}, u32[]{:S(2)}) copy-start(f32[256]{0:T(256)} %param.9) | copy-start | bytes 3076
  35.3 9.6 %copy-start.2 = (bf16[3,8,256,256]{3,2,1,0:T(8,128)(2,1)S(1)}, bf16[3,8,256,256]{3,2,1,0:T(8,128)(2,1)}, u32[]{:S(2)}) copy-start(bf16[3,8,256,256]{3,2,1,0:T(8,128)(2,1)} %copy-done.1) | copy-start | bytes 9437188
  40.2 1.3 %copy-start.7 = (f32[8,256,256]{2,1,0:T(8,128)}, f32[8,256,256]{2,1,0:T(8,128)S(1)}, u32[]{:S(2)}) copy-start(f32[8,256,256]{2,1,0:T(8,128)S(1)} %get-tuple-element.35.refs_1_) | copy-start | bytes 6291460
  44.9 3.0 %copy-start.9 = (f32[8,256,256]{2,1,0:T(8,128)}, f32[8,256,256]{2,1,0:T(8,128)S(1)}, u32[]{:S(2)}) copy-start(f32[8,256,256]{2,1,0:T(8,128)S(1)} %get-tuple-element.37.refs_2_) | copy-start | bytes 6291460
  44.9 3.0 %copy-start.11 = (f32[8,256,256]{2,1,0:T(8,128)}, f32[8,256,256]{2,1,0:T(8,128)S(1)}, u32[]{:S(2)}) copy-start(f32[8,256,256]{2,1,0:T(8,128)S(1)} %get-tuple-element.38.refs_3_) | copy-start | bytes 6291460
  44.9 3.0 %copy-start.13 = (f32[5,3,32,256]{3,2,1,0:T(8,128)}, f32[5,3,32,256]{3,2,1,0:T(8,128)S(1)}, u32[]{:S(2)}) copy-start(f32[5,3,32,256]{3,2,1,0:T(8,128)S(1)} %get-tuple-element.39.refs_4_.refs_0_) | copy-start | bytes 1474564
  48.0 1.4 %collective-permute-start.8 = (f32[144,256]{1,0:T(8,128)S(1)}, f32[144,256]{1,0:T(8,128)S(1)}, u32[]{:S(2)}, u32[]{:S(2)}) collective-permute-start(f32[144,256]{1,0:T(8,128)S(1)} %dynamic-slice_bitcast_fusion), channel_id=1, source_target_pairs={{0,1},{1,0},{2,3},{3,2},{4,5},{5,4},{6,7},{7,6},{8,9},{9,8},{10,11... | collective-permute-start | bytes 442376 | tf_op jit(solution)/shard_map/ppermute | solution.py:473
  49.4 10.9 %collective-permute-start.14 = (f32[144,256]{1,0:T(8,128)S(1)}, f32[144,256]{1,0:T(8,128)S(1)}, u32[]{:S(2)}, u32[]{:S(2)}) collective-permute-start(f32[144,256]{1,0:T(8,128)S(1)} %bitcast_add_fusion.refs_7_.refs_0_), channel_id=1, source_target_pairs={{0,8},{8,0},{16,24},{24,16},{1,9},{9,1},{17,25},{25,17},{2,10},{10... | collective-permute-start | bytes 442376 | tf_op jit(solution)/shard_map/ppermute | solution.py:483
  50.9 1.6 %copy-start.8 = (f32[8,256,256]{2,1,0:T(8,128)S(1)}, f32[8,256,256]{2,1,0:T(8,128)}, u32[]{:S(2)}) copy-start(f32[8,256,256]{2,1,0:T(8,128)} %copy-done.7) | copy-start | bytes 6291460
  52.5 1.6 %copy-start.10 = (f32[8,256,256]{2,1,0:T(8,128)S(1)}, f32[8,256,256]{2,1,0:T(8,128)}, u32[]{:S(2)}) copy-start(f32[8,256,256]{2,1,0:T(8,128)} %copy-done.9) | copy-start | bytes 6291460
  54.1 1.6 %copy-start.12 = (f32[8,256,256]{2,1,0:T(8,128)S(1)}, f32[8,256,256]{2,1,0:T(8,128)}, u32[]{:S(2)}) copy-start(f32[8,256,256]{2,1,0:T(8,128)} %copy-done.11) | copy-start | bytes 6291460
  55.7 1.0 %copy-start.14 = (f32[5,3,32,256]{3,2,1,0:T(8,128)S(1)}, f32[5,3,32,256]{3,2,1,0:T(8,128)}, u32[]{:S(2)}) copy-start(f32[5,3,32,256]{3,2,1,0:T(8,128)} %copy-done.13) | copy-start | bytes 1474564
  60.4 11.2 %collective-permute-start.15 = (f32[144,256]{1,0:T(8,128)S(1)}, f32[144,256]{1,0:T(8,128)S(1)}, u32[]{:S(2)}, u32[]{:S(2)}) collective-permute-start(f32[144,256]{1,0:T(8,128)S(1)} %shard_map.99.refs_0_), channel_id=1, source_target_pairs={{0,16},{8,24},{16,0},{24,8},{1,17},{9,25},{17,1},{25,9},{2,18},{10... | collective-permute-start | bytes 442376 | tf_op jit(solution)/shard_map/ppermute | solution.py:497
  62.3 1.2 %collective-permute-start.9 = (f32[40,256]{1,0:T(8,128)S(1)}, f32[40,256]{1,0:T(8,128)S(1)}, u32[]{:S(2)}, u32[]{:S(2)}) collective-permute-start(f32[40,256]{1,0:T(8,128)S(1)} %get-tuple-element.44.refs_2_), channel_id=1, source_target_pairs={{0,1},{1,0},{2,3},{3,2},{4,5},{5,4},{6,7},{7,6},{8,9},{9,8},{10,11... | collective-permute-start | bytes 122888 | tf_op jit(solution)/shard_map/ppermute | solution.py:485
  63.5 4.0 %collective-permute-start.10 = (f32[40,256]{1,0:T(8,128)S(1)}, f32[40,256]{1,0:T(8,128)S(1)}, u32[]{:S(2)}, u32[]{:S(2)}) collective-permute-start(f32[40,256]{1,0:T(8,128)S(1)} %add.42), channel_id=1, source_target_pairs={{0,2},{1,3},{2,0},{3,1},{4,6},{5,7},{6,4},{7,5},{8,10},{9,11},{10,... | collective-permute-start | bytes 122888 | tf_op jit(solution)/shard_map/ppermute | solution.py:485
  67.5 4.0 %collective-permute-start.11 = (f32[40,256]{1,0:T(8,128)S(1)}, f32[40,256]{1,0:T(8,128)S(1)}, u32[]{:S(2)}, u32[]{:S(2)}) collective-permute-start(f32[40,256]{1,0:T(8,128)S(1)} %add.43), channel_id=1, source_target_pairs={{0,4},{4,0},{1,5},{5,1},{2,6},{6,2},{3,7},{7,3},{8,12},{12,8},{9,1... | collective-permute-start | bytes 122888 | tf_op jit(solution)/shard_map/ppermute | solution.py:485
  71.6 5.6 %collective-permute-start.16 = (f32[144,256]{1,0:T(8,128)S(1)}, f32[144,256]{1,0:T(8,128)S(1)}, u32[]{:S(2)}, u32[]{:S(2)}) collective-permute-start(f32[144,256]{1,0:T(8,128)S(1)} %shard_map.100.refs_0_), channel_id=1, source_target_pairs={{0,2},{1,3},{2,0},{3,1},{4,6},{5,7},{6,4},{7,5},{8,10},{9,11},{10,... | collective-permute-start | bytes 442376 | tf_op jit(solution)/shard_map/ppermute | solution.py:497
  73.1 4.0 %collective-permute-start.12 = (f32[40,256]{1,0:T(8,128)S(1)}, f32[40,256]{1,0:T(8,128)S(1)}, u32[]{:S(2)}, u32[]{:S(2)}) collective-permute-start(f32[40,256]{1,0:T(8,128)S(1)} %add.44.refs_2_), channel_id=1, source_target_pairs={{0,8},{8,0},{16,24},{24,16},{1,9},{9,1},{17,25},{25,17},{2,10},{10... | collective-permute-start | bytes 122888 | tf_op jit(solution)/shard_map/ppermute | solution.py:485
  77.2 6.5 %collective-permute-start.17 = (f32[144,256]{1,0:T(8,128)S(1)}, f32[144,256]{1,0:T(8,128)S(1)}, u32[]{:S(2)}, u32[]{:S(2)}) collective-permute-start(f32[144,256]{1,0:T(8,128)S(1)} %shard_map.101), channel_id=1, source_target_pairs={{0,4},{4,0},{1,5},{5,1},{2,6},{6,2},{3,7},{7,3},{8,12},{12,8},{9,1... | collective-permute-start | bytes 442376 | tf_op jit(solution)/shard_map/ppermute | solution.py:497
  78.8 4.9 %collective-permute-start.13 = (f32[40,256]{1,0:T(8,128)S(1)}, f32[40,256]{1,0:T(8,128)S(1)}, u32[]{:S(2)}, u32[]{:S(2)}) collective-permute-start(f32[40,256]{1,0:T(8,128)S(1)} %add.45.refs_3_.refs_0_.refs_2_), channel_id=1, source_target_pairs={{0,16},{8,24},{16,0},{24,8},{1,17},{9,25},{17,1},{25,9},{2,18},{10... | collective-permute-start | bytes 122888 | tf_op jit(solution)/shard_map/ppermute | solution.py:485
  79.8 1.0 %copy-start.15 = (f32[5,3,32,256]{3,2,1,0:T(8,128)S(1)}, f32[5,3,32,256]{3,2,1,0:T(8,128)}, u32[]{:S(2)}) copy-start(f32[5,3,32,256]{3,2,1,0:T(8,128)} %copy-done.13) | copy-start | bytes 1474564
  83.7 7.5 %collective-permute-start.18 = (f32[144,256]{1,0:T(8,128)S(1)}, f32[144,256]{1,0:T(8,128)S(1)}, u32[]{:S(2)}, u32[]{:S(2)}) collective-permute-start(f32[144,256]{1,0:T(8,128)S(1)} %broadcast_multiply_fusion), channel_id=1, source_target_pairs={{0,1},{1,0},{2,3},{3,2},{4,5},{5,4},{6,7},{7,6},{8,9},{9,8},{10,11... | collective-permute-start | bytes 442376 | tf_op jit(solution)/shard_map/ppermute | solution.py:510

commit v2 on v1

--- a/solution.py
+++ b/solution.py
@@ -21,22 +21,32 @@
 NO_COST = pl.CostEstimate(flops=0, bytes_accessed=0, transcendentals=0)
 
 
-def run(body, out_shapes, operands, scratch=(), after=()):
+def run(body, out_shapes, operands, scratch=(), after=(), grid=(), in_blocks={}, out_blocks={}):
     many = isinstance(out_shapes, (tuple, list))
     count = len(operands)
 
     def kernel(*refs):
         body(*refs[:count], *refs[count + len(after) :])
 
+    out_specs = [out_blocks.get(i, VMEM_SPEC) for i in range(len(out_shapes) if many else 1)]
     return pl.pallas_call(
         kernel,
+        grid=grid,
         out_shape=out_shapes,
-        in_specs=[VMEM_SPEC] * count + [pl.BlockSpec(memory_space=pl.ANY)] * len(after),
-        out_specs=[VMEM_SPEC] * len(out_shapes) if many else VMEM_SPEC,
+        in_specs=[in_blocks.get(i, VMEM_SPEC) for i in range(count)] + [pl.BlockSpec(memory_space=pl.ANY)] * len(after),
+        out_specs=out_specs if many else out_specs[0],
         scratch_shapes=list(scratch),
-        compiler_params=pltpu.CompilerParams(vmem_limit_bytes=8 * 2**20),
+        compiler_params=pltpu.CompilerParams(vmem_limit_bytes=10 * 2**20),
         cost_estimate=NO_COST,
     )(*operands, *after)
+
+
+def at_first(step):
+    pl.when(pl.program_id(0) == 0)(step)
+
+
+def at_last(step):
+    pl.when(pl.program_id(0) == pl.num_programs(0) - 1)(step)
 
 
 TOKEN = jax.ShapeDtypeStruct((8, 128), F32)
@@ -154,15 +164,19 @@
     return dot(jnp.concatenate(bands, axis=1), jnp.concatenate(weights, axis=0))
 
 
-def pack_kernel(up_ref, left_ref, right_ref, odd_ref, first_ref, second_ref, token_ref):
-    rows, width = up_ref.shape[0], up_ref.shape[1]
-    d = DILATION_RATE
+def pack_kernel(top_ref, bottom_ref, left_ref, right_ref, odd_ref, first_ref, second_ref, token_ref):
+    rows, width = left_ref.shape[0], top_ref.shape[1]
+    r = pl.program_id(0)
     odd = odd_ref[0:1] > 0.5
-    for r in range(d):
-        for begin, size, ref in ((0, width, up_ref), (width, 8, left_ref), (width + 8, 8, right_ref)):
-            top, bottom = ref[r].astype(F32), ref[rows - d + r].astype(F32)
-            first_ref[r, begin : begin + size] = jnp.where(odd, top, bottom).astype(BF16)
-            second_ref[r, begin : begin + size] = jnp.where(odd, bottom, top).astype(BF16)
+    low = rows - DILATION_RATE + r
+    sides = ((top_ref[0], bottom_ref[0]), (left_ref[r], left_ref[low]), (right_ref[r], right_ref[low]))
+    begin = 0
+    for top, bottom in sides:
+        top, bottom = top.astype(F32), bottom.astype(F32)
+        size = top.shape[0]
+        first_ref[0, begin : begin + size] = jnp.where(odd, top, bottom).astype(BF16)
+        second_ref[0, begin : begin + size] = jnp.where(odd, bottom, top).astype(BF16)
+        begin += size
     leave(token_ref)
 
 
@@ -181,51 +195,50 @@
     leave(token_ref)
 
 
+def by_rows(rows, cases, step):
+    r = pl.program_id(0)
+    for first, last, shifts in cases:
+        pl.when((r >= first) & (r < last))(functools.partial(step, r, shifts))
+
+
 def near_kernel(moved_ref, weight_ref, out_ref, token_ref):
-    rows = out_ref.shape[0]
-    d = DILATION_RATE
-    for first, last, taps in ((0, rows - d, {0: d, 1: 0}), (rows - d, d, {1: 0}), (d, rows, {1: 0, 2: -d})):
-
-        def row(r, carry, taps=taps):
-            out_ref[r] = tap_rows(moved_ref, weight_ref, [(a, r + step) for a, step in taps.items()])
+    rows, d = moved_ref.shape[1], DILATION_RATE
+
+    def step(r, shifts):
+        out_ref[0] = tap_rows(moved_ref, weight_ref, [(a, r + shift) for a, shift in shifts.items()])
+
+    by_rows(rows, ((0, rows - d, {0: d, 1: 0}), (rows - d, d, {1: 0}), (d, rows, {1: 0, 2: -d})), step)
+    leave(token_ref)
+
+
+def far_kernel(rows, even_ref, odd_ref, first_ref, second_ref, weight_ref, near_ref, moved_ref, out_ref, token_ref, bands_ref):
+    d, width = DILATION_RATE, out_ref.shape[1]
+
+    @at_first
+    def _():
+        def outer(r, carry):
+            first, second = first_ref[r], second_ref[r]
+            for begin, place in ((0, odd_ref), (d, even_ref)):
+                halo = jnp.where(place[0:1] > 0.5, first.astype(F32), second.astype(F32)).astype(BF16)
+                shift_band(
+                    moved_ref, bands_ref, begin + r, halo[0:width], halo[width : width + 8], halo[width + 8 :]
+                )
             return carry
 
-        lax.fori_loop(first, last, row, 0)
-    leave(token_ref)
-
-
-def far_kernel(even_ref, odd_ref, first_ref, second_ref, weight_ref, near_ref, moved_ref, out_ref, token_ref, bands_ref):
-    rows, width = out_ref.shape[0], out_ref.shape[1]
-    d = DILATION_RATE
-
-    def outer(r, carry):
-        first, second = first_ref[r], second_ref[r]
-        for begin, place in ((0, odd_ref), (d, even_ref)):
-            halo = jnp.where(place[0:1] > 0.5, first.astype(F32), second.astype(F32)).astype(BF16)
-            shift_band(
-                moved_ref, bands_ref, begin + r, halo[0:width], halo[width : width + 8], halo[width + 8 :]
-            )
-        return carry
-
-    lax.fori_loop(0, d, outer, 0)
+        lax.fori_loop(0, d, outer, 0)
+        leave(token_ref)
+
+    def step(r, shifts):
+        out_ref[0] = near_ref[0] + tap_rows(moved_ref, weight_ref, [(a, r + shift) for a, shift in shifts.items()])
+
     back = 2 * d - rows
-    for first, last, taps in ((0, rows - d, {2: 0}), (rows - d, d, {0: back, 2: 0}), (d, rows, {0: back})):
-
-        def row(r, carry, taps=taps):
-            far = tap_rows(moved_ref, weight_ref, [(a, r + step) for a, step in taps.items()])
-            out_ref[r] = near_ref[r] + far
-            return carry
-
-        lax.fori_loop(first, last, row, 0)
-    leave(token_ref)
-
-
-def act_kernel(x_ref, stats_ref, gain_ref, bias_ref, turned_ref, white_ref, slope_ref, kept_ref, mean_ref):
-    rows, width = x_ref.shape[0], x_ref.shape[1]
+    by_rows(rows, ((0, rows - d, {2: 0}), (rows - d, d, {0: back, 2: 0}), (d, rows, {0: back})), step)
+
+
+def newton(stats_ref, kept_ref, mean_ref, high_ref, low_ref, offset_ref):
     same = same_group()
     eye = unit()
-    gain, bias = gain_ref[0:1], bias_ref[0:1]
-    mean = stats_ref[2 * GS : 2 * GS + 1]
+    mean = stats_ref[2 * GS :]
     cov = stats_ref[0:GS] + EPSILON * eye
     trace = group_total(jnp.sum(cov * eye, axis=0, keepdims=True), same)[0:1]
     normed = cov / trace
@@ -235,31 +248,39 @@
         wide = spread_split(iterate, same)
         square = times(iterate, wide)
         scaled = times(iterate, normed_wide)
-        scaled_wide = spread_split(scaled, same)
-        cube_scaled = times(square, scaled_wide)
+        cube_scaled = times(square, spread_split(scaled, same))
         kept_ref[k, 0] = iterate
         kept_ref[k, 1] = square
         kept_ref[k, 2] = scaled
         iterate = 1.5 * iterate - 0.5 * cube_scaled
     whitener = iterate * lax.rsqrt(trace)
-    mean_wide = jnp.broadcast_to(mean, (8, C))
     kept_ref[ITERS - 1, 0] = whitener
     kept_ref[ITERS - 1, 1] = normed
     kept_ref[ITERS - 1, 2] = jnp.broadcast_to(trace, (GS, C))
-    mean_ref[...] = mean_wide
-    white_high, white_low = spread_split(whitener, same)
-    rounded = white_high.astype(F32) + white_low.astype(F32)
-    offset = jnp.dot(mean_wide, rounded, precision=lax.Precision.HIGHEST)[0:1]
-
-    for r in range(rows):
-        x = x_ref[r]
-        white = dot(x, white_high) + dot(x, white_low) - offset
-        pre = gain * white + bias
-        gate = 0.5 * jnp.tanh(0.5 * pre) + 0.5
-        act = pre * gate
-        turned_ref[:, r * width : (r + 1) * width] = act.T.astype(BF16)
-        white_ref[r] = white
-        slope_ref[r] = gate + act * (1.0 - gate)
+    mean_ref[...] = mean
+    high, low = spread_split(whitener, same)
+    high_ref[...] = high
+    low_ref[...] = low
+    rounded = high.astype(F32) + low.astype(F32)
+    offset_ref[...] = jnp.dot(mean, rounded, precision=lax.Precision.HIGHEST)
+
+
+def act_kernel(
+    x_ref, stats_ref, gain_ref, bias_ref, turned_ref, slope_ref, kept_ref, mean_ref, high_ref, low_ref, offset_ref
+):
+    r, width = pl.program_id(0), x_ref.shape[1]
+
+    @at_first
+    def _():
+        newton(stats_ref, kept_ref, mean_ref, high_ref, low_ref, offset_ref)
+
+    x = x_ref[0]
+    white = dot(x, high_ref[...]) + dot(x, low_ref[...]) - offset_ref[0:1]
+    pre = gain_ref[0:1] * white + bias_ref[0:1]
+    gate = 0.5 * jnp.tanh(0.5 * pre) + 0.5
+    act = pre * gate
+    turned_ref[:, pl.ds(pl.multiple_of(r * width, width), width)] = act.T.astype(BF16)
+    slope_ref[0] = gate + act * (1.0 - gate)
 
 
 def tap_kernel(turned_ref, near_ref, far_ref, out_ref):
@@ -281,32 +302,37 @@
     lax.fori_loop(0, 3, column, 0)
 
 
-def grad_kernel(x_ref, grad_ref, white_ref, slope_ref, kept_ref, mean_ref, gain_ref, back_ref, sums_ref):
-    rows = x_ref.shape[0]
-    same = same_group()
-    gain = gain_ref[0:1]
-    mean = mean_ref[0:1]
-    white_high, white_low = spread_split(kept_ref[ITERS - 1, 0], same)
-
-    def row(r, carry):
-        gain_sum, bias_sum, products = carry
-        pre_grad = grad_ref[r] * slope_ref[r]
-        gain_sum = gain_sum + jnp.sum(pre_grad * white_ref[r], axis=0, keepdims=True)
-        bias_sum = bias_sum + jnp.sum(pre_grad, axis=0, keepdims=True)
-        high, low = split(pre_grad * gain)
-        back_ref[r] = dot(high, white_high) + dot(low, white_high) + dot(high, white_low)
-        products = products + lax.dot_general(
-            x_ref[r], jnp.concatenate([high, low], axis=1), (((0,), (0,)), ((), ())), preferred_element_type=F32
-        )
-        return gain_sum, bias_sum, products
-
-    nothing = jnp.zeros((1, C), F32)
-    gain_sum, bias_sum, products = lax.fori_loop(0, rows, row, (nothing, nothing, jnp.zeros((C, 2 * C), F32)))
-    mean_column = jnp.broadcast_to(mean, (C, C)).T
-    full = products[:, :C] + products[:, C:] - mean_column * (gain * bias_sum)
-    sums_ref[0:GS] = fold(full + full.T, same)
-    line = lax.broadcasted_iota(jnp.int32, (8, C), 0)
-    sums_ref[GS : GS + 8] = jnp.where(line == 0, gain_sum, jnp.where(line == 1, bias_sum, 0.0))
+def grad_kernel(
+    x_ref, grad_ref, slope_ref, kept_ref, mean_ref, gain_ref, back_ref, sums_ref, high_ref, low_ref, total_ref, bias_ref
+):
+    same = same_group()
+
+    @at_first
+    def _():
+        weighted = (spread(kept_ref[ITERS - 1, 0], same) * gain_ref[0:1]).T
+        high, low = split(weighted)
+        high_ref[...] = high
+        low_ref[...] = low
+        total_ref[...] = jnp.zeros_like(total_ref)
+        bias_ref[...] = jnp.zeros_like(bias_ref)
+
+    pre_grad = grad_ref[0] * slope_ref[0]
+    high, low = split(pre_grad)
+    bias_ref[0:1] += jnp.sum(pre_grad, axis=0, keepdims=True)
+    back_ref[0] = dot(high, high_ref[...]) + dot(low, high_ref[...]) + dot(high, low_ref[...])
+    turn = lambda part: lax.dot_general(x_ref[0], part, (((0,), (0,)), ((), ())), preferred_element_type=F32)
+    total_ref[...] += turn(high) + turn(low)
+
+    @at_last
+    def _():
+        bias_sum = bias_ref[0:1]
+        mean_column = jnp.broadcast_to(mean_ref[0:1], (C, C)).T
+        full = total_ref[...] - mean_column * bias_sum
+        gain_sum = jnp.sum(full * spread(kept_ref[ITERS - 1, 0], same), axis=0, keepdims=True)
+        full = full * gain_ref[0:1]
+        sums_ref[0:GS] = fold(full + full.T, same)
+        line = lax.broadcasted_iota(jnp.int32, (8, C), 0)
+        sums_ref[GS : GS + 8] = jnp.where(line == 0, gain_sum, jnp.where(line == 1, bias_sum, 0.0))
 
 
 def prepare_kernel(kept_ref, mean_ref, gain_ref, wide_ref, lines_ref, token_ref):
@@ -333,19 +359,18 @@
     leave(token_ref)
 
 
-def final_kernel(cell_count, x_ref, back_ref, sums_ref, wide_ref, lines_ref, after_ref, out_ref, vector_ref, high_ref, low_ref, constant_ref):
-    del after_ref
-
-    @pl.when(pl.program_id(0) == 0)
+def final_kernel(cell_count, x_ref, back_ref, sums_ref, wide_ref, lines_ref, out_ref, gain_out_ref, bias_out_ref, high_ref, low_ref, constant_ref):
+    @at_first
     def _():
-        derivative(cell_count, sums_ref, wide_ref, lines_ref, vector_ref, high_ref, low_ref, constant_ref)
+        outs = (gain_out_ref, bias_out_ref, high_ref, low_ref, constant_ref)
+        derivative(cell_count, sums_ref, wide_ref, lines_ref, *outs)
 
     x = x_ref[0]
     moved = dot(x, high_ref[...]) + dot(x, low_ref[...])
     out_ref[0] = (moved + back_ref[0] - constant_ref[0:1]).astype(BF16)
 
 
-def derivative(cell_count, sums_ref, wide_ref, lines_ref, vector_ref, high_ref, low_ref, constant_ref):
+def derivative(cell_count, sums_ref, wide_ref, lines_ref, gain_out_ref, bias_out_ref, high_ref, low_ref, constant_ref):
     same = same_group()
     eye = unit()
     whitener, normed = lines_ref[3, 0], lines_ref[3, 1]
@@ -373,7 +398,8 @@
     constant_ref[...] = jnp.dot(
         both, jnp.concatenate([rounded, spread(whitener, same)], axis=0), precision=lax.Precision.HIGHEST
     )
-    vector_ref[...] = sums_ref[GS:] * (1.0 / math.sqrt(cell_count))
+    for line, ref in enumerate((gain_out_ref, bias_out_ref)):
+        ref[...] = sums_ref[GS + line] * (1.0 / math.sqrt(cell_count))
 
 
 def stages(axes):
@@ -424,7 +450,17 @@
     odd_line = jnp.broadcast_to((lax.axis_index("rows") % 2 == 1).astype(F32), (8, C))
     even_line = 1.0 - odd_line
     halo = shape((d, width + 16, C), BF16)
-    first, second, token = run(pack_kernel, (halo, halo, TOKEN), (up, left, right, odd_line))
+    block = pl.BlockSpec((1, width, C), lambda r: (r, 0, 0))
+    low_block = pl.BlockSpec((1, width, C), lambda r: (rows - d + r, 0, 0))
+    halo_block = pl.BlockSpec((1, width + 16, C), lambda r: (r, 0, 0))
+    first, second, token = run(
+        pack_kernel,
+        (halo, halo, TOKEN),
+        (up, up, left, right, odd_line),
+        grid=(d,),
+        in_blocks={0: block, 1: low_block},
+        out_blocks={0: halo_block, 1: halo_block},
+    )
     first, second = swap(first, second, "rows")
     stats = run(stats_kernel, shape((2 * GS + 8, C), F32), (x,), after=(token,))
     scratch = (pltpu.VMEM((width + 32, C), F32),)
@@ -441,28 +477,35 @@
             )
         if number == count - 2:
             near_grad, *token = run(
-                near_kernel, (shape(cells, F32), TOKEN), (near_bands, weights), after=(stats,)
+                near_kernel,
+                (shape(cells, F32), TOKEN),
+                (near_bands, weights),
+                after=(stats,),
+                grid=(rows,),
+                out_blocks={0: block},
             )
         if number == count - 1:
             far_bands, act_grad, *token = run(
-                far_kernel,
+                functools.partial(far_kernel, rows),
                 (shape((3, 2 * d, width, C), BF16), shape(cells, F32), TOKEN),
                 (even_line, odd_line, first, second, weights, near_grad),
                 scratch=scratch,
                 after=(stats,),
+                grid=(rows,),
+                in_blocks={5: block},
+                out_blocks={1: block},
             )
         stats = run(merge_kernel, shape(stats.shape, F32), (stats, other), after=token)
 
-    turned, white, slope, kept, mean = run(
+    square = pltpu.VMEM((C, C), BF16)
+    turned, slope, kept, mean = run(
         act_kernel,
-        (
-            shape((C, rows * width), BF16),
-            shape(cells, F32),
-            shape(cells, F32),
-            shape((ITERS, 3, GS, C), F32),
-            shape((8, C), F32),
-        ),
+        (shape((C, rows * width), BF16), shape(cells, F32), shape((ITERS, 3, GS, C), F32), shape((8, C), F32)),
         (x, stats, gain, bias),
+        scratch=(square, square, pltpu.VMEM((8, C), F32)),
+        grid=(rows,),
+        in_blocks={0: block},
+        out_blocks={1: block},
     )
     taps = run(tap_kernel, shape((9, GS, C), F32), (turned, near_bands, far_bands))
 
@@ -472,11 +515,16 @@
     half = lax.dynamic_index_in_dim(halves, later, 0, False)
     half = add(half, lax.ppermute(lax.dynamic_index_in_dim(halves, 1 - later, 0, False), tap_axis, tap_pairs))
 
+    whole = lambda array: pl.BlockSpec(array.shape, lambda r: (0,) * array.ndim)
     back, sums = run(
         grad_kernel,
         (shape(cells, F32), shape((GS + 8, C), F32)),
-        (x, act_grad, white, slope, kept, mean, gain),
+        (x, act_grad, slope, kept, mean, gain),
+        scratch=(square, square, pltpu.VMEM((C, C), F32), pltpu.VMEM((8, C), F32)),
         after=(half,),
+        grid=(rows,),
+        in_blocks={0: block, 1: block, 2: block, 3: whole(kept), 4: whole(mean), 5: whole(gain)},
+        out_blocks={0: block},
     )
     row_stages = [stage for stage in stage_pairs[1:] if stage[0] == "rows"]
     tap_stages = row_stages + [stage for stage in stage_pairs[1:] if stage[0] != "rows"]
@@ -495,25 +543,25 @@
         if 2 <= number < count:
             last = number == count - 1
             half = add(half, lax.ppermute(half, *tap_stages[number - 1]), after=() if last else (sums,))
-    block = pl.BlockSpec((1, width, C), lambda r: (r, 0, 0))
-    input_grad, vectors = pl.pallas_call(
+    line_block = pl.BlockSpec((C,), lambda r: (0,))
+    input_grad, gain_grad, bias_grad = run(
         functools.partial(final_kernel, cell_count),
+        (shape(cells, BF16), shape((C,), F32), shape((C,), F32)),
+        (x, back, sums, wide, lines),
+        scratch=(square, square, pltpu.VMEM((8, C), F32)),
+        after=(half,),
         grid=(rows,),
-        out_shape=(shape(cells, BF16), shape((8, C), F32)),
-        in_specs=[block, block] + [VMEM_SPEC] * 3 + [pl.BlockSpec(memory_space=pl.ANY)],
-        out_specs=[block, VMEM_SPEC],
-        scratch_shapes=[pltpu.VMEM((C, C), BF16), pltpu.VMEM((C, C), BF16), pltpu.VMEM((8, C), F32)],
-        compiler_params=pltpu.CompilerParams(vmem_limit_bytes=8 * 2**20),
-        cost_estimate=NO_COST,
-    )(x, back, sums, wide, lines, half)
+        in_blocks={0: block, 1: block},
+        out_blocks={0: block, 1: line_block, 2: line_block},
+    )
     half = half * (1.0 / math.sqrt(cell_count))
     other = lax.ppermute(half, tap_axis, tap_pairs)
     taps = jnp.where(later == 0, jnp.stack([half, other]), jnp.stack([other, half]))
     return (
         input_grad.reshape(features.shape),
         taps.reshape(3, 3, GS, C),
-        vectors[0],
-        vectors[1],
+        gain_grad,
+        bias_grad,
     )
 
 

time: 92.4 us -> 98.9 us (1.070)
  waiting for transfers between devices: 20 us -> 23.6 us
  other arithmetic: 1.7 us -> 4.9 us
  local copies, waits for them, and re-layouts: 12.9 us -> 9.87 us
  Pallas kernels: 30.4 us -> 33.3 us
    ppermute x3, waiting for transfers between devices: 0.01 us -> 3.63 us  [shards(): lax.ppermute(half, *tap_stages[number - 1])]
    unnamed x38 -> x36, local copies, waits for them, and re-layouts: 12.3 us -> 9.18 us
    pallas_call x19, Pallas kernels: 30.4 us -> 33.3 us  [run(): pl.pallas_call(kernel, grid=grid, out_shape=out_shapes, in_specs=[in_bloc...]
    select_n x1, other arithmetic: 0.74 us -> 1.73 us  [shards(): jnp.where(later == 0, jnp.stack([half, other]), jnp.stack([other, half]))]
  transfers between devices with their start and end apart: 19 -> 19, of which waited for: 10 -> 11; matrix products, arithmetic and copies ran while one was open for 1% -> 0% of each run, Pallas kernels for 25% -> 23%
where the time goes in v2:
time: 98.9 us; the launch traced here: 98.6 us
  Pallas kernels  33.3 us (34%)
  starting transfers between devices  25.9 us (26%)
  waiting for transfers between devices  23.6 us (24%)
  local copies, waits for them, and re-layouts  9.87 us (10%)
  other arithmetic  4.9 us (5%)
  between operations  1 us (1%)
    pallas_call x19, Pallas kernels, run(): pl.pallas_call(kernel, grid=grid, out_shape=out_shapes, in_specs=[in_bloc...  33.3 us
    ppermute x5, waiting for transfers between devices, shards(): other = lax.ppermute(sums, *stage)  10.3 us
    unnamed x36, local copies, waits for them, and re-layouts  9.18 us
    ppermute x5, starting transfers between devices, shards(): other = lax.ppermute(stats, axis, pairs)  6.83 us
    ppermute x3, starting transfers between devices, swap(): lax.ppermute(part, axis, pairs)  6.63 us
    ppermute x5, waiting for transfers between devices, shards(): other = lax.ppermute(stats, axis, pairs)  6.14 us
    ppermute x5, starting transfers between devices, shards(): other = lax.ppermute(sums, *stage)  6.04 us
    ppermute x3, starting transfers between devices, shards(): lax.ppermute(half, *tap_stages[number - 1])  4.9 us
  transfers between devices with their start and end apart: 19, of which 11 were waited for; matrix products, arithmetic and copies ran while one was open for 0% of the time, Pallas kernels for 23%

profile of v2, /device:TPU:0, one launch (start us, length us, event | category | flops | bytes accessed | tf_op | source)
XLA Modules:
  0.0 98.6 jit_solution(7745702513199405568)
XLA Ops:
  0.7 0.9 slice_select_fusion
  1.5 3.0 %collective-permute-start = (bf16[8,8,256]{2,1,0:T(8,128)(2,1)S(1)}, bf16[8,8,256]{2,1,0:T(8,128)(2,1)S(1)}, u32[]{:S(2)}, u32[]{:S(2)}) collective-permute-start(bf16[8,8,256]{2,1,0:T(8,128)(2,1)S(1)} %slice_select_fusion), channel_id=1, source_target_pairs={{0,4},{4,0},{1,5},{5,1},{2,6},{6,2},{3,7},{7,3},{8,12},{12,8},{9,1... | collective-permute-start | bytes 98312 | tf_op jit(solution)/shard_map/ppermute | solution.py:426
  4.5 1.9 %collective-permute-done = bf16[8,8,256]{2,1,0:T(8,128)(2,1)S(1)} collective-permute-done((bf16[8,8,256]{2,1,0:T(8,128)(2,1)S(1)}, bf16[8,8,256]{2,1,0:T(8,128)(2,1)S(1)}, u32[]{:S(2)}, u32[]{:S(2)}) %collective-permute-start) | collective-permute-done | bytes 32800 | tf_op jit(solution)/shard_map/ppermute | solution.py:426
  6.4 1.2 %copy-done.3 = bf16[1,8,256,256]{3,2,1,0:T(8,128)(2,1)S(1)} copy-done((bf16[1,8,256,256]{3,2,1,0:T(8,128)(2,1)S(1)}, bf16[1,8,256,256]{3,2,1,0:T(8,128)(2,1)}, u32[]{:S(2)}) %copy-start.3) | copy-done | bytes 1048600
  7.6 2.4 %shard_map.84 = (bf16[6,272,256]{2,1,0:T(8,128)(2,1)}, bf16[6,272,256]{2,1,0:T(8,128)(2,1)}, f32[8,128]{1,0:T(8,128)S(1)}) custom-call(bf16[8,256,256]{2,1,0:T(8,128)(2,1)S(1)} %bitcast.18, bf16[8,256,256]{2,1,0:T(8,128)(2,1)S(1)} %bitcast.19, bf16[8,8,256]{2,1,0:T(8,128)(2,1)S(1)} %get-tuple-element.53.refs_2_.refs_1_, ...), custom_call_target="tpu_custom_call" | custom-call | tf_op jit(solution)/shard_map/pallas_call | solution.py:32
  10.0 2.1 %collective-permute-start.1 = (bf16[6,272,256]{2,1,0:T(8,128)(2,1)}, bf16[6,272,256]{2,1,0:T(8,128)(2,1)S(1)}, u32[]{:S(2)}, u32[]{:S(2)}) collective-permute-start(bf16[6,272,256]{2,1,0:T(8,128)(2,1)} %get-tuple-element.27), channel_id=1, source_target_pairs={{0,8},{16,24},{8,0},{24,16},{1,9},{17,25},{9,1},{25,17},{2,10},{18... | collective-permute-start | bytes 2506760 | tf_op jit(solution)/shard_map/ppermute | solution.py:426
  12.1 1.6 %collective-permute-start.2 = (bf16[6,272,256]{2,1,0:T(8,128)(2,1)}, bf16[6,272,256]{2,1,0:T(8,128)(2,1)}, u32[]{:S(2)}, u32[]{:S(2)}) collective-permute-start(bf16[6,272,256]{2,1,0:T(8,128)(2,1)} %get-tuple-element.28), channel_id=1, source_target_pairs={{8,16},{16,8},{9,17},{17,9},{10,18},{18,10},{11,19},{19,11},{12,20... | collective-permute-start | bytes 2506760 | tf_op jit(solution)/shard_map/ppermute | solution.py:426
  13.7 3.0 %shard_map.85.refs_0_ = f32[72,256]{1,0:T(8,128)S(1)} custom-call(bf16[8,256,256]{2,1,0:T(8,128)(2,1)S(1)} %bitcast.13, f32[8,128]{1,0:T(8,128)S(1)} %get-tuple-element.29.refs_1_), custom_call_target="tpu_custom_call" | custom-call | tf_op jit(solution)/shard_map/pallas_call | solution.py:32
  16.8 1.3 %collective-permute-done.3.refs_1_ = f32[72,256]{1,0:T(8,128)S(1)} collective-permute-done((f32[72,256]{1,0:T(8,128)S(1)}, f32[72,256]{1,0:T(8,128)S(1)}, u32[]{:S(2)}, u32[]{:S(2)}) %collective-permute-start.3) | collective-permute-done | bytes 73760 | tf_op jit(solution)/shard_map/ppermute | solution.py:468
  18.1 1.6 %collective-permute-start.4 = (f32[72,256]{1,0:T(8,128)S(1)}, f32[72,256]{1,0:T(8,128)S(1)}, u32[]{:S(2)}, u32[]{:S(2)}) collective-permute-start(f32[72,256]{1,0:T(8,128)S(1)} %shard_map.86.refs_0_), channel_id=1, source_target_pairs={{0,2},{1,3},{2,0},{3,1},{4,6},{5,7},{6,4},{7,5},{8,10},{9,11},{10,... | collective-permute-start | bytes 221192 | tf_op jit(solution)/shard_map/ppermute | solution.py:468
  19.6 2.9 %collective-permute-done.4.refs_1_ = f32[72,256]{1,0:T(8,128)S(1)} collective-permute-done((f32[72,256]{1,0:T(8,128)S(1)}, f32[72,256]{1,0:T(8,128)S(1)}, u32[]{:S(2)}, u32[]{:S(2)}) %collective-permute-start.4) | collective-permute-done | bytes 73760 | tf_op jit(solution)/shard_map/ppermute | solution.py:468
  22.5 1.6 %collective-permute-start.5 = (f32[72,256]{1,0:T(8,128)S(1)}, f32[72,256]{1,0:T(8,128)S(1)}, u32[]{:S(2)}, u32[]{:S(2)}) collective-permute-start(f32[72,256]{1,0:T(8,128)S(1)} %shard_map.87.refs_4_.refs_0_), channel_id=1, source_target_pairs={{0,4},{4,0},{1,5},{5,1},{2,6},{6,2},{3,7},{7,3},{8,12},{12,8},{9,1... | collective-permute-start | bytes 221192 | tf_op jit(solution)/shard_map/ppermute | solution.py:468
  24.1 0.8 shard_map.88
  24.9 2.0 %collective-permute-done.5.refs_1_ = f32[72,256]{1,0:T(8,128)S(1)} collective-permute-done((f32[72,256]{1,0:T(8,128)S(1)}, f32[72,256]{1,0:T(8,128)S(1)}, u32[]{:S(2)}, u32[]{:S(2)}) %collective-permute-start.5) | collective-permute-done | bytes 73760 | tf_op jit(solution)/shard_map/ppermute | solution.py:468
  26.9 3.5 %collective-permute-start.6 = (f32[72,256]{1,0:T(8,128)S(1)}, f32[72,256]{1,0:T(8,128)S(1)}, u32[]{:S(2)}, u32[]{:S(2)}) collective-permute-start(f32[72,256]{1,0:T(8,128)S(1)} %shard_map.89.refs_2_.refs_0_), channel_id=1, source_target_pairs={{0,8},{8,0},{16,24},{24,16},{1,9},{9,1},{17,25},{25,17},{2,10},{10... | collective-permute-start | bytes 221192 | tf_op jit(solution)/shard_map/ppermute | solution.py:468
  30.5 2.7 %shard_map.90 = (f32[8,256,256]{2,1,0:T(8,128)S(1)}, f32[8,128]{1,0:T(8,128)S(1)}) custom-call(bf16[3,8,256,256]{3,2,1,0:T(8,128)(2,1)S(1)} %get-tuple-element.31.refs_0_.refs_1_, bf16[9,256,256]{2,1,0:T(8,128)(2,1)S(1)} %get-tuple-element.30.refs_1_.refs_4_, f32[72,256]{1,0:T(8,128)S(1)} %shard_map.89.refs_2_.refs_0_), custom_call_target="tpu_custom_call" | custom-call | tf_op jit(solution)/shard_map/pallas_call | solution.py:32
  33.2 1.3 %copy-done.5 = f32[8,256,256]{2,1,0:T(8,128)} copy-done((f32[8,256,256]{2,1,0:T(8,128)}, f32[8,256,256]{2,1,0:T(8,128)S(1)}, u32[]{:S(2)}) %copy-start.5) | copy-done | bytes 2097176
  34.8 1.6 %copy-done.6 = f32[8,256,256]{2,1,0:T(8,128)S(1)} copy-done((f32[8,256,256]{2,1,0:T(8,128)S(1)}, f32[8,256,256]{2,1,0:T(8,128)}, u32[]{:S(2)}) %copy-start.6) | copy-done | bytes 2097176
  36.3 5.0 %shard_map.92 = (bf16[3,12,256,256]{3,2,1,0:T(8,128)(2,1)S(1)}, f32[8,256,256]{2,1,0:T(8,128)S(1)}, f32[8,128]{1,0:T(8,128)S(1)}) custom-call(f32[8,256]{1,0:T(8,128)S(1)} %sub.10.refs_0_, f32[8,256]{1,0:T(8,128)S(1)} %broadcast_in_dim.8.refs_4_.refs_1_, bf16[6,272,256]{2,1,0:T(8,128)(2,1)S(1)} %collective-permute-done.1.refs_2_, ...), custom_call_target="tpu_custom_call" | custom-call | tf_op jit(solution)/shard_map/pallas_call | solution.py:32
  41.5 5.1 %shard_map.94 = (bf16[256,2048]{1,0:T(8,128)(2,1)S(1)}, f32[8,256,256]{2,1,0:T(8,128)S(1)}, f32[5,3,32,256]{3,2,1,0:T(8,128)S(1)}, f32[8,256]{1,0:T(8,128)S(1)}) custom-call(bf16[8,256,256]{2,1,0:T(8,128)(2,1)S(1)} %bitcast.14, f32[72,256]{1,0:T(8,128)S(1)} %shard_map.93.refs_1_, f32[8,256]{1,0:T(8,128)S(1)} %broadcast_in_dim.20.refs_2_.refs_5_, ...), custom_call_target="tpu_custom_call" | custom-call | tf_op jit(solution)/shard_map/pallas_call | solution.py:32
  46.6 3.0 %shard_map.95 = f32[9,32,256]{2,1,0:T(8,128)S(1)} custom-call(bf16[256,2048]{1,0:T(8,128)(2,1)S(1)} %get-tuple-element.40.refs_0_, bf16[3,8,256,256]{3,2,1,0:T(8,128)(2,1)S(1)} %copy-done.2, bf16[3,12,256,256]{3,2,1,0:T(8,128)(2,1)S(1)} %get-tuple-element.41.refs_2_), custom_call_target="tpu_custom_call" | custom-call | tf_op jit(solution)/shard_map/pallas_call | solution.py:32
  49.7 0.7 dynamic-slice_bitcast_fusion
  50.3 1.7 %collective-permute-done.8 = f32[144,256]{1,0:T(8,128)} collective-permute-done((f32[144,256]{1,0:T(8,128)}, f32[144,256]{1,0:T(8,128)}, u32[]{:S(2)}, u32[]{:S(2)}) %collective-permute-start.8) | collective-permute-done | bytes 147488 | tf_op jit(solution)/shard_map/ppermute | solution.py:516
  52.1 0.9 bitcast_add_fusion.refs_6_.refs_0_
  53.0 1.5 %collective-permute-start.14 = (f32[144,256]{1,0:T(8,128)S(1)}, f32[144,256]{1,0:T(8,128)S(1)}, u32[]{:S(2)}, u32[]{:S(2)}) collective-permute-start(f32[144,256]{1,0:T(8,128)S(1)} %bitcast_add_fusion.refs_6_.refs_0_), channel_id=1, source_target_pairs={{0,8},{8,0},{16,24},{24,16},{1,9},{9,1},{17,25},{25,17},{2,10},{10... | collective-permute-start | bytes 442376 | tf_op jit(solution)/shard_map/ppermute | solution.py:531
  54.5 1.6 %copy-done.8 = f32[8,256,256]{2,1,0:T(8,128)S(1)} copy-done((f32[8,256,256]{2,1,0:T(8,128)S(1)}, f32[8,256,256]{2,1,0:T(8,128)}, u32[]{:S(2)}) %copy-start.8) | copy-done | bytes 2097176
  56.1 1.0 %copy-done.12 = f32[5,3,32,256]{3,2,1,0:T(8,128)S(1)} copy-done((f32[5,3,32,256]{3,2,1,0:T(8,128)S(1)}, f32[5,3,32,256]{3,2,1,0:T(8,128)}, u32[]{:S(2)}) %copy-start.12) | copy-done | bytes 491544
  57.1 3.3 %shard_map.96 = (f32[8,256,256]{2,1,0:T(8,128)S(1)}, f32[40,256]{1,0:T(8,128)S(1)}) custom-call(bf16[8,256,256]{2,1,0:T(8,128)(2,1)S(1)} %bitcast.15, f32[8,256,256]{2,1,0:T(8,128)S(1)} %copy-done.8, f32[8,256,256]{2,1,0:T(8,128)S(1)} %get-tuple-element.37.refs_2_, f32[5,3,32,256]{3,2,1,0:T(8,128)S(1)} %copy-done.12, ...), custom_call_target="tpu_custom_call" | custom-call | tf_op jit(solution)/shard_map/pallas_call | solution.py:32
  60.4 1.3 %copy-done.9 = f32[8,256,256]{2,1,0:T(8,128)} copy-done((f32[8,256,256]{2,1,0:T(8,128)}, f32[8,256,256]{2,1,0:T(8,128)S(1)}, u32[]{:S(2)}) %copy-start.9) | copy-done | bytes 2097176
  61.8 1.8 %collective-permute-start.15 = (f32[144,256]{1,0:T(8,128)S(1)}, f32[144,256]{1,0:T(8,128)S(1)}, u32[]{:S(2)}, u32[]{:S(2)}) collective-permute-start(f32[144,256]{1,0:T(8,128)S(1)} %shard_map.99.refs_0_), channel_id=1, source_target_pairs={{0,16},{8,24},{16,0},{24,8},{1,17},{9,25},{17,1},{25,9},{2,18},{10... | collective-permute-start | bytes 442376 | tf_op jit(solution)/shard_map/ppermute | solution.py:545
  63.6 1.2 %collective-permute-done.9 = f32[40,256]{1,0:T(8,128)S(1)} collective-permute-done((f32[40,256]{1,0:T(8,128)S(1)}, f32[40,256]{1,0:T(8,128)S(1)}, u32[]{:S(2)}, u32[]{:S(2)}) %collective-permute-start.9) | collective-permute-done | bytes 40992 | tf_op jit(solution)/shard_map/ppermute | solution.py:533
  64.8 1.5 %collective-permute-start.10 = (f32[40,256]{1,0:T(8,128)S(1)}, f32[40,256]{1,0:T(8,128)S(1)}, u32[]{:S(2)}, u32[]{:S(2)}) collective-permute-start(f32[40,256]{1,0:T(8,128)S(1)} %add.42), channel_id=1, source_target_pairs={{0,2},{1,3},{2,0},{3,1},{4,6},{5,7},{6,4},{7,5},{8,10},{9,11},{10,... | collective-permute-start | bytes 122888 | tf_op jit(solution)/shard_map/ppermute | solution.py:533
  66.3 2.5 %collective-permute-done.10 = f32[40,256]{1,0:T(8,128)S(1)} collective-permute-done((f32[40,256]{1,0:T(8,128)S(1)}, f32[40,256]{1,0:T(8,128)S(1)}, u32[]{:S(2)}, u32[]{:S(2)}) %collective-permute-start.10) | collective-permute-done | bytes 40992 | tf_op jit(solution)/shard_map/ppermute | solution.py:533
  68.8 1.5 %collective-permute-start.11 = (f32[40,256]{1,0:T(8,128)S(1)}, f32[40,256]{1,0:T(8,128)S(1)}, u32[]{:S(2)}, u32[]{:S(2)}) collective-permute-start(f32[40,256]{1,0:T(8,128)S(1)} %add.43), channel_id=1, source_target_pairs={{0,4},{4,0},{1,5},{5,1},{2,6},{6,2},{3,7},{7,3},{8,12},{12,8},{9,1... | collective-permute-start | bytes 122888 | tf_op jit(solution)/shard_map/ppermute | solution.py:533
  70.3 2.5 %collective-permute-done.11 = f32[40,256]{1,0:T(8,128)S(1)} collective-permute-done((f32[40,256]{1,0:T(8,128)S(1)}, f32[40,256]{1,0:T(8,128)S(1)}, u32[]{:S(2)}, u32[]{:S(2)}) %collective-permute-start.11) | collective-permute-done | bytes 40992 | tf_op jit(solution)/shard_map/ppermute | solution.py:533
  72.8 1.6 %collective-permute-start.16 = (f32[144,256]{1,0:T(8,128)S(1)}, f32[144,256]{1,0:T(8,128)S(1)}, u32[]{:S(2)}, u32[]{:S(2)}) collective-permute-start(f32[144,256]{1,0:T(8,128)S(1)} %shard_map.100.refs_0_), channel_id=1, source_target_pairs={{0,2},{1,3},{2,0},{3,1},{4,6},{5,7},{6,4},{7,5},{8,10},{9,11},{10,... | collective-permute-start | bytes 442376 | tf_op jit(solution)/shard_map/ppermute | solution.py:545
  74.4 1.8 %collective-permute-start.12 = (f32[40,256]{1,0:T(8,128)S(1)}, f32[40,256]{1,0:T(8,128)S(1)}, u32[]{:S(2)}, u32[]{:S(2)}) collective-permute-start(f32[40,256]{1,0:T(8,128)S(1)} %add.44.refs_2_), channel_id=1, source_target_pairs={{0,8},{8,0},{16,24},{24,16},{1,9},{9,1},{17,25},{25,17},{2,10},{10... | collective-permute-start | bytes 122888 | tf_op jit(solution)/shard_map/ppermute | solution.py:533
  76.2 2.2 %collective-permute-done.12 = f32[40,256]{1,0:T(8,128)S(1)} collective-permute-done((f32[40,256]{1,0:T(8,128)S(1)}, f32[40,256]{1,0:T(8,128)S(1)}, u32[]{:S(2)}, u32[]{:S(2)}) %collective-permute-start.12) | collective-permute-done | bytes 40992 | tf_op jit(solution)/shard_map/ppermute | solution.py:533
  78.5 1.6 %collective-permute-start.17 = (f32[144,256]{1,0:T(8,128)S(1)}, f32[144,256]{1,0:T(8,128)S(1)}, u32[]{:S(2)}, u32[]{:S(2)}) collective-permute-start(f32[144,256]{1,0:T(8,128)S(1)} %shard_map.101), channel_id=1, source_target_pairs={{0,4},{4,0},{1,5},{5,1},{2,6},{6,2},{3,7},{7,3},{8,12},{12,8},{9,1... | collective-permute-start | bytes 442376 | tf_op jit(solution)/shard_map/ppermute | solution.py:545
  80.0 3.6 %collective-permute-done.17 = f32[144,256]{1,0:T(8,128)S(1)} collective-permute-done((f32[144,256]{1,0:T(8,128)S(1)}, f32[144,256]{1,0:T(8,128)S(1)}, u32[]{:S(2)}, u32[]{:S(2)}) %collective-permute-start.17) | collective-permute-done | bytes 147488 | tf_op jit(solution)/shard_map/ppermute | solution.py:545
  83.7 0.7 fusion
  84.3 0.7 broadcast_multiply_fusion
  85.0 1.2 %collective-permute-start.13 = (f32[40,256]{1,0:T(8,128)S(1)}, f32[40,256]{1,0:T(8,128)S(1)}, u32[]{:S(2)}, u32[]{:S(2)}) collective-permute-start(f32[40,256]{1,0:T(8,128)S(1)} %add.45.refs_3_.refs_0_.refs_2_), channel_id=1, source_target_pairs={{0,16},{8,24},{16,0},{24,8},{1,17},{9,25},{17,1},{25,9},{2,18},{10... | collective-permute-start | bytes 122888 | tf_op jit(solution)/shard_map/ppermute | solution.py:533
  86.2 1.0 %copy-done.13 = f32[5,3,32,256]{3,2,1,0:T(8,128)S(1)} copy-done((f32[5,3,32,256]{3,2,1,0:T(8,128)S(1)}, f32[5,3,32,256]{3,2,1,0:T(8,128)}, u32[]{:S(2)}) %copy-start.13) | copy-done | bytes 491544
  87.3 0.8 shard_map.97
  88.1 1.8 %collective-permute-done.13.refs_1_ = f32[40,256]{1,0:T(8,128)S(1)} collective-permute-done((f32[40,256]{1,0:T(8,128)S(1)}, f32[40,256]{1,0:T(8,128)S(1)}, u32[]{:S(2)}, u32[]{:S(2)}) %collective-permute-start.13) | collective-permute-done | bytes 40992 | tf_op jit(solution)/shard_map/ppermute | solution.py:533
  89.9 6.9 %shard_map.102 = (bf16[8,256,256]{2,1,0:T(8,128)(2,1)}, f32[256]{0:T(256)}, f32[256]{0:T(256)}) custom-call(bf16[8,256,256]{2,1,0:T(8,128)(2,1)S(1)} %bitcast.16, f32[8,256,256]{2,1,0:T(8,128)S(1)} %copy-done.10, f32[40,256]{1,0:T(8,128)S(1)} %shard_map.98.refs_2_, bf16[9,2,256,256]{3,2,1,0:T(8,128)(2,1)S(1)} %get-tuple-element.45.refs_3_, ...), custom_call_target="tpu_custom_call" | custom-call | tf_op jit(solution)/shard_map/pallas_call | solution.py:32
  96.8 1.7 %maximum_select_fusion = f32[2,144,256]{2,1,0:T(8,128)} fusion(f32[1,144,256]{2,1,0:T(8,128)} %bitcast.8, f32[1,144,256]{2,1,0:T(8,128)S(1)} %copy-done.15, pred[]{:T(512)S(6)} %eq.15), kind=kLoop, calls=%fused_computation | loop fusion | flops 221184 | bytes 589825 | tf_op jit(solution)/shard_map/jit(_where)/select_n | solution.py:559
  (60 shorter events, 0.4 us)
Async XLA Ops:
  0.6 13.1 %copy-start = (bf16[1,8,256,256]{3,2,1,0:T(8,128)(2,1)S(1)}, bf16[1,8,256,256]{3,2,1,0:T(8,128)(2,1)}, u32[]{:S(2)}) copy-start(bf16[1,8,256,256]{3,2,1,0:T(8,128)(2,1)} %param.5) | copy-start | bytes 3145732
  1.5 4.9 %collective-permute-start = (bf16[8,8,256]{2,1,0:T(8,128)(2,1)S(1)}, bf16[8,8,256]{2,1,0:T(8,128)(2,1)S(1)}, u32[]{:S(2)}, u32[]{:S(2)}) collective-permute-start(bf16[8,8,256]{2,1,0:T(8,128)(2,1)S(1)} %slice_select_fusion), channel_id=1, source_target_pairs={{0,4},{4,0},{1,5},{5,1},{2,6},{6,2},{3,7},{7,3},{8,12},{12,8},{9,1... | collective-permute-start | bytes 98312 | tf_op jit(solution)/shard_map/ppermute | solution.py:426
  6.4 1.2 %copy-start.3 = (bf16[1,8,256,256]{3,2,1,0:T(8,128)(2,1)S(1)}, bf16[1,8,256,256]{3,2,1,0:T(8,128)(2,1)}, u32[]{:S(2)}) copy-start(bf16[1,8,256,256]{3,2,1,0:T(8,128)(2,1)} %param.6) | copy-start | bytes 3145732
  7.6 16.5 %copy-start.4 = (bf16[1,8,256,256]{3,2,1,0:T(8,128)(2,1)S(1)}, bf16[1,8,256,256]{3,2,1,0:T(8,128)(2,1)}, u32[]{:S(2)}) copy-start(bf16[1,8,256,256]{3,2,1,0:T(8,128)(2,1)} %param.6) | copy-start | bytes 3145732
  7.6 16.5 %copy-start.14 = (bf16[3,3,32,256]{3,2,1,0:T(8,128)(2,1)S(1)}, bf16[3,3,32,256]{3,2,1,0:T(8,128)(2,1)}, u32[]{:S(2)}) copy-start(bf16[3,3,32,256]{3,2,1,0:T(8,128)(2,1)} %param.7) | copy-start | bytes 442372
  10.0 24.7 %collective-permute-start.1 = (bf16[6,272,256]{2,1,0:T(8,128)(2,1)}, bf16[6,272,256]{2,1,0:T(8,128)(2,1)S(1)}, u32[]{:S(2)}, u32[]{:S(2)}) collective-permute-start(bf16[6,272,256]{2,1,0:T(8,128)(2,1)} %get-tuple-element.27), channel_id=1, source_target_pairs={{0,8},{16,24},{8,0},{24,16},{1,9},{17,25},{9,1},{25,17},{2,10},{18... | collective-permute-start | bytes 2506760 | tf_op jit(solution)/shard_map/ppermute | solution.py:426
  12.1 22.6 %collective-permute-start.2 = (bf16[6,272,256]{2,1,0:T(8,128)(2,1)}, bf16[6,272,256]{2,1,0:T(8,128)(2,1)}, u32[]{:S(2)}, u32[]{:S(2)}) collective-permute-start(bf16[6,272,256]{2,1,0:T(8,128)(2,1)} %get-tuple-element.28), channel_id=1, source_target_pairs={{8,16},{16,8},{9,17},{17,9},{10,18},{18,10},{11,19},{19,11},{12,20... | collective-permute-start | bytes 2506760 | tf_op jit(solution)/shard_map/ppermute | solution.py:426
  16.7 1.3 %collective-permute-start.3 = (f32[72,256]{1,0:T(8,128)S(1)}, f32[72,256]{1,0:T(8,128)S(1)}, u32[]{:S(2)}, u32[]{:S(2)}) collective-permute-start(f32[72,256]{1,0:T(8,128)S(1)} %shard_map.85.refs_0_), channel_id=1, source_target_pairs={{0,1},{1,0},{2,3},{3,2},{4,5},{5,4},{6,7},{7,6},{8,9},{9,8},{10,11... | collective-permute-start | bytes 221192 | tf_op jit(solution)/shard_map/ppermute | solution.py:468
  18.1 4.4 %collective-permute-start.4 = (f32[72,256]{1,0:T(8,128)S(1)}, f32[72,256]{1,0:T(8,128)S(1)}, u32[]{:S(2)}, u32[]{:S(2)}) collective-permute-start(f32[72,256]{1,0:T(8,128)S(1)} %shard_map.86.refs_0_), channel_id=1, source_target_pairs={{0,2},{1,3},{2,0},{3,1},{4,6},{5,7},{6,4},{7,5},{8,10},{9,11},{10,... | collective-permute-start | bytes 221192 | tf_op jit(solution)/shard_map/ppermute | solution.py:468
  22.5 4.4 %collective-permute-start.5 = (f32[72,256]{1,0:T(8,128)S(1)}, f32[72,256]{1,0:T(8,128)S(1)}, u32[]{:S(2)}, u32[]{:S(2)}) collective-permute-start(f32[72,256]{1,0:T(8,128)S(1)} %shard_map.87.refs_4_.refs_0_), channel_id=1, source_target_pairs={{0,4},{4,0},{1,5},{5,1},{2,6},{6,2},{3,7},{7,3},{8,12},{12,8},{9,1... | collective-permute-start | bytes 221192 | tf_op jit(solution)/shard_map/ppermute | solution.py:468
  24.9 8.3 %copy-start.1 = (bf16[3,8,256,256]{3,2,1,0:T(8,128)(2,1)}, bf16[3,8,256,256]{3,2,1,0:T(8,128)(2,1)S(1)}, u32[]{:S(2)}) copy-start(bf16[3,8,256,256]{3,2,1,0:T(8,128)(2,1)S(1)} %get-tuple-element.31.refs_0_.refs_1_) | copy-start | bytes 9437188
  26.9 7.7 %collective-permute-start.6 = (f32[72,256]{1,0:T(8,128)S(1)}, f32[72,256]{1,0:T(8,128)S(1)}, u32[]{:S(2)}, u32[]{:S(2)}) collective-permute-start(f32[72,256]{1,0:T(8,128)S(1)} %shard_map.89.refs_2_.refs_0_), channel_id=1, source_target_pairs={{0,8},{8,0},{16,24},{24,16},{1,9},{9,1},{17,25},{25,17},{2,10},{10... | collective-permute-start | bytes 221192 | tf_op jit(solution)/shard_map/ppermute | solution.py:468
  33.2 1.3 %copy-start.5 = (f32[8,256,256]{2,1,0:T(8,128)}, f32[8,256,256]{2,1,0:T(8,128)S(1)}, u32[]{:S(2)}) copy-start(f32[8,256,256]{2,1,0:T(8,128)S(1)} %get-tuple-element.33.refs_5_) | copy-start | bytes 6291460
  34.6 6.8 %collective-permute-start.7 = (f32[72,256]{1,0:T(8,128)S(1)}, f32[72,256]{1,0:T(8,128)S(1)}, u32[]{:S(2)}, u32[]{:S(2)}) collective-permute-start(f32[72,256]{1,0:T(8,128)S(1)} %shard_map.91.refs_6_.refs_0_), channel_id=1, source_target_pairs={{0,16},{8,24},{16,0},{24,8},{1,17},{9,25},{17,1},{25,9},{2,18},{10... | collective-permute-start | bytes 221192 | tf_op jit(solution)/shard_map/ppermute | solution.py:468
  34.7 1.6 %copy-start.6 = (f32[8,256,256]{2,1,0:T(8,128)S(1)}, f32[8,256,256]{2,1,0:T(8,128)}, u32[]{:S(2)}) copy-start(f32[8,256,256]{2,1,0:T(8,128)} %copy-done.5) | copy-start | bytes 6291460
  36.3 5.1 %copy-start.16 = (f32[256]{0:T(256)S(1)}, f32[256]{0:T(256)}, u32[]{:S(2)}) copy-start(f32[256]{0:T(256)} %param.8) | copy-start | bytes 3076
  36.3 5.1 %copy-start.17 = (f32[256]{0:T(256)S(1)}, f32[256]{0:T(256)}, u32[]{:S(2)}) copy-start(f32[256]{0:T(256)} %param.9) | copy-start | bytes 3076
  36.3 10.3 %copy-start.2 = (bf16[3,8,256,256]{3,2,1,0:T(8,128)(2,1)S(1)}, bf16[3,8,256,256]{3,2,1,0:T(8,128)(2,1)}, u32[]{:S(2)}) copy-start(bf16[3,8,256,256]{3,2,1,0:T(8,128)(2,1)} %copy-done.1) | copy-start | bytes 9437188
  41.4 8.3 %copy-start.7 = (f32[8,256,256]{2,1,0:T(8,128)}, f32[8,256,256]{2,1,0:T(8,128)S(1)}, u32[]{:S(2)}) copy-start(f32[8,256,256]{2,1,0:T(8,128)S(1)} %get-tuple-element.35.refs_1_) | copy-start | bytes 6291460
  46.6 3.1 %copy-start.11 = (f32[5,3,32,256]{3,2,1,0:T(8,128)}, f32[5,3,32,256]{3,2,1,0:T(8,128)S(1)}, u32[]{:S(2)}) copy-start(f32[5,3,32,256]{3,2,1,0:T(8,128)S(1)} %get-tuple-element.38.refs_3_.refs_0_) | copy-start | bytes 1474564
  50.3 1.7 %collective-permute-start.8 = (f32[144,256]{1,0:T(8,128)}, f32[144,256]{1,0:T(8,128)}, u32[]{:S(2)}, u32[]{:S(2)}) collective-permute-start(f32[144,256]{1,0:T(8,128)} %dynamic-slice_bitcast_fusion), channel_id=1, source_target_pairs={{0,1},{1,0},{2,3},{3,2},{4,5},{5,4},{6,7},{7,6},{8,9},{9,8},{10,11... | collective-permute-start | bytes 442376 | tf_op jit(solution)/shard_map/ppermute | solution.py:516
  53.0 8.8 %collective-permute-start.14 = (f32[144,256]{1,0:T(8,128)S(1)}, f32[144,256]{1,0:T(8,128)S(1)}, u32[]{:S(2)}, u32[]{:S(2)}) collective-permute-start(f32[144,256]{1,0:T(8,128)S(1)} %bitcast_add_fusion.refs_6_.refs_0_), channel_id=1, source_target_pairs={{0,8},{8,0},{16,24},{24,16},{1,9},{9,1},{17,25},{25,17},{2,10},{10... | collective-permute-start | bytes 442376 | tf_op jit(solution)/shard_map/ppermute | solution.py:531
  54.5 1.6 %copy-start.8 = (f32[8,256,256]{2,1,0:T(8,128)S(1)}, f32[8,256,256]{2,1,0:T(8,128)}, u32[]{:S(2)}) copy-start(f32[8,256,256]{2,1,0:T(8,128)} %copy-done.7) | copy-start | bytes 6291460
  56.1 1.0 %copy-start.12 = (f32[5,3,32,256]{3,2,1,0:T(8,128)S(1)}, f32[5,3,32,256]{3,2,1,0:T(8,128)}, u32[]{:S(2)}) copy-start(f32[5,3,32,256]{3,2,1,0:T(8,128)} %copy-done.11) | copy-start | bytes 1474564
  60.4 1.3 %copy-start.9 = (f32[8,256,256]{2,1,0:T(8,128)}, f32[8,256,256]{2,1,0:T(8,128)S(1)}, u32[]{:S(2)}) copy-start(f32[8,256,256]{2,1,0:T(8,128)S(1)} %get-tuple-element.42.refs_1_) | copy-start | bytes 6291460
  61.8 28.1 %copy-start.10 = (f32[8,256,256]{2,1,0:T(8,128)S(1)}, f32[8,256,256]{2,1,0:T(8,128)}, u32[]{:S(2)}) copy-start(f32[8,256,256]{2,1,0:T(8,128)} %copy-done.9) | copy-start | bytes 6291460
  61.8 11.0 %collective-permute-start.15 = (f32[144,256]{1,0:T(8,128)S(1)}, f32[144,256]{1,0:T(8,128)S(1)}, u32[]{:S(2)}, u32[]{:S(2)}) collective-permute-start(f32[144,256]{1,0:T(8,128)S(1)} %shard_map.99.refs_0_), channel_id=1, source_target_pairs={{0,16},{8,24},{16,0},{24,8},{1,17},{9,25},{17,1},{25,9},{2,18},{10... | collective-permute-start | bytes 442376 | tf_op jit(solution)/shard_map/ppermute | solution.py:545
  63.6 1.2 %collective-permute-start.9 = (f32[40,256]{1,0:T(8,128)S(1)}, f32[40,256]{1,0:T(8,128)S(1)}, u32[]{:S(2)}, u32[]{:S(2)}) collective-permute-start(f32[40,256]{1,0:T(8,128)S(1)} %get-tuple-element.43.refs_2_), channel_id=1, source_target_pairs={{0,1},{1,0},{2,3},{3,2},{4,5},{5,4},{6,7},{7,6},{8,9},{9,8},{10,11... | collective-permute-start | bytes 122888 | tf_op jit(solution)/shard_map/ppermute | solution.py:533
  64.8 4.0 %collective-permute-start.10 = (f32[40,256]{1,0:T(8,128)S(1)}, f32[40,256]{1,0:T(8,128)S(1)}, u32[]{:S(2)}, u32[]{:S(2)}) collective-permute-start(f32[40,256]{1,0:T(8,128)S(1)} %add.42), channel_id=1, source_target_pairs={{0,2},{1,3},{2,0},{3,1},{4,6},{5,7},{6,4},{7,5},{8,10},{9,11},{10,... | collective-permute-start | bytes 122888 | tf_op jit(solution)/shard_map/ppermute | solution.py:533
  68.8 4.0 %collective-permute-start.11 = (f32[40,256]{1,0:T(8,128)S(1)}, f32[40,256]{1,0:T(8,128)S(1)}, u32[]{:S(2)}, u32[]{:S(2)}) collective-permute-start(f32[40,256]{1,0:T(8,128)S(1)} %add.43), channel_id=1, source_target_pairs={{0,4},{4,0},{1,5},{5,1},{2,6},{6,2},{3,7},{7,3},{8,12},{12,8},{9,1... | collective-permute-start | bytes 122888 | tf_op jit(solution)/shard_map/ppermute | solution.py:533
  72.8 5.6 %collective-permute-start.16 = (f32[144,256]{1,0:T(8,128)S(1)}, f32[144,256]{1,0:T(8,128)S(1)}, u32[]{:S(2)}, u32[]{:S(2)}) collective-permute-start(f32[144,256]{1,0:T(8,128)S(1)} %shard_map.100.refs_0_), channel_id=1, source_target_pairs={{0,2},{1,3},{2,0},{3,1},{4,6},{5,7},{6,4},{7,5},{8,10},{9,11},{10,... | collective-permute-start | bytes 442376 | tf_op jit(solution)/shard_map/ppermute | solution.py:545
  74.4 4.0 %collective-permute-start.12 = (f32[40,256]{1,0:T(8,128)S(1)}, f32[40,256]{1,0:T(8,128)S(1)}, u32[]{:S(2)}, u32[]{:S(2)}) collective-permute-start(f32[40,256]{1,0:T(8,128)S(1)} %add.44.refs_2_), channel_id=1, source_target_pairs={{0,8},{8,0},{16,24},{24,16},{1,9},{9,1},{17,25},{25,17},{2,10},{10... | collective-permute-start | bytes 122888 | tf_op jit(solution)/shard_map/ppermute | solution.py:533
  78.5 5.2 %collective-permute-start.17 = (f32[144,256]{1,0:T(8,128)S(1)}, f32[144,256]{1,0:T(8,128)S(1)}, u32[]{:S(2)}, u32[]{:S(2)}) collective-permute-start(f32[144,256]{1,0:T(8,128)S(1)} %shard_map.101), channel_id=1, source_target_pairs={{0,4},{4,0},{1,5},{5,1},{2,6},{6,2},{3,7},{7,3},{8,12},{12,8},{9,1... | collective-permute-start | bytes 442376 | tf_op jit(solution)/shard_map/ppermute | solution.py:545
  85.0 11.8 %collective-permute-start.18 = (f32[144,256]{1,0:T(8,128)}, f32[144,256]{1,0:T(8,128)}, u32[]{:S(2)}, u32[]{:S(2)}) collective-permute-start(f32[144,256]{1,0:T(8,128)} %broadcast_multiply_fusion), channel_id=1, source_target_pairs={{0,1},{1,0},{2,3},{3,2},{4,5},{5,4},{6,7},{7,6},{8,9},{9,8},{10,11... | collective-permute-start | bytes 442376 | tf_op jit(solution)/shard_map/ppermute | solution.py:558
  85.0 4.9 %collective-permute-start.13 = (f32[40,256]{1,0:T(8,128)S(1)}, f32[40,256]{1,0:T(8,128)S(1)}, u32[]{:S(2)}, u32[]{:S(2)}) collective-permute-start(f32[40,256]{1,0:T(8,128)S(1)} %add.45.refs_3_.refs_0_.refs_2_), channel_id=1, source_target_pairs={{0,16},{8,24},{16,0},{24,8},{1,17},{9,25},{17,1},{25,9},{2,18},{10... | collective-permute-start | bytes 122888 | tf_op jit(solution)/shard_map/ppermute | solution.py:533
  86.2 1.0 %copy-start.13 = (f32[5,3,32,256]{3,2,1,0:T(8,128)S(1)}, f32[5,3,32,256]{3,2,1,0:T(8,128)}, u32[]{:S(2)}) copy-start(f32[5,3,32,256]{3,2,1,0:T(8,128)} %copy-done.11) | copy-start | bytes 1474564
  89.9 6.9 %copy-start.15 = (f32[1,144,256]{2,1,0:T(8,128)S(1)}, f32[1,144,256]{2,1,0:T(8,128)}, u32[]{:S(2)}) copy-start(f32[1,144,256]{2,1,0:T(8,128)} %get-tuple-element.50) | copy-start | bytes 442372

commit v3 on v1

--- a/solution.py
+++ b/solution.py
@@ -220,7 +220,7 @@
     leave(token_ref)
 
 
-def act_kernel(x_ref, stats_ref, gain_ref, bias_ref, turned_ref, white_ref, slope_ref, kept_ref, mean_ref):
+def act_kernel(x_ref, stats_ref, gain_ref, bias_ref, turned_ref, slope_ref, kept_ref, mean_ref):
     rows, width = x_ref.shape[0], x_ref.shape[1]
     same = same_group()
     eye = unit()
@@ -258,7 +258,6 @@
         gate = 0.5 * jnp.tanh(0.5 * pre) + 0.5
         act = pre * gate
         turned_ref[:, r * width : (r + 1) * width] = act.T.astype(BF16)
-        white_ref[r] = white
         slope_ref[r] = gate + act * (1.0 - gate)
 
 
@@ -281,29 +280,27 @@
     lax.fori_loop(0, 3, column, 0)
 
 
-def grad_kernel(x_ref, grad_ref, white_ref, slope_ref, kept_ref, mean_ref, gain_ref, back_ref, sums_ref):
+def grad_kernel(x_ref, grad_ref, slope_ref, kept_ref, mean_ref, gain_ref, back_ref, sums_ref):
     rows = x_ref.shape[0]
     same = same_group()
     gain = gain_ref[0:1]
-    mean = mean_ref[0:1]
-    white_high, white_low = spread_split(kept_ref[ITERS - 1, 0], same)
+    whitener = spread(kept_ref[ITERS - 1, 0], same)
+    weighted_high, weighted_low = split((whitener * gain).T)
 
     def row(r, carry):
-        gain_sum, bias_sum, products = carry
+        bias_sum, total = carry
         pre_grad = grad_ref[r] * slope_ref[r]
-        gain_sum = gain_sum + jnp.sum(pre_grad * white_ref[r], axis=0, keepdims=True)
         bias_sum = bias_sum + jnp.sum(pre_grad, axis=0, keepdims=True)
-        high, low = split(pre_grad * gain)
-        back_ref[r] = dot(high, white_high) + dot(low, white_high) + dot(high, white_low)
-        products = products + lax.dot_general(
-            x_ref[r], jnp.concatenate([high, low], axis=1), (((0,), (0,)), ((), ())), preferred_element_type=F32
-        )
-        return gain_sum, bias_sum, products
-
-    nothing = jnp.zeros((1, C), F32)
-    gain_sum, bias_sum, products = lax.fori_loop(0, rows, row, (nothing, nothing, jnp.zeros((C, 2 * C), F32)))
-    mean_column = jnp.broadcast_to(mean, (C, C)).T
-    full = products[:, :C] + products[:, C:] - mean_column * (gain * bias_sum)
+        high, low = split(pre_grad)
+        back_ref[r] = dot(high, weighted_high) + dot(low, weighted_high) + dot(high, weighted_low)
+        turn = lambda part: lax.dot_general(x_ref[r], part, (((0,), (0,)), ((), ())), preferred_element_type=F32)
+        return bias_sum, total + turn(high) + turn(low)
+
+    bias_sum, total = lax.fori_loop(0, rows, row, (jnp.zeros((1, C), F32), jnp.zeros((C, C), F32)))
+    mean_column = jnp.broadcast_to(mean_ref[0:1], (C, C)).T
+    full = total - mean_column * bias_sum
+    gain_sum = jnp.sum(full * whitener, axis=0, keepdims=True)
+    full = full * gain
     sums_ref[0:GS] = fold(full + full.T, same)
     line = lax.broadcasted_iota(jnp.int32, (8, C), 0)
     sums_ref[GS : GS + 8] = jnp.where(line == 0, gain_sum, jnp.where(line == 1, bias_sum, 0.0))
@@ -333,19 +330,16 @@
     leave(token_ref)
 
 
-def final_kernel(cell_count, x_ref, back_ref, sums_ref, wide_ref, lines_ref, after_ref, out_ref, vector_ref, high_ref, low_ref, constant_ref):
-    del after_ref
-
-    @pl.when(pl.program_id(0) == 0)
-    def _():
-        derivative(cell_count, sums_ref, wide_ref, lines_ref, vector_ref, high_ref, low_ref, constant_ref)
-
-    x = x_ref[0]
-    moved = dot(x, high_ref[...]) + dot(x, low_ref[...])
-    out_ref[0] = (moved + back_ref[0] - constant_ref[0:1]).astype(BF16)
-
-
-def derivative(cell_count, sums_ref, wide_ref, lines_ref, vector_ref, high_ref, low_ref, constant_ref):
+def final_kernel(cell_count, x_ref, back_ref, sums_ref, wide_ref, lines_ref, out_ref, gain_out_ref, bias_out_ref):
+    high, low, constant = derivative(cell_count, sums_ref, wide_ref, lines_ref)
+    for r in range(x_ref.shape[0]):
+        moved = dot(x_ref[r], high) + dot(x_ref[r], low)
+        out_ref[r] = (moved + back_ref[r] - constant).astype(BF16)
+    for line, ref in enumerate((gain_out_ref, bias_out_ref)):
+        ref[...] = sums_ref[GS + line] * (1.0 / math.sqrt(cell_count))
+
+
+def derivative(cell_count, sums_ref, wide_ref, lines_ref):
     same = same_group()
     eye = unit()
     whitener, normed = lines_ref[3, 0], lines_ref[3, 1]
@@ -364,16 +358,14 @@
     inner = jnp.sum(change * normed + 0.5 * paired * whitener, axis=0, keepdims=True)
     symmetric = (change - eye * group_total(inner, same)[0:1]) / trace
     high, low = spread_split(symmetric * (1.0 / cell_count), same)
-    high_ref[...] = high
-    low_ref[...] = low
     rounded = high.astype(F32) + low.astype(F32)
     bias_sum = sums_ref[GS + 1 : GS + 2]
     weighted = gain * bias_sum * (1.0 / cell_count)
     both = jnp.concatenate([mean, weighted], axis=1)
-    constant_ref[...] = jnp.dot(
+    constant = jnp.dot(
         both, jnp.concatenate([rounded, spread(whitener, same)], axis=0), precision=lax.Precision.HIGHEST
     )
-    vector_ref[...] = sums_ref[GS:] * (1.0 / math.sqrt(cell_count))
+    return high, low, constant[0:1]
 
 
 def stages(axes):
@@ -415,6 +407,7 @@
     gain = jnp.broadcast_to(norm_gain[None], (8, C))
     bias = jnp.broadcast_to(norm_bias[None], (8, C))
     shape = jax.ShapeDtypeStruct
+    held = pltpu.VMEM
     cells = (rows, width, C)
 
     odd = lax.axis_index("cols") % 2 == 1
@@ -434,33 +427,32 @@
         if number == count - 3:
             near_bands, weights, *token = run(
                 bands_kernel,
-                (shape((3,) + cells, BF16), shape((9, C, C), BF16), TOKEN),
+                (held((3,) + cells, BF16), held((9, C, C), BF16), TOKEN),
                 (up, left, right, conv_weight.reshape(9, GS, C)),
                 scratch=scratch,
                 after=(stats,),
             )
         if number == count - 2:
             near_grad, *token = run(
-                near_kernel, (shape(cells, F32), TOKEN), (near_bands, weights), after=(stats,)
+                near_kernel, (held(cells, F32), TOKEN), (near_bands, weights), after=(stats,)
             )
         if number == count - 1:
             far_bands, act_grad, *token = run(
                 far_kernel,
-                (shape((3, 2 * d, width, C), BF16), shape(cells, F32), TOKEN),
+                (held((3, 2 * d, width, C), BF16), held(cells, F32), TOKEN),
                 (even_line, odd_line, first, second, weights, near_grad),
                 scratch=scratch,
                 after=(stats,),
             )
         stats = run(merge_kernel, shape(stats.shape, F32), (stats, other), after=token)
 
-    turned, white, slope, kept, mean = run(
+    turned, slope, kept, mean = run(
         act_kernel,
         (
-            shape((C, rows * width), BF16),
-            shape(cells, F32),
-            shape(cells, F32),
-            shape((ITERS, 3, GS, C), F32),
-            shape((8, C), F32),
+            held((C, rows * width), BF16),
+            held(cells, F32),
+            held((ITERS, 3, GS, C), F32),
+            held((8, C), F32),
         ),
         (x, stats, gain, bias),
     )
@@ -474,8 +466,8 @@
 
     back, sums = run(
         grad_kernel,
-        (shape(cells, F32), shape((GS + 8, C), F32)),
-        (x, act_grad, white, slope, kept, mean, gain),
+        (held(cells, F32), shape((GS + 8, C), F32)),
+        (x, act_grad, slope, kept, mean, gain),
         after=(half,),
     )
     row_stages = [stage for stage in stage_pairs[1:] if stage[0] == "rows"]
@@ -487,33 +479,27 @@
         if number == count - 1:
             wide, lines, *token = run(
                 prepare_kernel,
-                (shape((2 * ITERS - 1, 2, C, C), BF16), shape((4, ITERS - 1, GS, C), F32), TOKEN),
+                (held((2 * ITERS - 1, 2, C, C), BF16), held((4, ITERS - 1, GS, C), F32), TOKEN),
                 (kept, mean, gain),
                 after=(sums,),
             )
         sums = add(sums, other, after=token)
         if 2 <= number < count:
-            last = number == count - 1
-            half = add(half, lax.ppermute(half, *tap_stages[number - 1]), after=() if last else (sums,))
-    block = pl.BlockSpec((1, width, C), lambda r: (r, 0, 0))
-    input_grad, vectors = pl.pallas_call(
+            half = add(half, lax.ppermute(half, *tap_stages[number - 1]), after=(sums,))
+    input_grad, gain_grad, bias_grad = run(
         functools.partial(final_kernel, cell_count),
-        grid=(rows,),
-        out_shape=(shape(cells, BF16), shape((8, C), F32)),
-        in_specs=[block, block] + [VMEM_SPEC] * 3 + [pl.BlockSpec(memory_space=pl.ANY)],
-        out_specs=[block, VMEM_SPEC],
-        scratch_shapes=[pltpu.VMEM((C, C), BF16), pltpu.VMEM((C, C), BF16), pltpu.VMEM((8, C), F32)],
-        compiler_params=pltpu.CompilerParams(vmem_limit_bytes=8 * 2**20),
-        cost_estimate=NO_COST,
-    )(x, back, sums, wide, lines, half)
+        (shape(cells, BF16), shape((C,), F32), shape((C,), F32)),
+        (x, back, sums, wide, lines),
+        after=(half,),
+    )
     half = half * (1.0 / math.sqrt(cell_count))
     other = lax.ppermute(half, tap_axis, tap_pairs)
     taps = jnp.where(later == 0, jnp.stack([half, other]), jnp.stack([other, half]))
     return (
         input_grad.reshape(features.shape),
         taps.reshape(3, 3, GS, C),
-        vectors[0],
-        vectors[1],
+        gain_grad,
+        bias_grad,
     )
 
 

time: 92.4 us -> 93.3 us (level)
  Pallas kernels: 30.4 us -> 27.5 us
  other arithmetic: 1.7 us -> 4.29 us
  waiting for transfers between devices: 20 us -> 21.3 us
    pallas_call x1 -> x0, Pallas kernels: 6.86 us -> none  [shards(): pl.pallas_call(functools.partial(final_kernel, cell_count), grid=(rows,),...]
    pallas_call x18 -> x20, Pallas kernels: 23.6 us -> 27.5 us  [run(): pl.pallas_call(kernel, out_shape=out_shapes, in_specs=[VMEM_SPEC] * count...]
    select_n x1, other arithmetic: 0.74 us -> 1.73 us  [shards(): jnp.where(later == 0, jnp.stack([half, other]), jnp.stack([other, half]))]
    ppermute x5, waiting for transfers between devices: 10.6 us -> 11.6 us  [shards(): other = lax.ppermute(sums, *stage)]
    unnamed x38 -> x42, local copies, waits for them, and re-layouts: 12.3 us -> 12.2 us
  transfers between devices with their start and end apart: 19 -> 19, of which waited for: 10 -> 10; matrix products, arithmetic and copies ran while one was open for 1% -> 0% of each run, Pallas kernels for 25% -> 21%
where the time goes in v3:
time: 93.3 us; the launch traced here: 92.7 us
  Pallas kernels  27.5 us (29%)
  starting transfers between devices  25.7 us (28%)
  waiting for transfers between devices  21.3 us (23%)
  local copies, waits for them, and re-layouts  12.8 us (14%)
  other arithmetic  4.29 us (5%)
  between operations  1.02 us (1%)
    pallas_call x20, Pallas kernels, run(): pl.pallas_call(kernel, out_shape=out_shapes, in_specs=[VMEM_SPEC] * count...  27.5 us
    unnamed x42, local copies, waits for them, and re-layouts  12.2 us
    ppermute x5, waiting for transfers between devices, shards(): other = lax.ppermute(sums, *stage)  11.6 us
    ppermute x5, starting transfers between devices, shards(): other = lax.ppermute(stats, axis, pairs)  6.83 us
    ppermute x3, starting transfers between devices, swap(): lax.ppermute(part, axis, pairs)  6.63 us
    ppermute x5, waiting for transfers between devices, shards(): other = lax.ppermute(stats, axis, pairs)  6.14 us
    ppermute x5, starting transfers between devices, shards(): other = lax.ppermute(sums, *stage)  5.74 us
    ppermute x3, starting transfers between devices, shards(): half = add(half, lax.ppermute(half, *tap_stages[number - 1]), after=(sums,))  5.04 us
  transfers between devices with their start and end apart: 19, of which 10 were waited for; matrix products, arithmetic and copies ran while one was open for 0% of the time, Pallas kernels for 21%

profile of v3, /device:TPU:0, one launch (start us, length us, event | category | flops | bytes accessed | tf_op | source)
XLA Modules:
  0.0 92.7 jit_solution(6103919256408859308)
XLA Ops:
  0.7 0.9 slice_select_fusion
  1.5 3.0 %collective-permute-start = (bf16[8,8,256]{2,1,0:T(8,128)(2,1)S(1)}, bf16[8,8,256]{2,1,0:T(8,128)(2,1)S(1)}, u32[]{:S(2)}, u32[]{:S(2)}) collective-permute-start(bf16[8,8,256]{2,1,0:T(8,128)(2,1)S(1)} %slice_select_fusion), channel_id=1, source_target_pairs={{0,4},{4,0},{1,5},{5,1},{2,6},{6,2},{3,7},{7,3},{8,12},{12,8},{9,1... | collective-permute-start | bytes 98312 | tf_op jit(solution)/shard_map/ppermute | solution.py:392
  4.5 1.9 %collective-permute-done = bf16[8,8,256]{2,1,0:T(8,128)(2,1)S(1)} collective-permute-done((bf16[8,8,256]{2,1,0:T(8,128)(2,1)S(1)}, bf16[8,8,256]{2,1,0:T(8,128)(2,1)S(1)}, u32[]{:S(2)}, u32[]{:S(2)}) %collective-permute-start) | collective-permute-done | bytes 32800 | tf_op jit(solution)/shard_map/ppermute | solution.py:392
  6.4 1.2 %copy-done.3 = bf16[1,8,256,256]{3,2,1,0:T(8,128)(2,1)S(1)} copy-done((bf16[1,8,256,256]{3,2,1,0:T(8,128)(2,1)S(1)}, bf16[1,8,256,256]{3,2,1,0:T(8,128)(2,1)}, u32[]{:S(2)}) %copy-start.3) | copy-done | bytes 1048600
  7.6 1.5 %shard_map.84 = (bf16[6,272,256]{2,1,0:T(8,128)(2,1)}, bf16[6,272,256]{2,1,0:T(8,128)(2,1)}, f32[8,128]{1,0:T(8,128)S(1)}) custom-call(bf16[8,256,256]{2,1,0:T(8,128)(2,1)S(1)} %bitcast.18, bf16[8,8,256]{2,1,0:T(8,128)(2,1)S(1)} %get-tuple-element.53.refs_1_, bf16[8,8,256]{2,1,0:T(8,128)(2,1)S(1)} %get-tuple-element.52.refs_2_, ...), custom_call_target="tpu_custom_call" | custom-call | tf_op jit(solution)/shard_map/pallas_call | solution.py:31
  9.2 2.1 %collective-permute-start.1 = (bf16[6,272,256]{2,1,0:T(8,128)(2,1)}, bf16[6,272,256]{2,1,0:T(8,128)(2,1)S(1)}, u32[]{:S(2)}, u32[]{:S(2)}) collective-permute-start(bf16[6,272,256]{2,1,0:T(8,128)(2,1)} %get-tuple-element.27), channel_id=1, source_target_pairs={{0,8},{16,24},{8,0},{24,16},{1,9},{17,25},{9,1},{25,17},{2,10},{18... | collective-permute-start | bytes 2506760 | tf_op jit(solution)/shard_map/ppermute | solution.py:392
  11.3 1.6 %collective-permute-start.2 = (bf16[6,272,256]{2,1,0:T(8,128)(2,1)}, bf16[6,272,256]{2,1,0:T(8,128)(2,1)}, u32[]{:S(2)}, u32[]{:S(2)}) collective-permute-start(bf16[6,272,256]{2,1,0:T(8,128)(2,1)} %get-tuple-element.28), channel_id=1, source_target_pairs={{8,16},{16,8},{9,17},{17,9},{10,18},{18,10},{11,19},{19,11},{12,20... | collective-permute-start | bytes 2506760 | tf_op jit(solution)/shard_map/ppermute | solution.py:392
  12.8 3.0 %shard_map.85.refs_0_ = f32[72,256]{1,0:T(8,128)S(1)} custom-call(bf16[8,256,256]{2,1,0:T(8,128)(2,1)S(1)} %bitcast.13, f32[8,128]{1,0:T(8,128)S(1)} %get-tuple-element.29.refs_1_), custom_call_target="tpu_custom_call" | custom-call | tf_op jit(solution)/shard_map/pallas_call | solution.py:31
  15.9 1.3 %collective-permute-done.3.refs_1_ = f32[72,256]{1,0:T(8,128)S(1)} collective-permute-done((f32[72,256]{1,0:T(8,128)S(1)}, f32[72,256]{1,0:T(8,128)S(1)}, u32[]{:S(2)}, u32[]{:S(2)}) %collective-permute-start.3) | collective-permute-done | bytes 73760 | tf_op jit(solution)/shard_map/ppermute | solution.py:425
  17.2 1.6 %collective-permute-start.4 = (f32[72,256]{1,0:T(8,128)S(1)}, f32[72,256]{1,0:T(8,128)S(1)}, u32[]{:S(2)}, u32[]{:S(2)}) collective-permute-start(f32[72,256]{1,0:T(8,128)S(1)} %shard_map.86.refs_0_), channel_id=1, source_target_pairs={{0,2},{1,3},{2,0},{3,1},{4,6},{5,7},{6,4},{7,5},{8,10},{9,11},{10,... | collective-permute-start | bytes 221192 | tf_op jit(solution)/shard_map/ppermute | solution.py:425
  18.8 2.9 %collective-permute-done.4.refs_1_ = f32[72,256]{1,0:T(8,128)S(1)} collective-permute-done((f32[72,256]{1,0:T(8,128)S(1)}, f32[72,256]{1,0:T(8,128)S(1)}, u32[]{:S(2)}, u32[]{:S(2)}) %collective-permute-start.4) | collective-permute-done | bytes 73760 | tf_op jit(solution)/shard_map/ppermute | solution.py:425
  21.6 1.6 %collective-permute-start.5 = (f32[72,256]{1,0:T(8,128)S(1)}, f32[72,256]{1,0:T(8,128)S(1)}, u32[]{:S(2)}, u32[]{:S(2)}) collective-permute-start(f32[72,256]{1,0:T(8,128)S(1)} %shard_map.87.refs_4_.refs_0_), channel_id=1, source_target_pairs={{0,4},{4,0},{1,5},{5,1},{2,6},{6,2},{3,7},{7,3},{8,12},{12,8},{9,1... | collective-permute-start | bytes 221192 | tf_op jit(solution)/shard_map/ppermute | solution.py:425
  23.2 0.8 shard_map.88
  24.0 2.0 %collective-permute-done.5.refs_1_ = f32[72,256]{1,0:T(8,128)S(1)} collective-permute-done((f32[72,256]{1,0:T(8,128)S(1)}, f32[72,256]{1,0:T(8,128)S(1)}, u32[]{:S(2)}, u32[]{:S(2)}) %collective-permute-start.5) | collective-permute-done | bytes 73760 | tf_op jit(solution)/shard_map/ppermute | solution.py:425
  26.1 3.5 %collective-permute-start.6 = (f32[72,256]{1,0:T(8,128)S(1)}, f32[72,256]{1,0:T(8,128)S(1)}, u32[]{:S(2)}, u32[]{:S(2)}) collective-permute-start(f32[72,256]{1,0:T(8,128)S(1)} %shard_map.89.refs_2_.refs_0_), channel_id=1, source_target_pairs={{0,8},{8,0},{16,24},{24,16},{1,9},{9,1},{17,25},{25,17},{2,10},{10... | collective-permute-start | bytes 221192 | tf_op jit(solution)/shard_map/ppermute | solution.py:425
  29.6 2.6 %shard_map.90 = (f32[8,256,256]{2,1,0:T(8,128)S(1)}, f32[8,128]{1,0:T(8,128)S(1)}) custom-call(bf16[3,8,256,256]{3,2,1,0:T(8,128)(2,1)S(1)} %get-tuple-element.31.refs_0_.refs_1_, bf16[9,256,256]{2,1,0:T(8,128)(2,1)S(1)} %get-tuple-element.30.refs_1_.refs_4_, f32[72,256]{1,0:T(8,128)S(1)} %shard_map.89.refs_2_.refs_0_), custom_call_target="tpu_custom_call" | custom-call | tf_op jit(solution)/shard_map/pallas_call | solution.py:31
  32.2 1.3 %copy-done.5 = f32[8,256,256]{2,1,0:T(8,128)} copy-done((f32[8,256,256]{2,1,0:T(8,128)}, f32[8,256,256]{2,1,0:T(8,128)S(1)}, u32[]{:S(2)}) %copy-start.5) | copy-done | bytes 2097176
  33.7 1.6 %copy-done.6 = f32[8,256,256]{2,1,0:T(8,128)S(1)} copy-done((f32[8,256,256]{2,1,0:T(8,128)S(1)}, f32[8,256,256]{2,1,0:T(8,128)}, u32[]{:S(2)}) %copy-start.6) | copy-done | bytes 2097176
  35.3 4.9 %shard_map.92 = (bf16[3,12,256,256]{3,2,1,0:T(8,128)(2,1)S(1)}, f32[8,256,256]{2,1,0:T(8,128)S(1)}, f32[8,128]{1,0:T(8,128)S(1)}) custom-call(f32[8,256]{1,0:T(8,128)S(1)} %sub.10.refs_0_, f32[8,256]{1,0:T(8,128)S(1)} %broadcast_in_dim.8.refs_3_.refs_1_, bf16[6,272,256]{2,1,0:T(8,128)(2,1)S(1)} %collective-permute-done.1.refs_2_, ...), custom_call_target="tpu_custom_call" | custom-call | tf_op jit(solution)/shard_map/pallas_call | solution.py:31
  40.3 3.3 %shard_map.94 = (bf16[256,2048]{1,0:T(8,128)(2,1)S(1)}, f32[8,256,256]{2,1,0:T(8,128)S(1)}, f32[5,3,32,256]{3,2,1,0:T(8,128)S(1)}, f32[8,256]{1,0:T(8,128)S(1)}) custom-call(bf16[8,256,256]{2,1,0:T(8,128)(2,1)S(1)} %bitcast.14, f32[72,256]{1,0:T(8,128)S(1)} %shard_map.93.refs_1_, f32[8,256]{1,0:T(8,128)S(1)} %broadcast_in_dim.20.refs_2_.refs_5_, ...), custom_call_target="tpu_custom_call" | custom-call | tf_op jit(solution)/shard_map/pallas_call | solution.py:31
  43.6 3.0 %shard_map.95 = f32[9,32,256]{2,1,0:T(8,128)S(1)} custom-call(bf16[256,2048]{1,0:T(8,128)(2,1)S(1)} %get-tuple-element.40.refs_0_, bf16[3,8,256,256]{3,2,1,0:T(8,128)(2,1)S(1)} %copy-done.2, bf16[3,12,256,256]{3,2,1,0:T(8,128)(2,1)S(1)} %get-tuple-element.41.refs_2_), custom_call_target="tpu_custom_call" | custom-call | tf_op jit(solution)/shard_map/pallas_call | solution.py:31
  46.6 0.7 dynamic-slice_bitcast_fusion
  47.3 1.7 %collective-permute-done.8 = f32[144,256]{1,0:T(8,128)} collective-permute-done((f32[144,256]{1,0:T(8,128)}, f32[144,256]{1,0:T(8,128)}, u32[]{:S(2)}, u32[]{:S(2)}) %collective-permute-start.8) | collective-permute-done | bytes 147488 | tf_op jit(solution)/shard_map/ppermute | solution.py:465
  49.0 0.9 %bitcast_add_fusion.refs_6_.refs_0_ = f32[144,256]{1,0:T(8,128)S(1)} fusion(f32[144,256]{1,0:T(8,128)} %collective-permute-done.8, f32[2,144,256]{2,1,0:T(8,128)S(1)} %bitcast.21, s32[]{:T(128)S(6)} %select_n.57), kind=kLoop, calls=%fused_computation.1 | loop fusion | flops 36864 | bytes 442372 | tf_op jit(solution)/shard_map/add | solution.py:382
  49.9 1.5 %collective-permute-start.14 = (f32[144,256]{1,0:T(8,128)S(1)}, f32[144,256]{1,0:T(8,128)S(1)}, u32[]{:S(2)}, u32[]{:S(2)}) collective-permute-start(f32[144,256]{1,0:T(8,128)S(1)} %bitcast_add_fusion.refs_6_.refs_0_), channel_id=1, source_target_pairs={{0,8},{8,0},{16,24},{24,16},{1,9},{9,1},{17,25},{25,17},{2,10},{10... | collective-permute-start | bytes 442376 | tf_op jit(solution)/shard_map/ppermute | solution.py:475
  51.4 1.6 %copy-done.8 = f32[8,256,256]{2,1,0:T(8,128)S(1)} copy-done((f32[8,256,256]{2,1,0:T(8,128)S(1)}, f32[8,256,256]{2,1,0:T(8,128)}, u32[]{:S(2)}) %copy-start.8) | copy-done | bytes 2097176
  53.0 1.0 %copy-done.12 = f32[5,3,32,256]{3,2,1,0:T(8,128)S(1)} copy-done((f32[5,3,32,256]{3,2,1,0:T(8,128)S(1)}, f32[5,3,32,256]{3,2,1,0:T(8,128)}, u32[]{:S(2)}) %copy-start.12) | copy-done | bytes 491544
  54.0 3.3 %shard_map.96 = (f32[8,256,256]{2,1,0:T(8,128)S(1)}, f32[40,256]{1,0:T(8,128)S(1)}) custom-call(bf16[8,256,256]{2,1,0:T(8,128)(2,1)S(1)} %bitcast.15, f32[8,256,256]{2,1,0:T(8,128)S(1)} %copy-done.8, f32[8,256,256]{2,1,0:T(8,128)S(1)} %get-tuple-element.37.refs_2_, f32[5,3,32,256]{3,2,1,0:T(8,128)S(1)} %copy-done.12, ...), custom_call_target="tpu_custom_call" | custom-call | tf_op jit(solution)/shard_map/pallas_call | solution.py:31
  57.4 1.3 %copy-done.9 = f32[8,256,256]{2,1,0:T(8,128)} copy-done((f32[8,256,256]{2,1,0:T(8,128)}, f32[8,256,256]{2,1,0:T(8,128)S(1)}, u32[]{:S(2)}) %copy-start.9) | copy-done | bytes 2097176
  58.7 1.9 %collective-permute-start.15 = (f32[144,256]{1,0:T(8,128)S(1)}, f32[144,256]{1,0:T(8,128)S(1)}, u32[]{:S(2)}, u32[]{:S(2)}) collective-permute-start(f32[144,256]{1,0:T(8,128)S(1)} %shard_map.99.refs_0_), channel_id=1, source_target_pairs={{0,16},{8,24},{16,0},{24,8},{1,17},{9,25},{17,1},{25,9},{2,18},{10... | collective-permute-start | bytes 442376 | tf_op jit(solution)/shard_map/ppermute | solution.py:488
  60.6 1.2 %collective-permute-done.9 = f32[40,256]{1,0:T(8,128)S(1)} collective-permute-done((f32[40,256]{1,0:T(8,128)S(1)}, f32[40,256]{1,0:T(8,128)S(1)}, u32[]{:S(2)}, u32[]{:S(2)}) %collective-permute-start.9) | collective-permute-done | bytes 40992 | tf_op jit(solution)/shard_map/ppermute | solution.py:477
  61.9 1.5 %collective-permute-start.10 = (f32[40,256]{1,0:T(8,128)S(1)}, f32[40,256]{1,0:T(8,128)S(1)}, u32[]{:S(2)}, u32[]{:S(2)}) collective-permute-start(f32[40,256]{1,0:T(8,128)S(1)} %add.39), channel_id=1, source_target_pairs={{0,2},{1,3},{2,0},{3,1},{4,6},{5,7},{6,4},{7,5},{8,10},{9,11},{10,... | collective-permute-start | bytes 122888 | tf_op jit(solution)/shard_map/ppermute | solution.py:477
  63.3 2.5 %collective-permute-done.10 = f32[40,256]{1,0:T(8,128)S(1)} collective-permute-done((f32[40,256]{1,0:T(8,128)S(1)}, f32[40,256]{1,0:T(8,128)S(1)}, u32[]{:S(2)}, u32[]{:S(2)}) %collective-permute-start.10) | collective-permute-done | bytes 40992 | tf_op jit(solution)/shard_map/ppermute | solution.py:477
  65.9 1.5 %collective-permute-start.11 = (f32[40,256]{1,0:T(8,128)S(1)}, f32[40,256]{1,0:T(8,128)S(1)}, u32[]{:S(2)}, u32[]{:S(2)}) collective-permute-start(f32[40,256]{1,0:T(8,128)S(1)} %add.40), channel_id=1, source_target_pairs={{0,4},{4,0},{1,5},{5,1},{2,6},{6,2},{3,7},{7,3},{8,12},{12,8},{9,1... | collective-permute-start | bytes 122888 | tf_op jit(solution)/shard_map/ppermute | solution.py:477
  67.4 2.5 %collective-permute-done.11 = f32[40,256]{1,0:T(8,128)S(1)} collective-permute-done((f32[40,256]{1,0:T(8,128)S(1)}, f32[40,256]{1,0:T(8,128)S(1)}, u32[]{:S(2)}, u32[]{:S(2)}) %collective-permute-start.11) | collective-permute-done | bytes 40992 | tf_op jit(solution)/shard_map/ppermute | solution.py:477
  69.9 1.6 %collective-permute-start.16 = (f32[144,256]{1,0:T(8,128)S(1)}, f32[144,256]{1,0:T(8,128)S(1)}, u32[]{:S(2)}, u32[]{:S(2)}) collective-permute-start(f32[144,256]{1,0:T(8,128)S(1)} %shard_map.100.refs_0_), channel_id=1, source_target_pairs={{0,2},{1,3},{2,0},{3,1},{4,6},{5,7},{6,4},{7,5},{8,10},{9,11},{10,... | collective-permute-start | bytes 442376 | tf_op jit(solution)/shard_map/ppermute | solution.py:488
  71.5 1.6 %collective-permute-start.12 = (f32[40,256]{1,0:T(8,128)S(1)}, f32[40,256]{1,0:T(8,128)S(1)}, u32[]{:S(2)}, u32[]{:S(2)}) collective-permute-start(f32[40,256]{1,0:T(8,128)S(1)} %add.41.refs_2_), channel_id=1, source_target_pairs={{0,8},{8,0},{16,24},{24,16},{1,9},{9,1},{17,25},{25,17},{2,10},{10... | collective-permute-start | bytes 122888 | tf_op jit(solution)/shard_map/ppermute | solution.py:477
  73.1 2.4 %collective-permute-done.12 = f32[40,256]{1,0:T(8,128)S(1)} collective-permute-done((f32[40,256]{1,0:T(8,128)S(1)}, f32[40,256]{1,0:T(8,128)S(1)}, u32[]{:S(2)}, u32[]{:S(2)}) %collective-permute-start.12) | collective-permute-done | bytes 40992 | tf_op jit(solution)/shard_map/ppermute | solution.py:477
  75.5 1.6 %collective-permute-start.17 = (f32[144,256]{1,0:T(8,128)S(1)}, f32[144,256]{1,0:T(8,128)S(1)}, u32[]{:S(2)}, u32[]{:S(2)}) collective-permute-start(f32[144,256]{1,0:T(8,128)S(1)} %shard_map.101.refs_0_), channel_id=1, source_target_pairs={{0,4},{4,0},{1,5},{5,1},{2,6},{6,2},{3,7},{7,3},{8,12},{12,8},{9,1... | collective-permute-start | bytes 442376 | tf_op jit(solution)/shard_map/ppermute | solution.py:488
  77.1 1.1 %collective-permute-start.13 = (f32[40,256]{1,0:T(8,128)S(1)}, f32[40,256]{1,0:T(8,128)S(1)}, u32[]{:S(2)}, u32[]{:S(2)}) collective-permute-start(f32[40,256]{1,0:T(8,128)S(1)} %add.42.refs_3_.refs_0_.refs_2_), channel_id=1, source_target_pairs={{0,16},{8,24},{16,0},{24,8},{1,17},{9,25},{17,1},{25,9},{2,18},{10... | collective-permute-start | bytes 122888 | tf_op jit(solution)/shard_map/ppermute | solution.py:477
  78.2 0.8 shard_map.97
  79.0 3.0 %collective-permute-done.13.refs_1_ = f32[40,256]{1,0:T(8,128)S(1)} collective-permute-done((f32[40,256]{1,0:T(8,128)S(1)}, f32[40,256]{1,0:T(8,128)S(1)}, u32[]{:S(2)}, u32[]{:S(2)}) %collective-permute-start.13) | collective-permute-done | bytes 40992 | tf_op jit(solution)/shard_map/ppermute | solution.py:477
  82.7 0.7 fusion
  83.4 1.6 %copy-done.10 = f32[8,256,256]{2,1,0:T(8,128)S(1)} copy-done((f32[8,256,256]{2,1,0:T(8,128)S(1)}, f32[8,256,256]{2,1,0:T(8,128)}, u32[]{:S(2)}) %copy-start.10) | copy-done | bytes 2097176
  85.0 1.0 %copy-done.14 = f32[4,4,32,256]{3,2,1,0:T(8,128)S(1)} copy-done((f32[4,4,32,256]{3,2,1,0:T(8,128)S(1)}, f32[4,4,32,256]{3,2,1,0:T(8,128)}, u32[]{:S(2)}) %copy-start.14) | copy-done | bytes 524312
  86.0 0.8 copy-done.16
  86.8 4.2 %shard_map.103 = (bf16[8,256,256]{2,1,0:T(8,128)(2,1)}, f32[256]{0:T(256)}, f32[256]{0:T(256)}) custom-call(bf16[8,256,256]{2,1,0:T(8,128)(2,1)S(1)} %bitcast.16, f32[8,256,256]{2,1,0:T(8,128)S(1)} %copy-done.10, f32[40,256]{1,0:T(8,128)S(1)} %copy-done.16, bf16[9,2,256,256]{3,2,1,0:T(8,128)(2,1)S(1)} %get-tuple-element.45.refs_3_, ...), custom_call_target="tpu_custom_call" | custom-call | tf_op jit(solution)/shard_map/pallas_call | solution.py:31
  91.0 1.7 %maximum_select_fusion = f32[2,144,256]{2,1,0:T(8,128)} fusion(f32[1,144,256]{2,1,0:T(8,128)} %bitcast.8, f32[1,144,256]{2,1,0:T(8,128)S(1)} %copy-done.18, pred[]{:T(512)S(6)} %eq.15), kind=kLoop, calls=%fused_computation | loop fusion | flops 221184 | bytes 589825 | tf_op jit(solution)/shard_map/jit(_where)/select_n | solution.py:497
  (66 shorter events, 1.1 us)
Async XLA Ops:
  0.6 12.2 %copy-start = (bf16[1,8,256,256]{3,2,1,0:T(8,128)(2,1)S(1)}, bf16[1,8,256,256]{3,2,1,0:T(8,128)(2,1)}, u32[]{:S(2)}) copy-start(bf16[1,8,256,256]{3,2,1,0:T(8,128)(2,1)} %param.5) | copy-start | bytes 3145732
  1.5 4.9 %collective-permute-start = (bf16[8,8,256]{2,1,0:T(8,128)(2,1)S(1)}, bf16[8,8,256]{2,1,0:T(8,128)(2,1)S(1)}, u32[]{:S(2)}, u32[]{:S(2)}) collective-permute-start(bf16[8,8,256]{2,1,0:T(8,128)(2,1)S(1)} %slice_select_fusion), channel_id=1, source_target_pairs={{0,4},{4,0},{1,5},{5,1},{2,6},{6,2},{3,7},{7,3},{8,12},{12,8},{9,1... | collective-permute-start | bytes 98312 | tf_op jit(solution)/shard_map/ppermute | solution.py:392
  6.4 1.2 %copy-start.3 = (bf16[1,8,256,256]{3,2,1,0:T(8,128)(2,1)S(1)}, bf16[1,8,256,256]{3,2,1,0:T(8,128)(2,1)}, u32[]{:S(2)}) copy-start(bf16[1,8,256,256]{3,2,1,0:T(8,128)(2,1)} %param.6) | copy-start | bytes 3145732
  7.6 15.6 %copy-start.4 = (bf16[1,8,256,256]{3,2,1,0:T(8,128)(2,1)S(1)}, bf16[1,8,256,256]{3,2,1,0:T(8,128)(2,1)}, u32[]{:S(2)}) copy-start(bf16[1,8,256,256]{3,2,1,0:T(8,128)(2,1)} %param.6) | copy-start | bytes 3145732
  7.6 15.6 %copy-start.17 = (bf16[3,3,32,256]{3,2,1,0:T(8,128)(2,1)S(1)}, bf16[3,3,32,256]{3,2,1,0:T(8,128)(2,1)}, u32[]{:S(2)}) copy-start(bf16[3,3,32,256]{3,2,1,0:T(8,128)(2,1)} %param.7) | copy-start | bytes 442372
  9.2 24.5 %collective-permute-start.1 = (bf16[6,272,256]{2,1,0:T(8,128)(2,1)}, bf16[6,272,256]{2,1,0:T(8,128)(2,1)S(1)}, u32[]{:S(2)}, u32[]{:S(2)}) collective-permute-start(bf16[6,272,256]{2,1,0:T(8,128)(2,1)} %get-tuple-element.27), channel_id=1, source_target_pairs={{0,8},{16,24},{8,0},{24,16},{1,9},{17,25},{9,1},{25,17},{2,10},{18... | collective-permute-start | bytes 2506760 | tf_op jit(solution)/shard_map/ppermute | solution.py:392
  11.3 22.5 %collective-permute-start.2 = (bf16[6,272,256]{2,1,0:T(8,128)(2,1)}, bf16[6,272,256]{2,1,0:T(8,128)(2,1)}, u32[]{:S(2)}, u32[]{:S(2)}) collective-permute-start(bf16[6,272,256]{2,1,0:T(8,128)(2,1)} %get-tuple-element.28), channel_id=1, source_target_pairs={{8,16},{16,8},{9,17},{17,9},{10,18},{18,10},{11,19},{19,11},{12,20... | collective-permute-start | bytes 2506760 | tf_op jit(solution)/shard_map/ppermute | solution.py:392
  15.8 1.3 %collective-permute-start.3 = (f32[72,256]{1,0:T(8,128)S(1)}, f32[72,256]{1,0:T(8,128)S(1)}, u32[]{:S(2)}, u32[]{:S(2)}) collective-permute-start(f32[72,256]{1,0:T(8,128)S(1)} %shard_map.85.refs_0_), channel_id=1, source_target_pairs={{0,1},{1,0},{2,3},{3,2},{4,5},{5,4},{6,7},{7,6},{8,9},{9,8},{10,11... | collective-permute-start | bytes 221192 | tf_op jit(solution)/shard_map/ppermute | solution.py:425
  17.2 4.4 %collective-permute-start.4 = (f32[72,256]{1,0:T(8,128)S(1)}, f32[72,256]{1,0:T(8,128)S(1)}, u32[]{:S(2)}, u32[]{:S(2)}) collective-permute-start(f32[72,256]{1,0:T(8,128)S(1)} %shard_map.86.refs_0_), channel_id=1, source_target_pairs={{0,2},{1,3},{2,0},{3,1},{4,6},{5,7},{6,4},{7,5},{8,10},{9,11},{10,... | collective-permute-start | bytes 221192 | tf_op jit(solution)/shard_map/ppermute | solution.py:425
  21.6 4.4 %collective-permute-start.5 = (f32[72,256]{1,0:T(8,128)S(1)}, f32[72,256]{1,0:T(8,128)S(1)}, u32[]{:S(2)}, u32[]{:S(2)}) collective-permute-start(f32[72,256]{1,0:T(8,128)S(1)} %shard_map.87.refs_4_.refs_0_), channel_id=1, source_target_pairs={{0,4},{4,0},{1,5},{5,1},{2,6},{6,2},{3,7},{7,3},{8,12},{12,8},{9,1... | collective-permute-start | bytes 221192 | tf_op jit(solution)/shard_map/ppermute | solution.py:425
  24.0 8.2 %copy-start.1 = (bf16[3,8,256,256]{3,2,1,0:T(8,128)(2,1)}, bf16[3,8,256,256]{3,2,1,0:T(8,128)(2,1)S(1)}, u32[]{:S(2)}) copy-start(bf16[3,8,256,256]{3,2,1,0:T(8,128)(2,1)S(1)} %get-tuple-element.31.refs_0_.refs_1_) | copy-start | bytes 9437188
  26.1 7.5 %collective-permute-start.6 = (f32[72,256]{1,0:T(8,128)S(1)}, f32[72,256]{1,0:T(8,128)S(1)}, u32[]{:S(2)}, u32[]{:S(2)}) collective-permute-start(f32[72,256]{1,0:T(8,128)S(1)} %shard_map.89.refs_2_.refs_0_), channel_id=1, source_target_pairs={{0,8},{8,0},{16,24},{24,16},{1,9},{9,1},{17,25},{25,17},{2,10},{10... | collective-permute-start | bytes 221192 | tf_op jit(solution)/shard_map/ppermute | solution.py:425
  32.2 1.4 %copy-start.5 = (f32[8,256,256]{2,1,0:T(8,128)}, f32[8,256,256]{2,1,0:T(8,128)S(1)}, u32[]{:S(2)}) copy-start(f32[8,256,256]{2,1,0:T(8,128)S(1)} %get-tuple-element.33.refs_5_) | copy-start | bytes 6291460
  33.6 6.6 %collective-permute-start.7 = (f32[72,256]{1,0:T(8,128)S(1)}, f32[72,256]{1,0:T(8,128)S(1)}, u32[]{:S(2)}, u32[]{:S(2)}) collective-permute-start(f32[72,256]{1,0:T(8,128)S(1)} %shard_map.91.refs_6_.refs_0_), channel_id=1, source_target_pairs={{0,16},{8,24},{16,0},{24,8},{1,17},{9,25},{17,1},{25,9},{2,18},{10... | collective-permute-start | bytes 221192 | tf_op jit(solution)/shard_map/ppermute | solution.py:425
  33.7 1.6 %copy-start.6 = (f32[8,256,256]{2,1,0:T(8,128)S(1)}, f32[8,256,256]{2,1,0:T(8,128)}, u32[]{:S(2)}) copy-start(f32[8,256,256]{2,1,0:T(8,128)} %copy-done.5) | copy-start | bytes 6291460
  35.3 4.9 %copy-start.19 = (f32[256]{0:T(256)S(1)}, f32[256]{0:T(256)}, u32[]{:S(2)}) copy-start(f32[256]{0:T(256)} %param.8) | copy-start | bytes 3076
  35.3 4.9 %copy-start.20 = (f32[256]{0:T(256)S(1)}, f32[256]{0:T(256)}, u32[]{:S(2)}) copy-start(f32[256]{0:T(256)} %param.9) | copy-start | bytes 3076
  35.3 8.2 %copy-start.2 = (bf16[3,8,256,256]{3,2,1,0:T(8,128)(2,1)S(1)}, bf16[3,8,256,256]{3,2,1,0:T(8,128)(2,1)}, u32[]{:S(2)}) copy-start(bf16[3,8,256,256]{3,2,1,0:T(8,128)(2,1)} %copy-done.1) | copy-start | bytes 9437188
  40.2 6.4 %copy-start.7 = (f32[8,256,256]{2,1,0:T(8,128)}, f32[8,256,256]{2,1,0:T(8,128)S(1)}, u32[]{:S(2)}) copy-start(f32[8,256,256]{2,1,0:T(8,128)S(1)} %get-tuple-element.35.refs_1_) | copy-start | bytes 6291460
  43.5 3.1 %copy-start.11 = (f32[5,3,32,256]{3,2,1,0:T(8,128)}, f32[5,3,32,256]{3,2,1,0:T(8,128)S(1)}, u32[]{:S(2)}) copy-start(f32[5,3,32,256]{3,2,1,0:T(8,128)S(1)} %get-tuple-element.38.refs_3_.refs_0_) | copy-start | bytes 1474564
  47.3 1.7 %collective-permute-start.8 = (f32[144,256]{1,0:T(8,128)}, f32[144,256]{1,0:T(8,128)}, u32[]{:S(2)}, u32[]{:S(2)}) collective-permute-start(f32[144,256]{1,0:T(8,128)} %dynamic-slice_bitcast_fusion), channel_id=1, source_target_pairs={{0,1},{1,0},{2,3},{3,2},{4,5},{5,4},{6,7},{7,6},{8,9},{9,8},{10,11... | collective-permute-start | bytes 442376 | tf_op jit(solution)/shard_map/ppermute | solution.py:465
  49.9 8.8 %collective-permute-start.14 = (f32[144,256]{1,0:T(8,128)S(1)}, f32[144,256]{1,0:T(8,128)S(1)}, u32[]{:S(2)}, u32[]{:S(2)}) collective-permute-start(f32[144,256]{1,0:T(8,128)S(1)} %bitcast_add_fusion.refs_6_.refs_0_), channel_id=1, source_target_pairs={{0,8},{8,0},{16,24},{24,16},{1,9},{9,1},{17,25},{25,17},{2,10},{10... | collective-permute-start | bytes 442376 | tf_op jit(solution)/shard_map/ppermute | solution.py:475
  51.4 1.6 %copy-start.8 = (f32[8,256,256]{2,1,0:T(8,128)S(1)}, f32[8,256,256]{2,1,0:T(8,128)}, u32[]{:S(2)}) copy-start(f32[8,256,256]{2,1,0:T(8,128)} %copy-done.7) | copy-start | bytes 6291460
  53.0 1.0 %copy-start.12 = (f32[5,3,32,256]{3,2,1,0:T(8,128)S(1)}, f32[5,3,32,256]{3,2,1,0:T(8,128)}, u32[]{:S(2)}) copy-start(f32[5,3,32,256]{3,2,1,0:T(8,128)} %copy-done.11) | copy-start | bytes 1474564
  57.4 1.3 %copy-start.9 = (f32[8,256,256]{2,1,0:T(8,128)}, f32[8,256,256]{2,1,0:T(8,128)S(1)}, u32[]{:S(2)}) copy-start(f32[8,256,256]{2,1,0:T(8,128)S(1)} %get-tuple-element.42.refs_1_) | copy-start | bytes 6291460
  58.7 11.1 %collective-permute-start.15 = (f32[144,256]{1,0:T(8,128)S(1)}, f32[144,256]{1,0:T(8,128)S(1)}, u32[]{:S(2)}, u32[]{:S(2)}) collective-permute-start(f32[144,256]{1,0:T(8,128)S(1)} %shard_map.99.refs_0_), channel_id=1, source_target_pairs={{0,16},{8,24},{16,0},{24,8},{1,17},{9,25},{17,1},{25,9},{2,18},{10... | collective-permute-start | bytes 442376 | tf_op jit(solution)/shard_map/ppermute | solution.py:488
  60.6 1.2 %collective-permute-start.9 = (f32[40,256]{1,0:T(8,128)S(1)}, f32[40,256]{1,0:T(8,128)S(1)}, u32[]{:S(2)}, u32[]{:S(2)}) collective-permute-start(f32[40,256]{1,0:T(8,128)S(1)} %get-tuple-element.43.refs_2_), channel_id=1, source_target_pairs={{0,1},{1,0},{2,3},{3,2},{4,5},{5,4},{6,7},{7,6},{8,9},{9,8},{10,11... | collective-permute-start | bytes 122888 | tf_op jit(solution)/shard_map/ppermute | solution.py:477
  61.9 4.0 %collective-permute-start.10 = (f32[40,256]{1,0:T(8,128)S(1)}, f32[40,256]{1,0:T(8,128)S(1)}, u32[]{:S(2)}, u32[]{:S(2)}) collective-permute-start(f32[40,256]{1,0:T(8,128)S(1)} %add.39), channel_id=1, source_target_pairs={{0,2},{1,3},{2,0},{3,1},{4,6},{5,7},{6,4},{7,5},{8,10},{9,11},{10,... | collective-permute-start | bytes 122888 | tf_op jit(solution)/shard_map/ppermute | solution.py:477
  65.9 4.0 %collective-permute-start.11 = (f32[40,256]{1,0:T(8,128)S(1)}, f32[40,256]{1,0:T(8,128)S(1)}, u32[]{:S(2)}, u32[]{:S(2)}) collective-permute-start(f32[40,256]{1,0:T(8,128)S(1)} %add.40), channel_id=1, source_target_pairs={{0,4},{4,0},{1,5},{5,1},{2,6},{6,2},{3,7},{7,3},{8,12},{12,8},{9,1... | collective-permute-start | bytes 122888 | tf_op jit(solution)/shard_map/ppermute | solution.py:477
  69.9 5.6 %collective-permute-start.16 = (f32[144,256]{1,0:T(8,128)S(1)}, f32[144,256]{1,0:T(8,128)S(1)}, u32[]{:S(2)}, u32[]{:S(2)}) collective-permute-start(f32[144,256]{1,0:T(8,128)S(1)} %shard_map.100.refs_0_), channel_id=1, source_target_pairs={{0,2},{1,3},{2,0},{3,1},{4,6},{5,7},{6,4},{7,5},{8,10},{9,11},{10,... | collective-permute-start | bytes 442376 | tf_op jit(solution)/shard_map/ppermute | solution.py:488
  71.5 4.0 %collective-permute-start.12 = (f32[40,256]{1,0:T(8,128)S(1)}, f32[40,256]{1,0:T(8,128)S(1)}, u32[]{:S(2)}, u32[]{:S(2)}) collective-permute-start(f32[40,256]{1,0:T(8,128)S(1)} %add.41.refs_2_), channel_id=1, source_target_pairs={{0,8},{8,0},{16,24},{24,16},{1,9},{9,1},{17,25},{25,17},{2,10},{10... | collective-permute-start | bytes 122888 | tf_op jit(solution)/shard_map/ppermute | solution.py:477
  75.5 6.5 %collective-permute-start.17 = (f32[144,256]{1,0:T(8,128)S(1)}, f32[144,256]{1,0:T(8,128)S(1)}, u32[]{:S(2)}, u32[]{:S(2)}) collective-permute-start(f32[144,256]{1,0:T(8,128)S(1)} %shard_map.101.refs_0_), channel_id=1, source_target_pairs={{0,4},{4,0},{1,5},{5,1},{2,6},{6,2},{3,7},{7,3},{8,12},{12,8},{9,1... | collective-permute-start | bytes 442376 | tf_op jit(solution)/shard_map/ppermute | solution.py:488
  77.1 4.9 %collective-permute-start.13 = (f32[40,256]{1,0:T(8,128)S(1)}, f32[40,256]{1,0:T(8,128)S(1)}, u32[]{:S(2)}, u32[]{:S(2)}) collective-permute-start(f32[40,256]{1,0:T(8,128)S(1)} %add.42.refs_3_.refs_0_.refs_2_), channel_id=1, source_target_pairs={{0,16},{8,24},{16,0},{24,8},{1,17},{9,25},{17,1},{25,9},{2,18},{10... | collective-permute-start | bytes 122888 | tf_op jit(solution)/shard_map/ppermute | solution.py:477
  79.0 3.1 %copy-start.13 = (f32[4,4,32,256]{3,2,1,0:T(8,128)}, f32[4,4,32,256]{3,2,1,0:T(8,128)S(1)}, u32[]{:S(2)}) copy-start(f32[4,4,32,256]{3,2,1,0:T(8,128)S(1)} %get-tuple-element.46.refs_4_) | copy-start | bytes 1572868
  82.0 0.6 copy-start.15
  83.4 7.6 %collective-permute-start.18 = (f32[144,256]{1,0:T(8,128)}, f32[144,256]{1,0:T(8,128)}, u32[]{:S(2)}, u32[]{:S(2)}) collective-permute-start(f32[144,256]{1,0:T(8,128)} %get-tuple-element.51), channel_id=1, source_target_pairs={{0,1},{1,0},{2,3},{3,2},{4,5},{5,4},{6,7},{7,6},{8,9},{9,8},{10,11... | collective-permute-start | bytes 442376 | tf_op jit(solution)/shard_map/ppermute | solution.py:496
  83.4 1.6 %copy-start.10 = (f32[8,256,256]{2,1,0:T(8,128)S(1)}, f32[8,256,256]{2,1,0:T(8,128)}, u32[]{:S(2)}) copy-start(f32[8,256,256]{2,1,0:T(8,128)} %copy-done.9) | copy-start | bytes 6291460
  85.0 1.0 %copy-start.14 = (f32[4,4,32,256]{3,2,1,0:T(8,128)S(1)}, f32[4,4,32,256]{3,2,1,0:T(8,128)}, u32[]{:S(2)}) copy-start(f32[4,4,32,256]{3,2,1,0:T(8,128)} %copy-done.13) | copy-start | bytes 1572868
  86.0 0.8 copy-start.16
  86.8 4.2 %copy-start.18 = (f32[1,144,256]{2,1,0:T(8,128)S(1)}, f32[1,144,256]{2,1,0:T(8,128)}, u32[]{:S(2)}) copy-start(f32[1,144,256]{2,1,0:T(8,128)} %get-tuple-element.50) | copy-start | bytes 442372

commit v4 on v3

--- a/solution.py
+++ b/solution.py
@@ -194,14 +194,15 @@
     leave(token_ref)
 
 
-def far_kernel(even_ref, odd_ref, first_ref, second_ref, weight_ref, near_ref, moved_ref, out_ref, token_ref, bands_ref):
+def far_kernel(odd_ref, first_ref, second_ref, weight_ref, near_ref, moved_ref, out_ref, token_ref, bands_ref):
     rows, width = out_ref.shape[0], out_ref.shape[1]
     d = DILATION_RATE
 
     def outer(r, carry):
-        first, second = first_ref[r], second_ref[r]
-        for begin, place in ((0, odd_ref), (d, even_ref)):
-            halo = jnp.where(place[0:1] > 0.5, first.astype(F32), second.astype(F32)).astype(BF16)
+        odd = odd_ref[0:1] > 0.5
+        first, second = first_ref[r].astype(F32), second_ref[r].astype(F32)
+        for begin, halo in ((0, jnp.where(odd, first, second)), (d, jnp.where(odd, second, first))):
+            halo = halo.astype(BF16)
             shift_band(
                 moved_ref, bands_ref, begin + r, halo[0:width], halo[width : width + 8], halo[width + 8 :]
             )
@@ -261,7 +262,7 @@
         slope_ref[r] = gate + act * (1.0 - gate)
 
 
-def tap_kernel(turned_ref, near_ref, far_ref, out_ref):
+def tap_kernel(turned_ref, near_ref, far_ref, later_ref, own_ref, other_ref, total_ref):
     rows, width = near_ref.shape[1], near_ref.shape[2]
     d = DILATION_RATE
     gap = rows - d
@@ -272,12 +273,25 @@
         return dot(turned, ref[b, band : band + count].reshape(count * width, C))
 
     def column(b, carry):
-        out_ref[b] = fold(pair(b, 0, gap, near_ref, d) + pair(b, gap, d, far_ref, d), same)
-        out_ref[3 + b] = fold(pair(b, 0, rows, near_ref, 0), same)
-        out_ref[6 + b] = fold(pair(b, 0, d, far_ref, 0) + pair(b, d, gap, near_ref, 0), same)
+        total_ref[b] = fold(pair(b, 0, gap, near_ref, d) + pair(b, gap, d, far_ref, d), same)
+        total_ref[3 + b] = fold(pair(b, 0, rows, near_ref, 0), same)
+        total_ref[6 + b] = fold(pair(b, 0, d, far_ref, 0) + pair(b, d, gap, near_ref, 0), same)
         return carry
 
     lax.fori_loop(0, 3, column, 0)
+    later = later_ref[0:1] > 0.5
+    total = total_ref[...].reshape(9 * GS, C)
+    first, second = total[: own_ref.shape[0]], total[own_ref.shape[0] :]
+    own_ref[...] = jnp.where(later, second, first)
+    other_ref[...] = jnp.where(later, first, second)
+
+
+def join_kernel(scale, own_ref, other_ref, later_ref, out_ref):
+    later = later_ref[0:1] > 0.5
+    own, other = own_ref[...] * scale, other_ref[...] * scale
+    size = own.shape[0]
+    out_ref[:size] = jnp.where(later, other, own)
+    out_ref[size:] = jnp.where(later, own, other)
 
 
 def grad_kernel(x_ref, grad_ref, slope_ref, kept_ref, mean_ref, gain_ref, back_ref, sums_ref):
@@ -415,9 +429,10 @@
     first, second = swap(jnp.where(odd, first, second), jnp.where(odd, second, first), "cols")
     left, right = jnp.where(odd, first, second), jnp.where(odd, second, first)
     odd_line = jnp.broadcast_to((lax.axis_index("rows") % 2 == 1).astype(F32), (8, C))
-    even_line = 1.0 - odd_line
+    tap_axis, tap_pairs = stage_pairs[0]
+    later_line = jnp.broadcast_to((lax.axis_index(tap_axis) % 2 == 1).astype(F32), (8, C))
     halo = shape((d, width + 16, C), BF16)
-    first, second, token = run(pack_kernel, (halo, halo, TOKEN), (up, left, right, odd_line))
+    first, second, token = run(pack_kernel, (halo, halo, TOKEN), (up, left, right, odd_line), after=(later_line,))
     first, second = swap(first, second, "rows")
     stats = run(stats_kernel, shape((2 * GS + 8, C), F32), (x,), after=(token,))
     scratch = (pltpu.VMEM((width + 32, C), F32),)
@@ -440,7 +455,7 @@
             far_bands, act_grad, *token = run(
                 far_kernel,
                 (held((3, 2 * d, width, C), BF16), held(cells, F32), TOKEN),
-                (even_line, odd_line, first, second, weights, near_grad),
+                (odd_line, first, second, weights, near_grad),
                 scratch=scratch,
                 after=(stats,),
             )
@@ -456,13 +471,14 @@
         ),
         (x, stats, gain, bias),
     )
-    taps = run(tap_kernel, shape((9, GS, C), F32), (turned, near_bands, far_bands))
-
-    tap_axis, tap_pairs = stage_pairs[0]
-    later = lax.axis_index(tap_axis) % 2
-    halves = taps.reshape(2, -1, C)
-    half = lax.dynamic_index_in_dim(halves, later, 0, False)
-    half = add(half, lax.ppermute(lax.dynamic_index_in_dim(halves, 1 - later, 0, False), tap_axis, tap_pairs))
+    half = shape((9 * GS // 2, C), F32)
+    half, other = run(
+        tap_kernel,
+        (half, half),
+        (turned, near_bands, far_bands, later_line),
+        scratch=(pltpu.VMEM((9, GS, C), F32),),
+    )
+    half = add(half, lax.ppermute(other, tap_axis, tap_pairs))
 
     back, sums = run(
         grad_kernel,
@@ -492,9 +508,12 @@
         (x, back, sums, wide, lines),
         after=(half,),
     )
-    half = half * (1.0 / math.sqrt(cell_count))
     other = lax.ppermute(half, tap_axis, tap_pairs)
-    taps = jnp.where(later == 0, jnp.stack([half, other]), jnp.stack([other, half]))
+    taps = run(
+        functools.partial(join_kernel, 1.0 / math.sqrt(cell_count)),
+        shape((9 * GS, C), F32),
+        (half, other, later_line),
+    )
     return (
         input_grad.reshape(features.shape),
         taps.reshape(3, 3, GS, C),

time: 93.3 us -> 78.6 us (0.84)
  local copies, waits for them, and re-layouts: 12.8 us -> 1.25 us
  other arithmetic: 4.29 us -> 0.92 us
  starting transfers between devices: 25.7 us -> 27.5 us
  Pallas kernels: 27.5 us -> 25.9 us
    unnamed x42 -> x12, local copies, waits for them, and re-layouts: 12.2 us -> 1.24 us
    ppermute x5, starting transfers between devices: 6.83 us -> 8.87 us  [shards(): other = lax.ppermute(stats, axis, pairs)]
    select_n x1 -> x0, other arithmetic: 1.73 us -> none  [shards(): jnp.where(later == 0, jnp.stack([half, other]), jnp.stack([other, half]))]
    pallas_call x20 -> x21, Pallas kernels: 27.5 us -> 25.9 us  [run(): pl.pallas_call(kernel, out_shape=out_shapes, in_specs=[VMEM_SPEC] * count...]
  transfers between devices with their start and end apart: 19 -> 19, of which waited for: 10 -> 12; matrix products, arithmetic and copies ran while one was open for 0% -> 0% of each run, Pallas kernels for 21% -> 23%
where the time goes in v4:
time: 78.6 us; the launch traced here: 78.3 us
  starting transfers between devices  27.5 us (35%)
  Pallas kernels  25.9 us (33%)
  waiting for transfers between devices  21.8 us (28%)
  local copies, waits for them, and re-layouts  1.25 us (2%)
  other arithmetic  0.92 us (1%)
  between operations  0.9 us (1%)
    pallas_call x21, Pallas kernels, run(): pl.pallas_call(kernel, out_shape=out_shapes, in_specs=[VMEM_SPEC] * count...  25.9 us
    ppermute x5, waiting for transfers between devices, shards(): other = lax.ppermute(sums, *stage)  11.1 us
    ppermute x5, starting transfers between devices, shards(): other = lax.ppermute(stats, axis, pairs)  8.87 us
    ppermute x5, waiting for transfers between devices, shards(): other = lax.ppermute(stats, axis, pairs)  6.65 us
    ppermute x5, starting transfers between devices, shards(): other = lax.ppermute(sums, *stage)  6.24 us
    ppermute x3, starting transfers between devices, swap(): lax.ppermute(part, axis, pairs)  5.81 us
    ppermute x3, starting transfers between devices, shards(): half = add(half, lax.ppermute(half, *tap_stages[number - 1]), after=(sums,))  4.65 us
    ppermute x3, waiting for transfers between devices, swap(): lax.ppermute(part, axis, pairs)  1.9 us
  transfers between devices with their start and end apart: 19, of which 12 were waited for; matrix products, arithmetic and copies ran while one was open for 0% of the time, Pallas kernels for 23%

profile of v4, /device:TPU:0, one launch (start us, length us, event | category | flops | bytes accessed | tf_op | source)
XLA Modules:
  0.0 78.3 jit_solution(14220555526885415433)
XLA Ops:
  0.7 0.9 %slice_select_fusion = bf16[8,8,256]{2,1,0:T(8,128)(2,1)S(1)} fusion(bf16[8,256,256]{2,1,0:T(8,128)(2,1)} %bitcast.9, pred[]{:T(512)S(6)} %eq.14), kind=kLoop, calls=%fused_computation | loop fusion | flops 16384 | bytes 98305 | tf_op jit(solution)/shard_map/jit(_where)/select_n | solution.py:429
  1.5 3.0 %collective-permute-start = (bf16[8,8,256]{2,1,0:T(8,128)(2,1)S(1)}, bf16[8,8,256]{2,1,0:T(8,128)(2,1)S(1)}, u32[]{:S(2)}, u32[]{:S(2)}) collective-permute-start(bf16[8,8,256]{2,1,0:T(8,128)(2,1)S(1)} %slice_select_fusion), channel_id=1, source_target_pairs={{0,4},{4,0},{1,5},{5,1},{2,6},{6,2},{3,7},{7,3},{8,12},{12,8},{9,1... | collective-permute-start | bytes 98312 | tf_op jit(solution)/shard_map/ppermute | solution.py:406
  4.5 1.9 %collective-permute-done = bf16[8,8,256]{2,1,0:T(8,128)(2,1)S(1)} collective-permute-done((bf16[8,8,256]{2,1,0:T(8,128)(2,1)S(1)}, bf16[8,8,256]{2,1,0:T(8,128)(2,1)S(1)}, u32[]{:S(2)}, u32[]{:S(2)}) %collective-permute-start) | collective-permute-done | bytes 32800 | tf_op jit(solution)/shard_map/ppermute | solution.py:406
  6.4 0.0 copy-start.1
  6.4 1.2 %copy-done.1 = bf16[1,8,256,256]{3,2,1,0:T(8,128)(2,1)S(1)} copy-done((bf16[1,8,256,256]{3,2,1,0:T(8,128)(2,1)S(1)}, bf16[1,8,256,256]{3,2,1,0:T(8,128)(2,1)}, u32[]{:S(2)}) %copy-start.1) | copy-done | bytes 1048600
  7.6 0.4 shard_map.84
  8.0 2.1 %collective-permute-start.1 = (bf16[6,272,256]{2,1,0:T(8,128)(2,1)S(1)}, bf16[6,272,256]{2,1,0:T(8,128)(2,1)S(1)}, u32[]{:S(2)}, u32[]{:S(2)}) collective-permute-start(bf16[6,272,256]{2,1,0:T(8,128)(2,1)S(1)} %get-tuple-element.29), channel_id=1, source_target_pairs={{0,8},{16,24},{8,0},{24,16},{1,9},{17,25},{9,1},{25,17},{2,10},{18... | collective-permute-start | bytes 2506760 | tf_op jit(solution)/shard_map/ppermute | solution.py:406
  10.2 0.7 collective-permute-start.2
  10.9 3.0 %shard_map.85.refs_0_ = f32[72,256]{1,0:T(8,128)S(1)} custom-call(bf16[8,256,256]{2,1,0:T(8,128)(2,1)S(1)} %bitcast.5, f32[8,128]{1,0:T(8,128)S(1)} %get-tuple-element.31.refs_1_), custom_call_target="tpu_custom_call" | custom-call | tf_op jit(solution)/shard_map/pallas_call | solution.py:31
  13.9 0.1 collective-permute-start.3
  14.0 1.3 %collective-permute-done.3.refs_1_ = f32[72,256]{1,0:T(8,128)S(1)} collective-permute-done((f32[72,256]{1,0:T(8,128)S(1)}, f32[72,256]{1,0:T(8,128)S(1)}, u32[]{:S(2)}, u32[]{:S(2)}) %collective-permute-start.3) | collective-permute-done | bytes 73760 | tf_op jit(solution)/shard_map/ppermute | solution.py:440
  15.3 1.6 %collective-permute-start.4 = (f32[72,256]{1,0:T(8,128)S(1)}, f32[72,256]{1,0:T(8,128)S(1)}, u32[]{:S(2)}, u32[]{:S(2)}) collective-permute-start(f32[72,256]{1,0:T(8,128)S(1)} %shard_map.86.refs_0_), channel_id=1, source_target_pairs={{0,2},{1,3},{2,0},{3,1},{4,6},{5,7},{6,4},{7,5},{8,10},{9,11},{10,... | collective-permute-start | bytes 221192 | tf_op jit(solution)/shard_map/ppermute | solution.py:440
  16.8 2.9 %collective-permute-done.4.refs_1_ = f32[72,256]{1,0:T(8,128)S(1)} collective-permute-done((f32[72,256]{1,0:T(8,128)S(1)}, f32[72,256]{1,0:T(8,128)S(1)}, u32[]{:S(2)}, u32[]{:S(2)}) %collective-permute-start.4) | collective-permute-done | bytes 73760 | tf_op jit(solution)/shard_map/ppermute | solution.py:440
  19.7 1.6 %collective-permute-start.5 = (f32[72,256]{1,0:T(8,128)S(1)}, f32[72,256]{1,0:T(8,128)S(1)}, u32[]{:S(2)}, u32[]{:S(2)}) collective-permute-start(f32[72,256]{1,0:T(8,128)S(1)} %shard_map.87.refs_4_.refs_0_), channel_id=1, source_target_pairs={{0,4},{4,0},{1,5},{5,1},{2,6},{6,2},{3,7},{7,3},{8,12},{12,8},{9,1... | collective-permute-start | bytes 221192 | tf_op jit(solution)/shard_map/ppermute | solution.py:440
  21.3 0.8 %shard_map.88 = (bf16[3,8,256,256]{3,2,1,0:T(8,128)(2,1)S(1)}, bf16[9,256,256]{2,1,0:T(8,128)(2,1)S(1)}, f32[8,128]{1,0:T(8,128)S(1)}) custom-call(bf16[8,256,256]{2,1,0:T(8,128)(2,1)S(1)} %bitcast.11, bf16[8,8,256]{2,1,0:T(8,128)(2,1)S(1)} %get-tuple-element.55.refs_1_, bf16[8,8,256]{2,1,0:T(8,128)(2,1)S(1)} %get-tuple-element.54.refs_2_, ...), custom_call_target="tpu_custom_call" | custom-call | tf_op jit(solution)/shard_map/pallas_call | solution.py:31
  22.1 2.0 %collective-permute-done.5.refs_1_ = f32[72,256]{1,0:T(8,128)S(1)} collective-permute-done((f32[72,256]{1,0:T(8,128)S(1)}, f32[72,256]{1,0:T(8,128)S(1)}, u32[]{:S(2)}, u32[]{:S(2)}) %collective-permute-start.5) | collective-permute-done | bytes 73760 | tf_op jit(solution)/shard_map/ppermute | solution.py:440
  24.1 4.4 %collective-permute-start.6 = (f32[72,256]{1,0:T(8,128)S(1)}, f32[72,256]{1,0:T(8,128)S(1)}, u32[]{:S(2)}, u32[]{:S(2)}) collective-permute-start(f32[72,256]{1,0:T(8,128)S(1)} %shard_map.89.refs_2_.refs_0_), channel_id=1, source_target_pairs={{0,8},{8,0},{16,24},{24,16},{1,9},{9,1},{17,25},{25,17},{2,10},{10... | collective-permute-start | bytes 221192 | tf_op jit(solution)/shard_map/ppermute | solution.py:440
  28.5 2.6 %shard_map.90 = (f32[8,256,256]{2,1,0:T(8,128)S(1)}, f32[8,128]{1,0:T(8,128)S(1)}) custom-call(bf16[3,8,256,256]{3,2,1,0:T(8,128)(2,1)S(1)} %get-tuple-element.33.refs_0_.refs_1_, bf16[9,256,256]{2,1,0:T(8,128)(2,1)S(1)} %get-tuple-element.32.refs_1_.refs_3_, f32[72,256]{1,0:T(8,128)S(1)} %shard_map.89.refs_2_.refs_0_), custom_call_target="tpu_custom_call" | custom-call | tf_op jit(solution)/shard_map/pallas_call | solution.py:31
  31.2 1.2 %collective-permute-start.7 = (f32[72,256]{1,0:T(8,128)S(1)}, f32[72,256]{1,0:T(8,128)S(1)}, u32[]{:S(2)}, u32[]{:S(2)}) collective-permute-start(f32[72,256]{1,0:T(8,128)S(1)} %shard_map.91.refs_5_.refs_0_), channel_id=1, source_target_pairs={{0,16},{8,24},{16,0},{24,8},{1,17},{9,25},{17,1},{25,9},{2,18},{10... | collective-permute-start | bytes 221192 | tf_op jit(solution)/shard_map/ppermute | solution.py:440
  32.4 0.0 copy-start.5
  32.4 3.5 %shard_map.92 = (bf16[3,12,256,256]{3,2,1,0:T(8,128)(2,1)S(1)}, f32[8,256,256]{2,1,0:T(8,128)S(1)}, f32[8,128]{1,0:T(8,128)S(1)}) custom-call(f32[8,256]{1,0:T(8,128)S(1)} %broadcast_in_dim.10.refs_3_.refs_0_, bf16[6,272,256]{2,1,0:T(8,128)(2,1)S(1)} %collective-permute-done.1.refs_1_, bf16[6,272,256]{2,1,0:T(8,128)(2,1)S(1)} %collective-permute-done.2.refs_2_, ...), custom_call_target="tpu_custom_call" | custom-call | tf_op jit(solution)/shard_map/pallas_call | solution.py:31
  36.0 0.5 collective-permute-done.7.refs_1_
  36.6 3.3 %shard_map.94 = (bf16[256,2048]{1,0:T(8,128)(2,1)S(1)}, f32[8,256,256]{2,1,0:T(8,128)S(1)}, f32[5,3,32,256]{3,2,1,0:T(8,128)S(1)}, f32[8,256]{1,0:T(8,128)S(1)}) custom-call(bf16[8,256,256]{2,1,0:T(8,128)(2,1)S(1)} %bitcast.6, f32[72,256]{1,0:T(8,128)S(1)} %shard_map.93.refs_1_, f32[8,256]{1,0:T(8,128)S(1)} %broadcast_in_dim.24.refs_2_.refs_5_, ...), custom_call_target="tpu_custom_call" | custom-call | tf_op jit(solution)/shard_map/pallas_call | solution.py:31
  39.8 3.0 %shard_map.95 = (f32[144,256]{1,0:T(8,128)S(1)}, f32[144,256]{1,0:T(8,128)S(1)}) custom-call(bf16[256,2048]{1,0:T(8,128)(2,1)S(1)} %get-tuple-element.42.refs_0_, bf16[3,8,256,256]{3,2,1,0:T(8,128)(2,1)S(1)} %get-tuple-element.33.refs_0_.refs_1_, bf16[3,12,256,256]{3,2,1,0:T(8,128)(2,1)S(1)} %get-tuple-element.43.refs_2_, ...), custom_call_target="tpu_custom_call" | custom-call | tf_op jit(solution)/shard_map/pallas_call | solution.py:31
  42.8 0.1 collective-permute-start.8
  42.9 1.4 %collective-permute-done.8 = f32[144,256]{1,0:T(8,128)S(1)} collective-permute-done((f32[144,256]{1,0:T(8,128)S(1)}, f32[144,256]{1,0:T(8,128)S(1)}, u32[]{:S(2)}, u32[]{:S(2)}) %collective-permute-start.8) | collective-permute-done | bytes 147488 | tf_op jit(solution)/shard_map/ppermute | solution.py:481
  44.3 1.8 %collective-permute-start.14 = (f32[144,256]{1,0:T(8,128)S(1)}, f32[144,256]{1,0:T(8,128)S(1)}, u32[]{:S(2)}, u32[]{:S(2)}) collective-permute-start(f32[144,256]{1,0:T(8,128)S(1)} %add.28.refs_6_.refs_0_), channel_id=1, source_target_pairs={{0,8},{8,0},{16,24},{24,16},{1,9},{9,1},{17,25},{25,17},{2,10},{10... | collective-permute-start | bytes 442376 | tf_op jit(solution)/shard_map/ppermute | solution.py:491
  46.1 3.3 %shard_map.96 = (f32[8,256,256]{2,1,0:T(8,128)S(1)}, f32[40,256]{1,0:T(8,128)S(1)}) custom-call(bf16[8,256,256]{2,1,0:T(8,128)(2,1)S(1)} %bitcast.7, f32[8,256,256]{2,1,0:T(8,128)S(1)} %get-tuple-element.37.refs_1_, f32[8,256,256]{2,1,0:T(8,128)S(1)} %get-tuple-element.39.refs_2_, f32[5,3,32,256]{3,2,1,0:T(8,128)S(1)} %get-tuple-element.40.refs_3_.refs_0_, ...), custom_call_target="tpu_custom_call" | custom-call | tf_op jit(solution)/shard_map/pallas_call | solution.py:31
  49.4 0.8 %collective-permute-done.14.refs_1_ = f32[144,256]{1,0:T(8,128)S(1)} collective-permute-done((f32[144,256]{1,0:T(8,128)S(1)}, f32[144,256]{1,0:T(8,128)S(1)}, u32[]{:S(2)}, u32[]{:S(2)}) %collective-permute-start.14) | collective-permute-done | bytes 147488 | tf_op jit(solution)/shard_map/ppermute | solution.py:491
  50.3 1.5 %collective-permute-start.15 = (f32[144,256]{1,0:T(8,128)S(1)}, f32[144,256]{1,0:T(8,128)S(1)}, u32[]{:S(2)}, u32[]{:S(2)}) collective-permute-start(f32[144,256]{1,0:T(8,128)S(1)} %shard_map.99.refs_0_), channel_id=1, source_target_pairs={{0,16},{8,24},{16,0},{24,8},{1,17},{9,25},{17,1},{25,9},{2,18},{10... | collective-permute-start | bytes 442376 | tf_op jit(solution)/shard_map/ppermute | solution.py:504
  51.8 0.0 collective-permute-start.9
  51.8 1.2 %collective-permute-done.9 = f32[40,256]{1,0:T(8,128)S(1)} collective-permute-done((f32[40,256]{1,0:T(8,128)S(1)}, f32[40,256]{1,0:T(8,128)S(1)}, u32[]{:S(2)}, u32[]{:S(2)}) %collective-permute-start.9) | collective-permute-done | bytes 40992 | tf_op jit(solution)/shard_map/ppermute | solution.py:493
  53.0 1.5 %collective-permute-start.10 = (f32[40,256]{1,0:T(8,128)S(1)}, f32[40,256]{1,0:T(8,128)S(1)}, u32[]{:S(2)}, u32[]{:S(2)}) collective-permute-start(f32[40,256]{1,0:T(8,128)S(1)} %add.29), channel_id=1, source_target_pairs={{0,2},{1,3},{2,0},{3,1},{4,6},{5,7},{6,4},{7,5},{8,10},{9,11},{10,... | collective-permute-start | bytes 122888 | tf_op jit(solution)/shard_map/ppermute | solution.py:493
  54.5 2.5 %collective-permute-done.10 = f32[40,256]{1,0:T(8,128)S(1)} collective-permute-done((f32[40,256]{1,0:T(8,128)S(1)}, f32[40,256]{1,0:T(8,128)S(1)}, u32[]{:S(2)}, u32[]{:S(2)}) %collective-permute-start.10) | collective-permute-done | bytes 40992 | tf_op jit(solution)/shard_map/ppermute | solution.py:493
  57.0 1.5 %collective-permute-start.11 = (f32[40,256]{1,0:T(8,128)S(1)}, f32[40,256]{1,0:T(8,128)S(1)}, u32[]{:S(2)}, u32[]{:S(2)}) collective-permute-start(f32[40,256]{1,0:T(8,128)S(1)} %add.30), channel_id=1, source_target_pairs={{0,4},{4,0},{1,5},{5,1},{2,6},{6,2},{3,7},{7,3},{8,12},{12,8},{9,1... | collective-permute-start | bytes 122888 | tf_op jit(solution)/shard_map/ppermute | solution.py:493
  58.5 2.5 %collective-permute-done.11 = f32[40,256]{1,0:T(8,128)S(1)} collective-permute-done((f32[40,256]{1,0:T(8,128)S(1)}, f32[40,256]{1,0:T(8,128)S(1)}, u32[]{:S(2)}, u32[]{:S(2)}) %collective-permute-start.11) | collective-permute-done | bytes 40992 | tf_op jit(solution)/shard_map/ppermute | solution.py:493
  61.1 1.6 %collective-permute-start.16 = (f32[144,256]{1,0:T(8,128)S(1)}, f32[144,256]{1,0:T(8,128)S(1)}, u32[]{:S(2)}, u32[]{:S(2)}) collective-permute-start(f32[144,256]{1,0:T(8,128)S(1)} %shard_map.100.refs_0_), channel_id=1, source_target_pairs={{0,2},{1,3},{2,0},{3,1},{4,6},{5,7},{6,4},{7,5},{8,10},{9,11},{10,... | collective-permute-start | bytes 442376 | tf_op jit(solution)/shard_map/ppermute | solution.py:504
  62.6 1.7 %collective-permute-start.12 = (f32[40,256]{1,0:T(8,128)S(1)}, f32[40,256]{1,0:T(8,128)S(1)}, u32[]{:S(2)}, u32[]{:S(2)}) collective-permute-start(f32[40,256]{1,0:T(8,128)S(1)} %add.31.refs_2_), channel_id=1, source_target_pairs={{0,8},{8,0},{16,24},{24,16},{1,9},{9,1},{17,25},{25,17},{2,10},{10... | collective-permute-start | bytes 122888 | tf_op jit(solution)/shard_map/ppermute | solution.py:493
  64.4 2.3 %collective-permute-done.12 = f32[40,256]{1,0:T(8,128)S(1)} collective-permute-done((f32[40,256]{1,0:T(8,128)S(1)}, f32[40,256]{1,0:T(8,128)S(1)}, u32[]{:S(2)}, u32[]{:S(2)}) %collective-permute-start.12) | collective-permute-done | bytes 40992 | tf_op jit(solution)/shard_map/ppermute | solution.py:493
  66.6 0.0 collective-permute-done.16.refs_1_
  66.7 1.6 %collective-permute-start.17 = (f32[144,256]{1,0:T(8,128)S(1)}, f32[144,256]{1,0:T(8,128)S(1)}, u32[]{:S(2)}, u32[]{:S(2)}) collective-permute-start(f32[144,256]{1,0:T(8,128)S(1)} %shard_map.101.refs_0_), channel_id=1, source_target_pairs={{0,4},{4,0},{1,5},{5,1},{2,6},{6,2},{3,7},{7,3},{8,12},{12,8},{9,1... | collective-permute-start | bytes 442376 | tf_op jit(solution)/shard_map/ppermute | solution.py:504
  68.3 1.5 %collective-permute-start.13 = (f32[40,256]{1,0:T(8,128)S(1)}, f32[40,256]{1,0:T(8,128)S(1)}, u32[]{:S(2)}, u32[]{:S(2)}) collective-permute-start(f32[40,256]{1,0:T(8,128)S(1)} %add.32.refs_3_.refs_0_.refs_2_), channel_id=1, source_target_pairs={{0,16},{8,24},{16,0},{24,8},{1,17},{9,25},{17,1},{25,9},{2,18},{10... | collective-permute-start | bytes 122888 | tf_op jit(solution)/shard_map/ppermute | solution.py:493
  69.7 0.8 shard_map.97
  70.5 2.6 %collective-permute-done.13.refs_1_ = f32[40,256]{1,0:T(8,128)S(1)} collective-permute-done((f32[40,256]{1,0:T(8,128)S(1)}, f32[40,256]{1,0:T(8,128)S(1)}, u32[]{:S(2)}, u32[]{:S(2)}) %collective-permute-start.13) | collective-permute-done | bytes 40992 | tf_op jit(solution)/shard_map/ppermute | solution.py:493
  73.2 0.1 collective-permute-start.18
  73.3 4.3 %shard_map.103 = (bf16[8,256,256]{2,1,0:T(8,128)(2,1)}, f32[256]{0:T(256)}, f32[256]{0:T(256)}) custom-call(bf16[8,256,256]{2,1,0:T(8,128)(2,1)S(1)} %bitcast.8, f32[8,256,256]{2,1,0:T(8,128)S(1)} %get-tuple-element.46.refs_1_, f32[40,256]{1,0:T(8,128)S(1)} %shard_map.98.refs_2_, bf16[9,2,256,256]{3,2,1,0:T(8,128)(2,1)S(1)} %get-tuple-element.49.refs_3_, ...), custom_call_target="tpu_custom_call" | custom-call | tf_op jit(solution)/shard_map/pallas_call | solution.py:31
  77.6 0.0 collective-permute-done.18.refs_1_
  77.6 0.8 shard_map.104
  (34 shorter events, 0.3 us)
Async XLA Ops:
  0.6 10.3 %copy-start = (bf16[1,8,256,256]{3,2,1,0:T(8,128)(2,1)S(1)}, bf16[1,8,256,256]{3,2,1,0:T(8,128)(2,1)}, u32[]{:S(2)}) copy-start(bf16[1,8,256,256]{3,2,1,0:T(8,128)(2,1)} %param.5) | copy-start | bytes 3145732
  1.5 4.9 %collective-permute-start = (bf16[8,8,256]{2,1,0:T(8,128)(2,1)S(1)}, bf16[8,8,256]{2,1,0:T(8,128)(2,1)S(1)}, u32[]{:S(2)}, u32[]{:S(2)}) collective-permute-start(bf16[8,8,256]{2,1,0:T(8,128)(2,1)S(1)} %slice_select_fusion), channel_id=1, source_target_pairs={{0,4},{4,0},{1,5},{5,1},{2,6},{6,2},{3,7},{7,3},{8,12},{12,8},{9,1... | collective-permute-start | bytes 98312 | tf_op jit(solution)/shard_map/ppermute | solution.py:406
  6.4 1.2 %copy-start.1 = (bf16[1,8,256,256]{3,2,1,0:T(8,128)(2,1)S(1)}, bf16[1,8,256,256]{3,2,1,0:T(8,128)(2,1)}, u32[]{:S(2)}) copy-start(bf16[1,8,256,256]{3,2,1,0:T(8,128)(2,1)} %param.6) | copy-start | bytes 3145732
  7.6 13.6 %copy-start.2 = (bf16[1,8,256,256]{3,2,1,0:T(8,128)(2,1)S(1)}, bf16[1,8,256,256]{3,2,1,0:T(8,128)(2,1)}, u32[]{:S(2)}) copy-start(bf16[1,8,256,256]{3,2,1,0:T(8,128)(2,1)} %param.6) | copy-start | bytes 3145732
  7.6 13.6 %copy-start.3 = (bf16[3,3,32,256]{3,2,1,0:T(8,128)(2,1)S(1)}, bf16[3,3,32,256]{3,2,1,0:T(8,128)(2,1)}, u32[]{:S(2)}) copy-start(bf16[3,3,32,256]{3,2,1,0:T(8,128)(2,1)} %param.7) | copy-start | bytes 442372
  8.0 24.4 %collective-permute-start.1 = (bf16[6,272,256]{2,1,0:T(8,128)(2,1)S(1)}, bf16[6,272,256]{2,1,0:T(8,128)(2,1)S(1)}, u32[]{:S(2)}, u32[]{:S(2)}) collective-permute-start(bf16[6,272,256]{2,1,0:T(8,128)(2,1)S(1)} %get-tuple-element.29), channel_id=1, source_target_pairs={{0,8},{16,24},{8,0},{24,16},{1,9},{17,25},{9,1},{25,17},{2,10},{18... | collective-permute-start | bytes 2506760 | tf_op jit(solution)/shard_map/ppermute | solution.py:406
  10.2 22.2 %collective-permute-start.2 = (bf16[6,272,256]{2,1,0:T(8,128)(2,1)S(1)}, bf16[6,272,256]{2,1,0:T(8,128)(2,1)S(1)}, u32[]{:S(2)}, u32[]{:S(2)}) collective-permute-start(bf16[6,272,256]{2,1,0:T(8,128)(2,1)S(1)} %get-tuple-element.30), channel_id=1, source_target_pairs={{8,16},{16,8},{9,17},{17,9},{10,18},{18,10},{11,19},{19,11},{12,20... | collective-permute-start | bytes 2506760 | tf_op jit(solution)/shard_map/ppermute | solution.py:406
  13.9 1.3 %collective-permute-start.3 = (f32[72,256]{1,0:T(8,128)S(1)}, f32[72,256]{1,0:T(8,128)S(1)}, u32[]{:S(2)}, u32[]{:S(2)}) collective-permute-start(f32[72,256]{1,0:T(8,128)S(1)} %shard_map.85.refs_0_), channel_id=1, source_target_pairs={{0,1},{1,0},{2,3},{3,2},{4,5},{5,4},{6,7},{7,6},{8,9},{9,8},{10,11... | collective-permute-start | bytes 221192 | tf_op jit(solution)/shard_map/ppermute | solution.py:440
  15.3 4.4 %collective-permute-start.4 = (f32[72,256]{1,0:T(8,128)S(1)}, f32[72,256]{1,0:T(8,128)S(1)}, u32[]{:S(2)}, u32[]{:S(2)}) collective-permute-start(f32[72,256]{1,0:T(8,128)S(1)} %shard_map.86.refs_0_), channel_id=1, source_target_pairs={{0,2},{1,3},{2,0},{3,1},{4,6},{5,7},{6,4},{7,5},{8,10},{9,11},{10,... | collective-permute-start | bytes 221192 | tf_op jit(solution)/shard_map/ppermute | solution.py:440
  19.7 4.4 %collective-permute-start.5 = (f32[72,256]{1,0:T(8,128)S(1)}, f32[72,256]{1,0:T(8,128)S(1)}, u32[]{:S(2)}, u32[]{:S(2)}) collective-permute-start(f32[72,256]{1,0:T(8,128)S(1)} %shard_map.87.refs_4_.refs_0_), channel_id=1, source_target_pairs={{0,4},{4,0},{1,5},{5,1},{2,6},{6,2},{3,7},{7,3},{8,12},{12,8},{9,1... | collective-permute-start | bytes 221192 | tf_op jit(solution)/shard_map/ppermute | solution.py:440
  24.1 7.0 %collective-permute-start.6 = (f32[72,256]{1,0:T(8,128)S(1)}, f32[72,256]{1,0:T(8,128)S(1)}, u32[]{:S(2)}, u32[]{:S(2)}) collective-permute-start(f32[72,256]{1,0:T(8,128)S(1)} %shard_map.89.refs_2_.refs_0_), channel_id=1, source_target_pairs={{0,8},{8,0},{16,24},{24,16},{1,9},{9,1},{17,25},{25,17},{2,10},{10... | collective-permute-start | bytes 221192 | tf_op jit(solution)/shard_map/ppermute | solution.py:440
  31.2 5.3 %collective-permute-start.7 = (f32[72,256]{1,0:T(8,128)S(1)}, f32[72,256]{1,0:T(8,128)S(1)}, u32[]{:S(2)}, u32[]{:S(2)}) collective-permute-start(f32[72,256]{1,0:T(8,128)S(1)} %shard_map.91.refs_5_.refs_0_), channel_id=1, source_target_pairs={{0,16},{8,24},{16,0},{24,8},{1,17},{9,25},{17,1},{25,9},{2,18},{10... | collective-permute-start | bytes 221192 | tf_op jit(solution)/shard_map/ppermute | solution.py:440
  32.4 4.1 %copy-start.4 = (f32[256]{0:T(256)S(1)}, f32[256]{0:T(256)}, u32[]{:S(2)}) copy-start(f32[256]{0:T(256)} %param.8) | copy-start | bytes 3076
  32.4 4.1 %copy-start.5 = (f32[256]{0:T(256)S(1)}, f32[256]{0:T(256)}, u32[]{:S(2)}) copy-start(f32[256]{0:T(256)} %param.9) | copy-start | bytes 3076
  42.8 1.4 %collective-permute-start.8 = (f32[144,256]{1,0:T(8,128)S(1)}, f32[144,256]{1,0:T(8,128)S(1)}, u32[]{:S(2)}, u32[]{:S(2)}) collective-permute-start(f32[144,256]{1,0:T(8,128)S(1)} %get-tuple-element.45), channel_id=1, source_target_pairs={{0,1},{1,0},{2,3},{3,2},{4,5},{5,4},{6,7},{7,6},{8,9},{9,8},{10,11... | collective-permute-start | bytes 442376 | tf_op jit(solution)/shard_map/ppermute | solution.py:481
  44.3 6.0 %collective-permute-start.14 = (f32[144,256]{1,0:T(8,128)S(1)}, f32[144,256]{1,0:T(8,128)S(1)}, u32[]{:S(2)}, u32[]{:S(2)}) collective-permute-start(f32[144,256]{1,0:T(8,128)S(1)} %add.28.refs_6_.refs_0_), channel_id=1, source_target_pairs={{0,8},{8,0},{16,24},{24,16},{1,9},{9,1},{17,25},{25,17},{2,10},{10... | collective-permute-start | bytes 442376 | tf_op jit(solution)/shard_map/ppermute | solution.py:491
  50.3 10.7 %collective-permute-start.15 = (f32[144,256]{1,0:T(8,128)S(1)}, f32[144,256]{1,0:T(8,128)S(1)}, u32[]{:S(2)}, u32[]{:S(2)}) collective-permute-start(f32[144,256]{1,0:T(8,128)S(1)} %shard_map.99.refs_0_), channel_id=1, source_target_pairs={{0,16},{8,24},{16,0},{24,8},{1,17},{9,25},{17,1},{25,9},{2,18},{10... | collective-permute-start | bytes 442376 | tf_op jit(solution)/shard_map/ppermute | solution.py:504
  51.8 1.2 %collective-permute-start.9 = (f32[40,256]{1,0:T(8,128)S(1)}, f32[40,256]{1,0:T(8,128)S(1)}, u32[]{:S(2)}, u32[]{:S(2)}) collective-permute-start(f32[40,256]{1,0:T(8,128)S(1)} %get-tuple-element.47.refs_2_), channel_id=1, source_target_pairs={{0,1},{1,0},{2,3},{3,2},{4,5},{5,4},{6,7},{7,6},{8,9},{9,8},{10,11... | collective-permute-start | bytes 122888 | tf_op jit(solution)/shard_map/ppermute | solution.py:493
  53.0 4.0 %collective-permute-start.10 = (f32[40,256]{1,0:T(8,128)S(1)}, f32[40,256]{1,0:T(8,128)S(1)}, u32[]{:S(2)}, u32[]{:S(2)}) collective-permute-start(f32[40,256]{1,0:T(8,128)S(1)} %add.29), channel_id=1, source_target_pairs={{0,2},{1,3},{2,0},{3,1},{4,6},{5,7},{6,4},{7,5},{8,10},{9,11},{10,... | collective-permute-start | bytes 122888 | tf_op jit(solution)/shard_map/ppermute | solution.py:493
  57.0 4.0 %collective-permute-start.11 = (f32[40,256]{1,0:T(8,128)S(1)}, f32[40,256]{1,0:T(8,128)S(1)}, u32[]{:S(2)}, u32[]{:S(2)}) collective-permute-start(f32[40,256]{1,0:T(8,128)S(1)} %add.30), channel_id=1, source_target_pairs={{0,4},{4,0},{1,5},{5,1},{2,6},{6,2},{3,7},{7,3},{8,12},{12,8},{9,1... | collective-permute-start | bytes 122888 | tf_op jit(solution)/shard_map/ppermute | solution.py:493
  61.1 5.6 %collective-permute-start.16 = (f32[144,256]{1,0:T(8,128)S(1)}, f32[144,256]{1,0:T(8,128)S(1)}, u32[]{:S(2)}, u32[]{:S(2)}) collective-permute-start(f32[144,256]{1,0:T(8,128)S(1)} %shard_map.100.refs_0_), channel_id=1, source_target_pairs={{0,2},{1,3},{2,0},{3,1},{4,6},{5,7},{6,4},{7,5},{8,10},{9,11},{10,... | collective-permute-start | bytes 442376 | tf_op jit(solution)/shard_map/ppermute | solution.py:504
  62.6 4.0 %collective-permute-start.12 = (f32[40,256]{1,0:T(8,128)S(1)}, f32[40,256]{1,0:T(8,128)S(1)}, u32[]{:S(2)}, u32[]{:S(2)}) collective-permute-start(f32[40,256]{1,0:T(8,128)S(1)} %add.31.refs_2_), channel_id=1, source_target_pairs={{0,8},{8,0},{16,24},{24,16},{1,9},{9,1},{17,25},{25,17},{2,10},{10... | collective-permute-start | bytes 122888 | tf_op jit(solution)/shard_map/ppermute | solution.py:493
  66.7 6.5 %collective-permute-start.17 = (f32[144,256]{1,0:T(8,128)S(1)}, f32[144,256]{1,0:T(8,128)S(1)}, u32[]{:S(2)}, u32[]{:S(2)}) collective-permute-start(f32[144,256]{1,0:T(8,128)S(1)} %shard_map.101.refs_0_), channel_id=1, source_target_pairs={{0,4},{4,0},{1,5},{5,1},{2,6},{6,2},{3,7},{7,3},{8,12},{12,8},{9,1... | collective-permute-start | bytes 442376 | tf_op jit(solution)/shard_map/ppermute | solution.py:504
  68.3 4.9 %collective-permute-start.13 = (f32[40,256]{1,0:T(8,128)S(1)}, f32[40,256]{1,0:T(8,128)S(1)}, u32[]{:S(2)}, u32[]{:S(2)}) collective-permute-start(f32[40,256]{1,0:T(8,128)S(1)} %add.32.refs_3_.refs_0_.refs_2_), channel_id=1, source_target_pairs={{0,16},{8,24},{16,0},{24,8},{1,17},{9,25},{17,1},{25,9},{2,18},{10... | collective-permute-start | bytes 122888 | tf_op jit(solution)/shard_map/ppermute | solution.py:493
  73.2 4.4 %collective-permute-start.18 = (f32[144,256]{1,0:T(8,128)S(1)}, f32[144,256]{1,0:T(8,128)S(1)}, u32[]{:S(2)}, u32[]{:S(2)}) collective-permute-start(f32[144,256]{1,0:T(8,128)S(1)} %shard_map.102.refs_5_.refs_0_), channel_id=1, source_target_pairs={{0,1},{1,0},{2,3},{3,2},{4,5},{5,4},{6,7},{7,6},{8,9},{9,8},{10,11... | collective-permute-start | bytes 442376 | tf_op jit(solution)/shard_map/ppermute | solution.py:511

commit v5 on v4

--- a/solution.py
+++ b/solution.py
@@ -133,8 +133,9 @@
     out_ref[GS:] = half[GS:]
 
 
-def add_kernel(a_ref, b_ref, out_ref):
+def add_kernel(a_ref, b_ref, out_ref, token_ref):
     out_ref[...] = a_ref[...] + b_ref[...]
+    leave(token_ref)
 
 
 def shift_band(moved_ref, bands_ref, e, middle, left, right):
@@ -154,10 +155,24 @@
     return dot(jnp.concatenate(bands, axis=1), jnp.concatenate(weights, axis=0))
 
 
-def pack_kernel(up_ref, left_ref, right_ref, odd_ref, first_ref, second_ref, token_ref):
+def edge_kernel(up_ref, odd_ref, first_ref, second_ref):
+    odd = odd_ref[0:1] > 0.5
+    for r in range(up_ref.shape[0]):
+        left, right = up_ref[r, :8].astype(F32), up_ref[r, up_ref.shape[1] - 8 :].astype(F32)
+        first_ref[r] = jnp.where(odd, left, right).astype(BF16)
+        second_ref[r] = jnp.where(odd, right, left).astype(BF16)
+
+
+def pack_kernel(
+    up_ref, early_ref, late_ref, odd_column_ref, odd_ref, left_ref, right_ref, first_ref, second_ref, token_ref
+):
     rows, width = up_ref.shape[0], up_ref.shape[1]
     d = DILATION_RATE
-    odd = odd_ref[0:1] > 0.5
+    odd_column, odd = odd_column_ref[0:1] > 0.5, odd_ref[0:1] > 0.5
+    for r in range(rows):
+        early, late = early_ref[r].astype(F32), late_ref[r].astype(F32)
+        left_ref[r] = jnp.where(odd_column, early, late).astype(BF16)
+        right_ref[r] = jnp.where(odd_column, late, early).astype(BF16)
     for r in range(d):
         for begin, size, ref in ((0, width, up_ref), (width, 8, left_ref), (width + 8, 8, right_ref)):
             top, bottom = ref[r].astype(F32), ref[rows - d + r].astype(F32)
@@ -392,9 +407,7 @@
 
 
 def add(part, other, after=()):
-    if not after:
-        return part + other
-    return run(add_kernel, jax.ShapeDtypeStruct(part.shape, F32), (part, other), after=after)
+    return run(add_kernel, (jax.ShapeDtypeStruct(part.shape, F32), TOKEN), (part, other), after=after)
 
 
 def swap(earlier, later, axis):
@@ -424,15 +437,16 @@
     held = pltpu.VMEM
     cells = (rows, width, C)
 
-    odd = lax.axis_index("cols") % 2 == 1
-    first, second = up[:, :8], up[:, -8:]
-    first, second = swap(jnp.where(odd, first, second), jnp.where(odd, second, first), "cols")
-    left, right = jnp.where(odd, first, second), jnp.where(odd, second, first)
-    odd_line = jnp.broadcast_to((lax.axis_index("rows") % 2 == 1).astype(F32), (8, C))
+    odd_line = lambda axis: jnp.broadcast_to((lax.axis_index(axis) % 2 == 1).astype(F32), (8, C))
     tap_axis, tap_pairs = stage_pairs[0]
-    later_line = jnp.broadcast_to((lax.axis_index(tap_axis) % 2 == 1).astype(F32), (8, C))
+    odd_column, odd_row, later_line = odd_line("cols"), odd_line("rows"), odd_line(tap_axis)
+    edge = shape((rows, 8, C), BF16)
+    first, second = run(edge_kernel, (edge, edge), (up, odd_column), after=(odd_row, later_line))
+    first, second = swap(first, second, "cols")
     halo = shape((d, width + 16, C), BF16)
-    first, second, token = run(pack_kernel, (halo, halo, TOKEN), (up, left, right, odd_line), after=(later_line,))
+    left, right, first, second, token = run(
+        pack_kernel, (edge, edge, halo, halo, TOKEN), (up, first, second, odd_column, odd_row)
+    )
     first, second = swap(first, second, "rows")
     stats = run(stats_kernel, shape((2 * GS + 8, C), F32), (x,), after=(token,))
     scratch = (pltpu.VMEM((width + 32, C), F32),)
@@ -455,7 +469,7 @@
             far_bands, act_grad, *token = run(
                 far_kernel,
                 (held((3, 2 * d, width, C), BF16), held(cells, F32), TOKEN),
-                (odd_line, first, second, weights, near_grad),
+                (odd_row, first, second, weights, near_grad),
                 scratch=scratch,
                 after=(stats,),
             )
@@ -478,7 +492,7 @@
         (turned, near_bands, far_bands, later_line),
         scratch=(pltpu.VMEM((9, GS, C), F32),),
     )
-    half = add(half, lax.ppermute(other, tap_axis, tap_pairs))
+    half, _ = add(half, lax.ppermute(other, tap_axis, tap_pairs))
 
     back, sums = run(
         grad_kernel,
@@ -488,20 +502,23 @@
     )
     row_stages = [stage for stage in stage_pairs[1:] if stage[0] == "rows"]
     tap_stages = row_stages + [stage for stage in stage_pairs[1:] if stage[0] != "rows"]
-    half = add(half, lax.ppermute(half, *tap_stages[0]), after=(sums,))
+    in_flight = lax.ppermute(half, *tap_stages[0])
     for number, stage in enumerate(stage_pairs):
         other = lax.ppermute(sums, *stage)
         token = ()
+        if number == 1 or 2 < number:
+            half, *token = add(half, in_flight, after=(sums,))
+            in_flight = lax.ppermute(half, *tap_stages[max(number - 1, 1)])
         if number == count - 1:
-            wide, lines, *token = run(
+            wide, lines, tag = run(
                 prepare_kernel,
                 (held((2 * ITERS - 1, 2, C, C), BF16), held((4, ITERS - 1, GS, C), F32), TOKEN),
                 (kept, mean, gain),
                 after=(sums,),
             )
-        sums = add(sums, other, after=token)
-        if 2 <= number < count:
-            half = add(half, lax.ppermute(half, *tap_stages[number - 1]), after=(sums,))
+            token = [*token, tag]
+        sums, _ = add(sums, other, after=token)
+    half, _ = add(half, in_flight, after=(sums,))
     input_grad, gain_grad, bias_grad = run(
         functools.partial(final_kernel, cell_count),
         (shape(cells, BF16), shape((C,), F32), shape((C,), F32)),

time: 78.6 us -> 83.4 us (1.061)
  Pallas kernels: 25.9 us -> 30.8 us
  local copies, waits for them, and re-layouts: 1.25 us -> 2.56 us
  starting transfers between devices: 27.5 us -> 26.4 us
  other arithmetic: 0.92 us -> 0 us
    pallas_call x21 -> x27, Pallas kernels: 25.9 us -> 30.8 us  [run(): pl.pallas_call(kernel, out_shape=out_shapes, in_specs=[VMEM_SPEC] * count...]
    ppermute x5, waiting for transfers between devices: 11.1 us -> 12.6 us  [shards(): other = lax.ppermute(sums, *stage)]
    unnamed x12 -> x14, local copies, waits for them, and re-layouts: 1.24 us -> 2.54 us
    ppermute x5, starting transfers between devices: 6.24 us -> 5.26 us  [shards(): other = lax.ppermute(sums, *stage)]
    select_n x2 -> x0, other arithmetic: 0.88 us -> none  [the longest x1 0.87 us: shards(): jnp.where(odd, first, second)]
  transfers between devices with their start and end apart: 19 -> 19, of which waited for: 12 -> 11; matrix products, arithmetic and copies ran while one was open for 0% -> 0% of each run, Pallas kernels for 23% -> 26%
where the time goes in v5:
time: 83.4 us; the launch traced here: 83.2 us
  Pallas kernels  30.8 us (37%)
  starting transfers between devices  26.4 us (32%)
  waiting for transfers between devices  22.5 us (27%)
  local copies, waits for them, and re-layouts  2.56 us (3%)
  between operations  0.91 us (1%)
    pallas_call x27, Pallas kernels, run(): pl.pallas_call(kernel, out_shape=out_shapes, in_specs=[VMEM_SPEC] * count...  30.8 us
    ppermute x5, waiting for transfers between devices, shards(): other = lax.ppermute(sums, *stage)  12.6 us
    ppermute x5, starting transfers between devices, shards(): other = lax.ppermute(stats, axis, pairs)  8.88 us
    ppermute x5, waiting for transfers between devices, shards(): other = lax.ppermute(stats, axis, pairs)  6.65 us
    ppermute x3, starting transfers between devices, swap(): lax.ppermute(part, axis, pairs)  5.81 us
    ppermute x5, starting transfers between devices, shards(): other = lax.ppermute(sums, *stage)  5.26 us
    ppermute x3, starting transfers between devices, shards(): in_flight = lax.ppermute(half, *tap_stages[max(number - 1, 1)])  4.66 us
    unnamed x14, local copies, waits for them, and re-layouts  2.54 us
  transfers between devices with their start and end apart: 19, of which 11 were waited for; matrix products, arithmetic and copies ran while one was open for 0% of the time, Pallas kernels for 26%

profile of v5, /device:TPU:0, one launch (start us, length us, event | category | flops | bytes accessed | tf_op | source)
XLA Modules:
  0.0 83.2 jit_solution(12664720073195086642)
XLA Ops:
  0.7 1.3 %copy-done.1 = bf16[1,8,256,256]{3,2,1,0:T(8,128)(2,1)S(1)} copy-done((bf16[1,8,256,256]{3,2,1,0:T(8,128)(2,1)S(1)}, bf16[1,8,256,256]{3,2,1,0:T(8,128)(2,1)}, u32[]{:S(2)}) %copy-start.1) | copy-done | bytes 1048600
  2.0 0.6 shard_map.84
  2.6 3.0 %collective-permute-start = (bf16[8,8,256]{2,1,0:T(8,128)(2,1)S(1)}, bf16[8,8,256]{2,1,0:T(8,128)(2,1)S(1)}, u32[]{:S(2)}, u32[]{:S(2)}) collective-permute-start(bf16[8,8,256]{2,1,0:T(8,128)(2,1)S(1)} %get-tuple-element.45), channel_id=1, source_target_pairs={{0,4},{4,0},{1,5},{5,1},{2,6},{6,2},{3,7},{7,3},{8,12},{12,8},{9,1... | collective-permute-start | bytes 98312 | tf_op jit(solution)/shard_map/ppermute | solution.py:419
  5.6 1.9 %collective-permute-done.refs_1_ = bf16[8,8,256]{2,1,0:T(8,128)(2,1)S(1)} collective-permute-done((bf16[8,8,256]{2,1,0:T(8,128)(2,1)S(1)}, bf16[8,8,256]{2,1,0:T(8,128)(2,1)S(1)}, u32[]{:S(2)}, u32[]{:S(2)}) %collective-permute-start) | collective-permute-done | bytes 32800 | tf_op jit(solution)/shard_map/ppermute | solution.py:419
  7.5 1.2 %copy-done.2 = bf16[1,8,256,256]{3,2,1,0:T(8,128)(2,1)S(1)} copy-done((bf16[1,8,256,256]{3,2,1,0:T(8,128)(2,1)S(1)}, bf16[1,8,256,256]{3,2,1,0:T(8,128)(2,1)}, u32[]{:S(2)}) %copy-start.2) | copy-done | bytes 1048600
  8.7 0.5 shard_map.85
  9.3 2.1 %collective-permute-start.1 = (bf16[6,272,256]{2,1,0:T(8,128)(2,1)S(1)}, bf16[6,272,256]{2,1,0:T(8,128)(2,1)S(1)}, u32[]{:S(2)}, u32[]{:S(2)}) collective-permute-start(bf16[6,272,256]{2,1,0:T(8,128)(2,1)S(1)} %get-tuple-element.46), channel_id=1, source_target_pairs={{0,8},{16,24},{8,0},{24,16},{1,9},{17,25},{9,1},{25,17},{2,10},{18... | collective-permute-start | bytes 2506760 | tf_op jit(solution)/shard_map/ppermute | solution.py:419
  11.4 0.7 collective-permute-start.2
  12.1 3.0 %shard_map.86.refs_0_ = f32[72,256]{1,0:T(8,128)S(1)} custom-call(bf16[8,256,256]{2,1,0:T(8,128)(2,1)S(1)} %bitcast.5, f32[8,128]{1,0:T(8,128)S(1)} %get-tuple-element.50.refs_1_), custom_call_target="tpu_custom_call" | custom-call | tf_op jit(solution)/shard_map/pallas_call | solution.py:31
  15.2 1.3 %collective-permute-done.3.refs_1_ = f32[72,256]{1,0:T(8,128)S(1)} collective-permute-done((f32[72,256]{1,0:T(8,128)S(1)}, f32[72,256]{1,0:T(8,128)S(1)}, u32[]{:S(2)}, u32[]{:S(2)}) %collective-permute-start.3) | collective-permute-done | bytes 73760 | tf_op jit(solution)/shard_map/ppermute | solution.py:454
  16.5 1.6 %collective-permute-start.4 = (f32[72,256]{1,0:T(8,128)S(1)}, f32[72,256]{1,0:T(8,128)S(1)}, u32[]{:S(2)}, u32[]{:S(2)}) collective-permute-start(f32[72,256]{1,0:T(8,128)S(1)} %shard_map.87.refs_0_), channel_id=1, source_target_pairs={{0,2},{1,3},{2,0},{3,1},{4,6},{5,7},{6,4},{7,5},{8,10},{9,11},{10,... | collective-permute-start | bytes 221192 | tf_op jit(solution)/shard_map/ppermute | solution.py:454
  18.0 2.9 %collective-permute-done.4.refs_1_ = f32[72,256]{1,0:T(8,128)S(1)} collective-permute-done((f32[72,256]{1,0:T(8,128)S(1)}, f32[72,256]{1,0:T(8,128)S(1)}, u32[]{:S(2)}, u32[]{:S(2)}) %collective-permute-start.4) | collective-permute-done | bytes 73760 | tf_op jit(solution)/shard_map/ppermute | solution.py:454
  20.9 1.6 %collective-permute-start.5 = (f32[72,256]{1,0:T(8,128)S(1)}, f32[72,256]{1,0:T(8,128)S(1)}, u32[]{:S(2)}, u32[]{:S(2)}) collective-permute-start(f32[72,256]{1,0:T(8,128)S(1)} %shard_map.88.refs_4_.refs_0_), channel_id=1, source_target_pairs={{0,4},{4,0},{1,5},{5,1},{2,6},{6,2},{3,7},{7,3},{8,12},{12,8},{9,1... | collective-permute-start | bytes 221192 | tf_op jit(solution)/shard_map/ppermute | solution.py:454
  22.5 0.8 shard_map.89
  23.3 2.0 %collective-permute-done.5.refs_1_ = f32[72,256]{1,0:T(8,128)S(1)} collective-permute-done((f32[72,256]{1,0:T(8,128)S(1)}, f32[72,256]{1,0:T(8,128)S(1)}, u32[]{:S(2)}, u32[]{:S(2)}) %collective-permute-start.5) | collective-permute-done | bytes 73760 | tf_op jit(solution)/shard_map/ppermute | solution.py:454
  25.3 4.4 %collective-permute-start.6 = (f32[72,256]{1,0:T(8,128)S(1)}, f32[72,256]{1,0:T(8,128)S(1)}, u32[]{:S(2)}, u32[]{:S(2)}) collective-permute-start(f32[72,256]{1,0:T(8,128)S(1)} %shard_map.90.refs_2_.refs_0_), channel_id=1, source_target_pairs={{0,8},{8,0},{16,24},{24,16},{1,9},{9,1},{17,25},{25,17},{2,10},{10... | collective-permute-start | bytes 221192 | tf_op jit(solution)/shard_map/ppermute | solution.py:454
  29.8 2.6 %shard_map.91 = (f32[8,256,256]{2,1,0:T(8,128)S(1)}, f32[8,128]{1,0:T(8,128)S(1)}) custom-call(bf16[3,8,256,256]{3,2,1,0:T(8,128)(2,1)S(1)} %get-tuple-element.52.refs_0_.refs_1_, bf16[9,256,256]{2,1,0:T(8,128)(2,1)S(1)} %get-tuple-element.51.refs_1_.refs_3_, f32[72,256]{1,0:T(8,128)S(1)} %shard_map.90.refs_2_.refs_0_), custom_call_target="tpu_custom_call" | custom-call | tf_op jit(solution)/shard_map/pallas_call | solution.py:31
  32.4 1.3 %collective-permute-start.7 = (f32[72,256]{1,0:T(8,128)S(1)}, f32[72,256]{1,0:T(8,128)S(1)}, u32[]{:S(2)}, u32[]{:S(2)}) collective-permute-start(f32[72,256]{1,0:T(8,128)S(1)} %shard_map.92.refs_5_.refs_0_), channel_id=1, source_target_pairs={{0,16},{8,24},{16,0},{24,8},{1,17},{9,25},{17,1},{25,9},{2,18},{10... | collective-permute-start | bytes 221192 | tf_op jit(solution)/shard_map/ppermute | solution.py:454
  33.7 3.5 %shard_map.93 = (bf16[3,12,256,256]{3,2,1,0:T(8,128)(2,1)S(1)}, f32[8,256,256]{2,1,0:T(8,128)S(1)}, f32[8,128]{1,0:T(8,128)S(1)}) custom-call(f32[8,256]{1,0:T(8,128)S(1)} %broadcast_in_dim.24.refs_2_.refs_4_.refs_0_, bf16[6,272,256]{2,1,0:T(8,128)(2,1)S(1)} %collective-permute-done.1.refs_1_, bf16[6,272,256]{2,1,0:T(8,128)(2,1)S(1)} %collective-permute-done.2.refs_2_, ...), custom_call_target="tpu_custom_call" | custom-call | tf_op jit(solution)/shard_map/pallas_call | solution.py:31
  37.2 0.5 collective-permute-done.7.refs_1_
  37.8 3.3 %shard_map.95 = (bf16[256,2048]{1,0:T(8,128)(2,1)S(1)}, f32[8,256,256]{2,1,0:T(8,128)S(1)}, f32[5,3,32,256]{3,2,1,0:T(8,128)S(1)}, f32[8,256]{1,0:T(8,128)S(1)}) custom-call(bf16[8,256,256]{2,1,0:T(8,128)(2,1)S(1)} %bitcast.6, f32[72,256]{1,0:T(8,128)S(1)} %shard_map.94.refs_1_, f32[8,256]{1,0:T(8,128)S(1)} %broadcast_in_dim.28.refs_2_.refs_5_, ...), custom_call_target="tpu_custom_call" | custom-call | tf_op jit(solution)/shard_map/pallas_call | solution.py:31
  41.0 3.0 %shard_map.96 = (f32[144,256]{1,0:T(8,128)S(1)}, f32[144,256]{1,0:T(8,128)S(1)}) custom-call(bf16[256,2048]{1,0:T(8,128)(2,1)S(1)} %get-tuple-element.61.refs_0_, bf16[3,8,256,256]{3,2,1,0:T(8,128)(2,1)S(1)} %get-tuple-element.52.refs_0_.refs_1_, bf16[3,12,256,256]{3,2,1,0:T(8,128)(2,1)S(1)} %get-tuple-element.62.refs_2_, ...), custom_call_target="tpu_custom_call" | custom-call | tf_op jit(solution)/shard_map/pallas_call | solution.py:31
  44.1 0.1 collective-permute-start.8
  44.1 1.4 %collective-permute-done.8.refs_1_ = f32[144,256]{1,0:T(8,128)S(1)} collective-permute-done((f32[144,256]{1,0:T(8,128)S(1)}, f32[144,256]{1,0:T(8,128)S(1)}, u32[]{:S(2)}, u32[]{:S(2)}) %collective-permute-start.8) | collective-permute-done | bytes 147488 | tf_op jit(solution)/shard_map/ppermute | solution.py:495
  45.5 0.6 shard_map.97
  46.1 1.7 %collective-permute-start.11 = (f32[144,256]{1,0:T(8,128)S(1)}, f32[144,256]{1,0:T(8,128)S(1)}, u32[]{:S(2)}, u32[]{:S(2)}) collective-permute-start(f32[144,256]{1,0:T(8,128)S(1)} %get-tuple-element.65.refs_6_.refs_0_), channel_id=1, source_target_pairs={{0,8},{8,0},{16,24},{24,16},{1,9},{9,1},{17,25},{25,17},{2,10},{10... | collective-permute-start | bytes 442376 | tf_op jit(solution)/shard_map/ppermute | solution.py:505
  47.8 3.3 %shard_map.98 = (f32[8,256,256]{2,1,0:T(8,128)S(1)}, f32[40,256]{1,0:T(8,128)S(1)}) custom-call(bf16[8,256,256]{2,1,0:T(8,128)(2,1)S(1)} %bitcast.7, f32[8,256,256]{2,1,0:T(8,128)S(1)} %get-tuple-element.56.refs_1_, f32[8,256,256]{2,1,0:T(8,128)S(1)} %get-tuple-element.58.refs_2_, f32[5,3,32,256]{3,2,1,0:T(8,128)S(1)} %get-tuple-element.59.refs_3_.refs_0_, ...), custom_call_target="tpu_custom_call" | custom-call | tf_op jit(solution)/shard_map/pallas_call | solution.py:31
  51.3 1.2 %collective-permute-done.9.refs_1_ = f32[40,256]{1,0:T(8,128)S(1)} collective-permute-done((f32[40,256]{1,0:T(8,128)S(1)}, f32[40,256]{1,0:T(8,128)S(1)}, u32[]{:S(2)}, u32[]{:S(2)}) %collective-permute-start.9) | collective-permute-done | bytes 40992 | tf_op jit(solution)/shard_map/ppermute | solution.py:507
  52.5 0.6 shard_map.99
  53.1 1.5 %collective-permute-start.14 = (f32[144,256]{1,0:T(8,128)S(1)}, f32[144,256]{1,0:T(8,128)S(1)}, u32[]{:S(2)}, u32[]{:S(2)}) collective-permute-start(f32[144,256]{1,0:T(8,128)S(1)} %get-tuple-element.72.refs_0_), channel_id=1, source_target_pairs={{0,16},{8,24},{16,0},{24,8},{1,17},{9,25},{17,1},{25,9},{2,18},{10... | collective-permute-start | bytes 442376 | tf_op jit(solution)/shard_map/ppermute | solution.py:511
  54.6 1.5 %collective-permute-start.10 = (f32[40,256]{1,0:T(8,128)S(1)}, f32[40,256]{1,0:T(8,128)S(1)}, u32[]{:S(2)}, u32[]{:S(2)}) collective-permute-start(f32[40,256]{1,0:T(8,128)S(1)} %get-tuple-element.68.refs_2_.refs_0_), channel_id=1, source_target_pairs={{0,2},{1,3},{2,0},{3,1},{4,6},{5,7},{6,4},{7,5},{8,10},{9,11},{10,... | collective-permute-start | bytes 122888 | tf_op jit(solution)/shard_map/ppermute | solution.py:507
  56.1 2.5 %collective-permute-done.10.refs_1_ = f32[40,256]{1,0:T(8,128)S(1)} collective-permute-done((f32[40,256]{1,0:T(8,128)S(1)}, f32[40,256]{1,0:T(8,128)S(1)}, u32[]{:S(2)}, u32[]{:S(2)}) %collective-permute-start.10) | collective-permute-done | bytes 40992 | tf_op jit(solution)/shard_map/ppermute | solution.py:507
  58.6 0.6 shard_map.101
  59.2 1.5 %collective-permute-start.12 = (f32[40,256]{1,0:T(8,128)S(1)}, f32[40,256]{1,0:T(8,128)S(1)}, u32[]{:S(2)}, u32[]{:S(2)}) collective-permute-start(f32[40,256]{1,0:T(8,128)S(1)} %get-tuple-element.70.refs_0_), channel_id=1, source_target_pairs={{0,4},{4,0},{1,5},{5,1},{2,6},{6,2},{3,7},{7,3},{8,12},{12,8},{9,1... | collective-permute-start | bytes 122888 | tf_op jit(solution)/shard_map/ppermute | solution.py:507
  60.7 2.5 %collective-permute-done.12.refs_1_ = f32[40,256]{1,0:T(8,128)S(1)} collective-permute-done((f32[40,256]{1,0:T(8,128)S(1)}, f32[40,256]{1,0:T(8,128)S(1)}, u32[]{:S(2)}, u32[]{:S(2)}) %collective-permute-start.12) | collective-permute-done | bytes 40992 | tf_op jit(solution)/shard_map/ppermute | solution.py:507
  63.2 0.6 shard_map.102
  63.8 1.6 %collective-permute-start.16 = (f32[144,256]{1,0:T(8,128)S(1)}, f32[144,256]{1,0:T(8,128)S(1)}, u32[]{:S(2)}, u32[]{:S(2)}) collective-permute-start(f32[144,256]{1,0:T(8,128)S(1)} %get-tuple-element.75.refs_0_), channel_id=1, source_target_pairs={{0,2},{1,3},{2,0},{3,1},{4,6},{5,7},{6,4},{7,5},{8,10},{9,11},{10,... | collective-permute-start | bytes 442376 | tf_op jit(solution)/shard_map/ppermute | solution.py:511
  65.4 0.7 collective-permute-start.13
  66.1 3.3 %collective-permute-done.13.refs_1_ = f32[40,256]{1,0:T(8,128)S(1)} collective-permute-done((f32[40,256]{1,0:T(8,128)S(1)}, f32[40,256]{1,0:T(8,128)S(1)}, u32[]{:S(2)}, u32[]{:S(2)}) %collective-permute-start.13) | collective-permute-done | bytes 40992 | tf_op jit(solution)/shard_map/ppermute | solution.py:507
  69.4 0.6 shard_map.104
  70.0 1.6 %collective-permute-start.17 = (f32[144,256]{1,0:T(8,128)S(1)}, f32[144,256]{1,0:T(8,128)S(1)}, u32[]{:S(2)}, u32[]{:S(2)}) collective-permute-start(f32[144,256]{1,0:T(8,128)S(1)} %get-tuple-element.81.refs_0_), channel_id=1, source_target_pairs={{0,4},{4,0},{1,5},{5,1},{2,6},{6,2},{3,7},{7,3},{8,12},{12,8},{9,1... | collective-permute-start | bytes 442376 | tf_op jit(solution)/shard_map/ppermute | solution.py:511
  71.6 1.5 %collective-permute-start.15 = (f32[40,256]{1,0:T(8,128)S(1)}, f32[40,256]{1,0:T(8,128)S(1)}, u32[]{:S(2)}, u32[]{:S(2)}) collective-permute-start(f32[40,256]{1,0:T(8,128)S(1)} %get-tuple-element.74.refs_2_.refs_3_.refs_0_), channel_id=1, source_target_pairs={{0,16},{8,24},{16,0},{24,8},{1,17},{9,25},{17,1},{25,9},{2,18},{10... | collective-permute-start | bytes 122888 | tf_op jit(solution)/shard_map/ppermute | solution.py:507
  73.1 0.8 shard_map.106
  73.9 3.1 %collective-permute-done.15.refs_1_ = f32[40,256]{1,0:T(8,128)S(1)} collective-permute-done((f32[40,256]{1,0:T(8,128)S(1)}, f32[40,256]{1,0:T(8,128)S(1)}, u32[]{:S(2)}, u32[]{:S(2)}) %collective-permute-start.15) | collective-permute-done | bytes 40992 | tf_op jit(solution)/shard_map/ppermute | solution.py:507
  76.9 0.6 shard_map.107
  77.5 0.6 shard_map.108
  78.2 4.3 %shard_map.109 = (bf16[8,256,256]{2,1,0:T(8,128)(2,1)}, f32[256]{0:T(256)}, f32[256]{0:T(256)}) custom-call(bf16[8,256,256]{2,1,0:T(8,128)(2,1)S(1)} %bitcast.8, f32[8,256,256]{2,1,0:T(8,128)S(1)} %get-tuple-element.66.refs_1_, f32[40,256]{1,0:T(8,128)S(1)} %get-tuple-element.78.refs_2_, bf16[9,2,256,256]{3,2,1,0:T(8,128)(2,1)S(1)} %get-tuple-element.79.refs_3_, ...), custom_call_target="tpu_custom_call" | custom-call | tf_op jit(solution)/shard_map/pallas_call | solution.py:31
  82.4 0.8 shard_map.110
  (37 shorter events, 0.3 us)
Async XLA Ops:
  0.6 11.5 %copy-start = (bf16[1,8,256,256]{3,2,1,0:T(8,128)(2,1)S(1)}, bf16[1,8,256,256]{3,2,1,0:T(8,128)(2,1)}, u32[]{:S(2)}) copy-start(bf16[1,8,256,256]{3,2,1,0:T(8,128)(2,1)} %param.5) | copy-start | bytes 3145732
  0.7 1.3 %copy-start.1 = (bf16[1,8,256,256]{3,2,1,0:T(8,128)(2,1)S(1)}, bf16[1,8,256,256]{3,2,1,0:T(8,128)(2,1)}, u32[]{:S(2)}) copy-start(bf16[1,8,256,256]{3,2,1,0:T(8,128)(2,1)} %param.6) | copy-start | bytes 3145732
  2.0 20.5 %copy-start.4 = (bf16[3,3,32,256]{3,2,1,0:T(8,128)(2,1)S(1)}, bf16[3,3,32,256]{3,2,1,0:T(8,128)(2,1)}, u32[]{:S(2)}) copy-start(bf16[3,3,32,256]{3,2,1,0:T(8,128)(2,1)} %param.7) | copy-start | bytes 442372
  2.6 4.9 %collective-permute-start = (bf16[8,8,256]{2,1,0:T(8,128)(2,1)S(1)}, bf16[8,8,256]{2,1,0:T(8,128)(2,1)S(1)}, u32[]{:S(2)}, u32[]{:S(2)}) collective-permute-start(bf16[8,8,256]{2,1,0:T(8,128)(2,1)S(1)} %get-tuple-element.45), channel_id=1, source_target_pairs={{0,4},{4,0},{1,5},{5,1},{2,6},{6,2},{3,7},{7,3},{8,12},{12,8},{9,1... | collective-permute-start | bytes 98312 | tf_op jit(solution)/shard_map/ppermute | solution.py:419
  7.5 1.2 %copy-start.2 = (bf16[1,8,256,256]{3,2,1,0:T(8,128)(2,1)S(1)}, bf16[1,8,256,256]{3,2,1,0:T(8,128)(2,1)}, u32[]{:S(2)}) copy-start(bf16[1,8,256,256]{3,2,1,0:T(8,128)(2,1)} %param.6) | copy-start | bytes 3145732
  8.7 13.8 %copy-start.3 = (bf16[1,8,256,256]{3,2,1,0:T(8,128)(2,1)S(1)}, bf16[1,8,256,256]{3,2,1,0:T(8,128)(2,1)}, u32[]{:S(2)}) copy-start(bf16[1,8,256,256]{3,2,1,0:T(8,128)(2,1)} %param.6) | copy-start | bytes 3145732
  9.3 24.4 %collective-permute-start.1 = (bf16[6,272,256]{2,1,0:T(8,128)(2,1)S(1)}, bf16[6,272,256]{2,1,0:T(8,128)(2,1)S(1)}, u32[]{:S(2)}, u32[]{:S(2)}) collective-permute-start(bf16[6,272,256]{2,1,0:T(8,128)(2,1)S(1)} %get-tuple-element.46), channel_id=1, source_target_pairs={{0,8},{16,24},{8,0},{24,16},{1,9},{17,25},{9,1},{25,17},{2,10},{18... | collective-permute-start | bytes 2506760 | tf_op jit(solution)/shard_map/ppermute | solution.py:419
  11.4 22.2 %collective-permute-start.2 = (bf16[6,272,256]{2,1,0:T(8,128)(2,1)S(1)}, bf16[6,272,256]{2,1,0:T(8,128)(2,1)S(1)}, u32[]{:S(2)}, u32[]{:S(2)}) collective-permute-start(bf16[6,272,256]{2,1,0:T(8,128)(2,1)S(1)} %get-tuple-element.47), channel_id=1, source_target_pairs={{8,16},{16,8},{9,17},{17,9},{10,18},{18,10},{11,19},{19,11},{12,20... | collective-permute-start | bytes 2506760 | tf_op jit(solution)/shard_map/ppermute | solution.py:419
  15.1 1.3 %collective-permute-start.3 = (f32[72,256]{1,0:T(8,128)S(1)}, f32[72,256]{1,0:T(8,128)S(1)}, u32[]{:S(2)}, u32[]{:S(2)}) collective-permute-start(f32[72,256]{1,0:T(8,128)S(1)} %shard_map.86.refs_0_), channel_id=1, source_target_pairs={{0,1},{1,0},{2,3},{3,2},{4,5},{5,4},{6,7},{7,6},{8,9},{9,8},{10,11... | collective-permute-start | bytes 221192 | tf_op jit(solution)/shard_map/ppermute | solution.py:454
  16.5 4.4 %collective-permute-start.4 = (f32[72,256]{1,0:T(8,128)S(1)}, f32[72,256]{1,0:T(8,128)S(1)}, u32[]{:S(2)}, u32[]{:S(2)}) collective-permute-start(f32[72,256]{1,0:T(8,128)S(1)} %shard_map.87.refs_0_), channel_id=1, source_target_pairs={{0,2},{1,3},{2,0},{3,1},{4,6},{5,7},{6,4},{7,5},{8,10},{9,11},{10,... | collective-permute-start | bytes 221192 | tf_op jit(solution)/shard_map/ppermute | solution.py:454
  20.9 4.4 %collective-permute-start.5 = (f32[72,256]{1,0:T(8,128)S(1)}, f32[72,256]{1,0:T(8,128)S(1)}, u32[]{:S(2)}, u32[]{:S(2)}) collective-permute-start(f32[72,256]{1,0:T(8,128)S(1)} %shard_map.88.refs_4_.refs_0_), channel_id=1, source_target_pairs={{0,4},{4,0},{1,5},{5,1},{2,6},{6,2},{3,7},{7,3},{8,12},{12,8},{9,1... | collective-permute-start | bytes 221192 | tf_op jit(solution)/shard_map/ppermute | solution.py:454
  25.3 7.0 %collective-permute-start.6 = (f32[72,256]{1,0:T(8,128)S(1)}, f32[72,256]{1,0:T(8,128)S(1)}, u32[]{:S(2)}, u32[]{:S(2)}) collective-permute-start(f32[72,256]{1,0:T(8,128)S(1)} %shard_map.90.refs_2_.refs_0_), channel_id=1, source_target_pairs={{0,8},{8,0},{16,24},{24,16},{1,9},{9,1},{17,25},{25,17},{2,10},{10... | collective-permute-start | bytes 221192 | tf_op jit(solution)/shard_map/ppermute | solution.py:454
  32.4 5.3 %collective-permute-start.7 = (f32[72,256]{1,0:T(8,128)S(1)}, f32[72,256]{1,0:T(8,128)S(1)}, u32[]{:S(2)}, u32[]{:S(2)}) collective-permute-start(f32[72,256]{1,0:T(8,128)S(1)} %shard_map.92.refs_5_.refs_0_), channel_id=1, source_target_pairs={{0,16},{8,24},{16,0},{24,8},{1,17},{9,25},{17,1},{25,9},{2,18},{10... | collective-permute-start | bytes 221192 | tf_op jit(solution)/shard_map/ppermute | solution.py:454
  33.7 4.1 %copy-start.5 = (f32[256]{0:T(256)S(1)}, f32[256]{0:T(256)}, u32[]{:S(2)}) copy-start(f32[256]{0:T(256)} %param.8) | copy-start | bytes 3076
  33.7 4.1 %copy-start.6 = (f32[256]{0:T(256)S(1)}, f32[256]{0:T(256)}, u32[]{:S(2)}) copy-start(f32[256]{0:T(256)} %param.9) | copy-start | bytes 3076
  44.1 1.4 %collective-permute-start.8 = (f32[144,256]{1,0:T(8,128)S(1)}, f32[144,256]{1,0:T(8,128)S(1)}, u32[]{:S(2)}, u32[]{:S(2)}) collective-permute-start(f32[144,256]{1,0:T(8,128)S(1)} %get-tuple-element.64), channel_id=1, source_target_pairs={{0,1},{1,0},{2,3},{3,2},{4,5},{5,4},{6,7},{7,6},{8,9},{9,8},{10,11... | collective-permute-start | bytes 442376 | tf_op jit(solution)/shard_map/ppermute | solution.py:495
  46.1 7.0 %collective-permute-start.11 = (f32[144,256]{1,0:T(8,128)S(1)}, f32[144,256]{1,0:T(8,128)S(1)}, u32[]{:S(2)}, u32[]{:S(2)}) collective-permute-start(f32[144,256]{1,0:T(8,128)S(1)} %get-tuple-element.65.refs_6_.refs_0_), channel_id=1, source_target_pairs={{0,8},{8,0},{16,24},{24,16},{1,9},{9,1},{17,25},{25,17},{2,10},{10... | collective-permute-start | bytes 442376 | tf_op jit(solution)/shard_map/ppermute | solution.py:505
  51.2 1.3 %collective-permute-start.9 = (f32[40,256]{1,0:T(8,128)S(1)}, f32[40,256]{1,0:T(8,128)S(1)}, u32[]{:S(2)}, u32[]{:S(2)}) collective-permute-start(f32[40,256]{1,0:T(8,128)S(1)} %get-tuple-element.67.refs_0_), channel_id=1, source_target_pairs={{0,1},{1,0},{2,3},{3,2},{4,5},{5,4},{6,7},{7,6},{8,9},{9,8},{10,11... | collective-permute-start | bytes 122888 | tf_op jit(solution)/shard_map/ppermute | solution.py:507
  53.1 10.7 %collective-permute-start.14 = (f32[144,256]{1,0:T(8,128)S(1)}, f32[144,256]{1,0:T(8,128)S(1)}, u32[]{:S(2)}, u32[]{:S(2)}) collective-permute-start(f32[144,256]{1,0:T(8,128)S(1)} %get-tuple-element.72.refs_0_), channel_id=1, source_target_pairs={{0,16},{8,24},{16,0},{24,8},{1,17},{9,25},{17,1},{25,9},{2,18},{10... | collective-permute-start | bytes 442376 | tf_op jit(solution)/shard_map/ppermute | solution.py:511
  54.6 4.0 %collective-permute-start.10 = (f32[40,256]{1,0:T(8,128)S(1)}, f32[40,256]{1,0:T(8,128)S(1)}, u32[]{:S(2)}, u32[]{:S(2)}) collective-permute-start(f32[40,256]{1,0:T(8,128)S(1)} %get-tuple-element.68.refs_2_.refs_0_), channel_id=1, source_target_pairs={{0,2},{1,3},{2,0},{3,1},{4,6},{5,7},{6,4},{7,5},{8,10},{9,11},{10,... | collective-permute-start | bytes 122888 | tf_op jit(solution)/shard_map/ppermute | solution.py:507
  59.2 4.0 %collective-permute-start.12 = (f32[40,256]{1,0:T(8,128)S(1)}, f32[40,256]{1,0:T(8,128)S(1)}, u32[]{:S(2)}, u32[]{:S(2)}) collective-permute-start(f32[40,256]{1,0:T(8,128)S(1)} %get-tuple-element.70.refs_0_), channel_id=1, source_target_pairs={{0,4},{4,0},{1,5},{5,1},{2,6},{6,2},{3,7},{7,3},{8,12},{12,8},{9,1... | collective-permute-start | bytes 122888 | tf_op jit(solution)/shard_map/ppermute | solution.py:507
  63.8 6.2 %collective-permute-start.16 = (f32[144,256]{1,0:T(8,128)S(1)}, f32[144,256]{1,0:T(8,128)S(1)}, u32[]{:S(2)}, u32[]{:S(2)}) collective-permute-start(f32[144,256]{1,0:T(8,128)S(1)} %get-tuple-element.75.refs_0_), channel_id=1, source_target_pairs={{0,2},{1,3},{2,0},{3,1},{4,6},{5,7},{6,4},{7,5},{8,10},{9,11},{10,... | collective-permute-start | bytes 442376 | tf_op jit(solution)/shard_map/ppermute | solution.py:511
  65.4 4.0 %collective-permute-start.13 = (f32[40,256]{1,0:T(8,128)S(1)}, f32[40,256]{1,0:T(8,128)S(1)}, u32[]{:S(2)}, u32[]{:S(2)}) collective-permute-start(f32[40,256]{1,0:T(8,128)S(1)} %get-tuple-element.71.refs_2_.refs_0_), channel_id=1, source_target_pairs={{0,8},{8,0},{16,24},{24,16},{1,9},{9,1},{17,25},{25,17},{2,10},{10... | collective-permute-start | bytes 122888 | tf_op jit(solution)/shard_map/ppermute | solution.py:507
  70.0 7.5 %collective-permute-start.17 = (f32[144,256]{1,0:T(8,128)S(1)}, f32[144,256]{1,0:T(8,128)S(1)}, u32[]{:S(2)}, u32[]{:S(2)}) collective-permute-start(f32[144,256]{1,0:T(8,128)S(1)} %get-tuple-element.81.refs_0_), channel_id=1, source_target_pairs={{0,4},{4,0},{1,5},{5,1},{2,6},{6,2},{3,7},{7,3},{8,12},{12,8},{9,1... | collective-permute-start | bytes 442376 | tf_op jit(solution)/shard_map/ppermute | solution.py:511
  71.6 5.3 %collective-permute-start.15 = (f32[40,256]{1,0:T(8,128)S(1)}, f32[40,256]{1,0:T(8,128)S(1)}, u32[]{:S(2)}, u32[]{:S(2)}) collective-permute-start(f32[40,256]{1,0:T(8,128)S(1)} %get-tuple-element.74.refs_2_.refs_3_.refs_0_), channel_id=1, source_target_pairs={{0,16},{8,24},{16,0},{24,8},{1,17},{9,25},{17,1},{25,9},{2,18},{10... | collective-permute-start | bytes 122888 | tf_op jit(solution)/shard_map/ppermute | solution.py:507
  78.1 4.3 %collective-permute-start.18 = (f32[144,256]{1,0:T(8,128)S(1)}, f32[144,256]{1,0:T(8,128)S(1)}, u32[]{:S(2)}, u32[]{:S(2)}) collective-permute-start(f32[144,256]{1,0:T(8,128)S(1)} %get-tuple-element.82.refs_5_.refs_0_), channel_id=1, source_target_pairs={{0,1},{1,0},{2,3},{3,2},{4,5},{5,4},{6,7},{7,6},{8,9},{9,8},{10,11... | collective-permute-start | bytes 442376 | tf_op jit(solution)/shard_map/ppermute | solution.py:528

commit v6 on v4

--- a/solution.py
+++ b/solution.py
@@ -154,19 +154,39 @@
     return dot(jnp.concatenate(bands, axis=1), jnp.concatenate(weights, axis=0))
 
 
-def pack_kernel(up_ref, left_ref, right_ref, odd_ref, first_ref, second_ref, token_ref):
+def pick(odd, first, second):
+    return jnp.where(odd, first.astype(F32), second.astype(F32)).astype(BF16)
+
+
+def pack_kernel(up_ref, odd_row_ref, odd_column_ref, first_ref, second_ref, early_ref, late_ref, token_ref):
     rows, width = up_ref.shape[0], up_ref.shape[1]
     d = DILATION_RATE
-    odd = odd_ref[0:1] > 0.5
+    odd_row, odd_column = odd_row_ref[0:1] > 0.5, odd_column_ref[0:1] > 0.5
     for r in range(d):
-        for begin, size, ref in ((0, width, up_ref), (width, 8, left_ref), (width + 8, 8, right_ref)):
-            top, bottom = ref[r].astype(F32), ref[rows - d + r].astype(F32)
-            first_ref[r, begin : begin + size] = jnp.where(odd, top, bottom).astype(BF16)
-            second_ref[r, begin : begin + size] = jnp.where(odd, bottom, top).astype(BF16)
+        top, bottom = up_ref[r], up_ref[rows - d + r]
+        first_ref[r] = pick(odd_row, top, bottom)
+        second_ref[r] = pick(odd_row, bottom, top)
+    for r in range(rows):
+        left, right = up_ref[r, :8], up_ref[r, width - 8 :]
+        early_ref[r] = pick(odd_column, left, right)
+        late_ref[r] = pick(odd_column, right, left)
     leave(token_ref)
 
 
-def bands_kernel(up_ref, left_ref, right_ref, w_ref, moved_ref, weight_ref, token_ref, bands_ref):
+def rim_kernel(first_ref, second_ref, odd_row_ref, odd_column_ref, early_ref, late_ref, token_ref):
+    d, width = first_ref.shape[0], first_ref.shape[1]
+    odd_row, odd_column = odd_row_ref[0:1] > 0.5, odd_column_ref[0:1] > 0.5
+    for r in range(d):
+        first = [first_ref[r, :8], first_ref[r, width - 8 :]]
+        second = [second_ref[r, :8], second_ref[r, width - 8 :]]
+        for place, one, two in ((r, first, second), (d + r, second, first)):
+            left, right = pick(odd_row, one[0], two[0]), pick(odd_row, one[1], two[1])
+            early_ref[place] = pick(odd_column, left, right)
+            late_ref[place] = pick(odd_column, right, left)
+    leave(token_ref)
+
+
+def bands_kernel(up_ref, early_ref, late_ref, odd_column_ref, w_ref, moved_ref, weight_ref, token_ref, bands_ref):
     rows = up_ref.shape[0]
     same = same_group()
     for tap in range(9):
@@ -174,7 +194,9 @@
         weight_ref[tap] = jnp.where(same, tile, 0.0).T.astype(BF16)
 
     def inner(r, carry):
-        shift_band(moved_ref, bands_ref, r, up_ref[r], left_ref[r], right_ref[r])
+        early, late = early_ref[r], late_ref[r]
+        odd = odd_column_ref[0:1] > 0.5
+        shift_band(moved_ref, bands_ref, r, up_ref[r], pick(odd, early, late), pick(odd, late, early))
         return carry
 
     lax.fori_loop(0, rows, inner, 0)
@@ -194,18 +216,20 @@
     leave(token_ref)
 
 
-def far_kernel(odd_ref, first_ref, second_ref, weight_ref, near_ref, moved_ref, out_ref, token_ref, bands_ref):
+def far_kernel(
+    odd_row_ref, odd_column_ref, first_ref, second_ref, early_ref, late_ref, weight_ref, near_ref,
+    moved_ref, out_ref, token_ref, bands_ref,
+):
     rows, width = out_ref.shape[0], out_ref.shape[1]
     d = DILATION_RATE
 
     def outer(r, carry):
-        odd = odd_ref[0:1] > 0.5
-        first, second = first_ref[r].astype(F32), second_ref[r].astype(F32)
-        for begin, halo in ((0, jnp.where(odd, first, second)), (d, jnp.where(odd, second, first))):
-            halo = halo.astype(BF16)
-            shift_band(
-                moved_ref, bands_ref, begin + r, halo[0:width], halo[width : width + 8], halo[width + 8 :]
-            )
+        odd_row, odd_column = odd_row_ref[0:1] > 0.5, odd_column_ref[0:1] > 0.5
+        first, second = first_ref[r], second_ref[r]
+        for begin, halo in ((0, pick(odd_row, first, second)), (d, pick(odd_row, second, first))):
+            early, late = early_ref[begin + r], late_ref[begin + r]
+            left, right = pick(odd_column, early, late), pick(odd_column, late, early)
+            shift_band(moved_ref, bands_ref, begin + r, halo, left, right)
         return carry
 
     lax.fori_loop(0, d, outer, 0)
@@ -424,16 +448,15 @@
     held = pltpu.VMEM
     cells = (rows, width, C)
 
-    odd = lax.axis_index("cols") % 2 == 1
-    first, second = up[:, :8], up[:, -8:]
-    first, second = swap(jnp.where(odd, first, second), jnp.where(odd, second, first), "cols")
-    left, right = jnp.where(odd, first, second), jnp.where(odd, second, first)
-    odd_line = jnp.broadcast_to((lax.axis_index("rows") % 2 == 1).astype(F32), (8, C))
+    odd_line = lambda axis: jnp.broadcast_to((lax.axis_index(axis) % 2 == 1).astype(F32), (8, C))
     tap_axis, tap_pairs = stage_pairs[0]
-    later_line = jnp.broadcast_to((lax.axis_index(tap_axis) % 2 == 1).astype(F32), (8, C))
-    halo = shape((d, width + 16, C), BF16)
-    first, second, token = run(pack_kernel, (halo, halo, TOKEN), (up, left, right, odd_line), after=(later_line,))
+    odd_column, odd_row, later_line = odd_line("cols"), odd_line("rows"), odd_line(tap_axis)
+    edge, halo, rim = (shape((size[0], size[1], C), BF16) for size in ((rows, 8), (d, width), (2 * d, 8)))
+    first, second, early, late, token = run(
+        pack_kernel, (halo, halo, edge, edge, TOKEN), (up, odd_row, odd_column), after=(later_line,)
+    )
     first, second = swap(first, second, "rows")
+    early, late = swap(early, late, "cols")
     stats = run(stats_kernel, shape((2 * GS + 8, C), F32), (x,), after=(token,))
     scratch = (pltpu.VMEM((width + 32, C), F32),)
     for number, (axis, pairs) in enumerate(stage_pairs):
@@ -443,19 +466,20 @@
             near_bands, weights, *token = run(
                 bands_kernel,
                 (held((3,) + cells, BF16), held((9, C, C), BF16), TOKEN),
-                (up, left, right, conv_weight.reshape(9, GS, C)),
+                (up, early, late, odd_column, conv_weight.reshape(9, GS, C)),
                 scratch=scratch,
                 after=(stats,),
             )
         if number == count - 2:
-            near_grad, *token = run(
-                near_kernel, (held(cells, F32), TOKEN), (near_bands, weights), after=(stats,)
-            )
+            near_grad, tag = run(near_kernel, (held(cells, F32), TOKEN), (near_bands, weights), after=(stats,))
+            rims = run(rim_kernel, (rim, rim, TOKEN), (first, second, odd_row, odd_column), after=(tag,))
+            token = (rims[2],)
+            rims = swap(rims[0], rims[1], "cols")
         if number == count - 1:
             far_bands, act_grad, *token = run(
                 far_kernel,
                 (held((3, 2 * d, width, C), BF16), held(cells, F32), TOKEN),
-                (odd_line, first, second, weights, near_grad),
+                (odd_row, odd_column, first, second, *rims, weights, near_grad),
                 scratch=scratch,
                 after=(stats,),
             )

time: 78.6 us -> 81.9 us (1.042)
  waiting for transfers between devices: 21.8 us -> 26.8 us
  starting transfers between devices: 27.5 us -> 23.6 us
  local copies, waits for them, and re-layouts: 1.25 us -> 3.39 us
  Pallas kernels: 25.9 us -> 26.8 us
  other arithmetic: 0.92 us -> 0.05 us
    ppermute x3 -> x4, waiting for transfers between devices: 1.9 us -> 6.71 us  [swap(): lax.ppermute(part, axis, pairs)]
    ppermute x5, waiting for transfers between devices: 6.65 us -> 4.12 us  [shards(): other = lax.ppermute(stats, axis, pairs)]
    unnamed x12 -> x14, local copies, waits for them, and re-layouts: 1.24 us -> 3.37 us
    ppermute x5, starting transfers between devices: 6.24 us -> 4.3 us  [shards(): other = lax.ppermute(sums, *stage)]
    ppermute x5, waiting for transfers between devices: 11.1 us -> 13 us  [shards(): other = lax.ppermute(sums, *stage)]
    pallas_call x21 -> x22, Pallas kernels: 25.9 us -> 26.8 us  [run(): pl.pallas_call(kernel, out_shape=out_shapes, in_specs=[VMEM_SPEC] * count...]
    select_n x2 -> x0, other arithmetic: 0.88 us -> none  [the longest x1 0.87 us: shards(): jnp.where(odd, first, second)]
    ppermute x3 -> x4, starting transfers between devices: 5.81 us -> 5.02 us  [swap(): lax.ppermute(part, axis, pairs)]
  transfers between devices with their start and end apart: 19 -> 20, of which waited for: 12 -> 11; matrix products, arithmetic and copies ran while one was open for 0% -> 0% of each run, Pallas kernels for 23% -> 23%
where the time goes in v6:
time: 81.9 us; the launch traced here: 81.6 us
  Pallas kernels  26.8 us (33%)
  waiting for transfers between devices  26.8 us (33%)
  starting transfers between devices  23.6 us (29%)
  local copies, waits for them, and re-layouts  3.39 us (4%)
  between operations  0.97 us (1%)
    pallas_call x22, Pallas kernels, run(): pl.pallas_call(kernel, out_shape=out_shapes, in_specs=[VMEM_SPEC] * count...  26.8 us
    ppermute x5, waiting for transfers between devices, shards(): other = lax.ppermute(sums, *stage)  13 us
    ppermute x5, starting transfers between devices, shards(): other = lax.ppermute(stats, axis, pairs)  8.25 us
    ppermute x4, waiting for transfers between devices, swap(): lax.ppermute(part, axis, pairs)  6.71 us
    ppermute x4, starting transfers between devices, swap(): lax.ppermute(part, axis, pairs)  5.02 us
    ppermute x3, starting transfers between devices, shards(): half = add(half, lax.ppermute(half, *tap_stages[number - 1]), after=(sums,))  4.85 us
    ppermute x5, starting transfers between devices, shards(): other = lax.ppermute(sums, *stage)  4.3 us
    ppermute x5, waiting for transfers between devices, shards(): other = lax.ppermute(stats, axis, pairs)  4.12 us
  transfers between devices with their start and end apart: 20, of which 11 were waited for; matrix products, arithmetic and copies ran while one was open for 0% of the time, Pallas kernels for 23%

profile of v6, /device:TPU:0, one launch (start us, length us, event | category | flops | bytes accessed | tf_op | source)
XLA Modules:
  0.0 81.6 jit_solution(11524265296770045945)
XLA Ops:
  0.7 0.0 copy-start.2
  0.7 1.2 %copy-done.2 = bf16[1,8,256,256]{3,2,1,0:T(8,128)(2,1)S(1)} copy-done((bf16[1,8,256,256]{3,2,1,0:T(8,128)(2,1)S(1)}, bf16[1,8,256,256]{3,2,1,0:T(8,128)(2,1)}, u32[]{:S(2)}) %copy-start.2) | copy-done | bytes 1048600
  1.9 0.6 shard_map.84
  2.6 3.0 %collective-permute-start = (bf16[6,256,256]{2,1,0:T(8,128)(2,1)S(1)}, bf16[6,256,256]{2,1,0:T(8,128)(2,1)S(1)}, u32[]{:S(2)}, u32[]{:S(2)}) collective-permute-start(bf16[6,256,256]{2,1,0:T(8,128)(2,1)S(1)} %get-tuple-element.32), channel_id=1, source_target_pairs={{0,8},{16,24},{8,0},{24,16},{1,9},{17,25},{9,1},{25,17},{2,10},{18... | collective-permute-start | bytes 2359304 | tf_op jit(solution)/shard_map/ppermute | solution.py:430
  5.6 0.7 collective-permute-start.1
  6.3 0.0 copy-start
  6.3 1.2 %copy-done = bf16[1,8,256,256]{3,2,1,0:T(8,128)(2,1)S(1)} copy-done((bf16[1,8,256,256]{3,2,1,0:T(8,128)(2,1)S(1)}, bf16[1,8,256,256]{3,2,1,0:T(8,128)(2,1)}, u32[]{:S(2)}) %copy-start) | copy-done | bytes 1048600
  7.5 3.0 %shard_map.85.refs_0_ = f32[72,256]{1,0:T(8,128)S(1)} custom-call(bf16[8,256,256]{2,1,0:T(8,128)(2,1)S(1)} %bitcast.5, f32[8,128]{1,0:T(8,128)S(1)} %get-tuple-element.35.refs_1_), custom_call_target="tpu_custom_call" | custom-call | tf_op jit(solution)/shard_map/pallas_call | solution.py:31
  10.5 0.1 collective-permute-start.3
  10.6 1.3 %collective-permute-done.3.refs_1_ = f32[72,256]{1,0:T(8,128)S(1)} collective-permute-done((f32[72,256]{1,0:T(8,128)S(1)}, f32[72,256]{1,0:T(8,128)S(1)}, u32[]{:S(2)}, u32[]{:S(2)}) %collective-permute-start.3) | collective-permute-done | bytes 73760 | tf_op jit(solution)/shard_map/ppermute | solution.py:463
  11.9 1.6 %collective-permute-start.4 = (f32[72,256]{1,0:T(8,128)S(1)}, f32[72,256]{1,0:T(8,128)S(1)}, u32[]{:S(2)}, u32[]{:S(2)}) collective-permute-start(f32[72,256]{1,0:T(8,128)S(1)} %shard_map.86.refs_0_), channel_id=1, source_target_pairs={{0,2},{1,3},{2,0},{3,1},{4,6},{5,7},{6,4},{7,5},{8,10},{9,11},{10,... | collective-permute-start | bytes 221192 | tf_op jit(solution)/shard_map/ppermute | solution.py:463
  13.4 2.9 %collective-permute-done.4.refs_1_ = f32[72,256]{1,0:T(8,128)S(1)} collective-permute-done((f32[72,256]{1,0:T(8,128)S(1)}, f32[72,256]{1,0:T(8,128)S(1)}, u32[]{:S(2)}, u32[]{:S(2)}) %collective-permute-start.4) | collective-permute-done | bytes 73760 | tf_op jit(solution)/shard_map/ppermute | solution.py:463
  16.3 1.6 %collective-permute-start.5 = (f32[72,256]{1,0:T(8,128)S(1)}, f32[72,256]{1,0:T(8,128)S(1)}, u32[]{:S(2)}, u32[]{:S(2)}) collective-permute-start(f32[72,256]{1,0:T(8,128)S(1)} %shard_map.87.refs_5_.refs_0_), channel_id=1, source_target_pairs={{0,4},{4,0},{1,5},{5,1},{2,6},{6,2},{3,7},{7,3},{8,12},{12,8},{9,1... | collective-permute-start | bytes 221192 | tf_op jit(solution)/shard_map/ppermute | solution.py:463
  17.9 0.5 collective-permute-start.2
  18.4 3.4 %collective-permute-done.2.refs_1_ = bf16[8,8,256]{2,1,0:T(8,128)(2,1)S(1)} collective-permute-done((bf16[8,8,256]{2,1,0:T(8,128)(2,1)S(1)}, bf16[8,8,256]{2,1,0:T(8,128)(2,1)S(1)}, u32[]{:S(2)}, u32[]{:S(2)}) %collective-permute-start.2) | collective-permute-done | bytes 32800 | tf_op jit(solution)/shard_map/ppermute | solution.py:430
  21.8 0.9 %copy-done.4 = bf16[3,3,32,256]{3,2,1,0:T(8,128)(2,1)S(1)} copy-done((bf16[3,3,32,256]{3,2,1,0:T(8,128)(2,1)S(1)}, bf16[3,3,32,256]{3,2,1,0:T(8,128)(2,1)}, u32[]{:S(2)}) %copy-start.4) | copy-done | bytes 147480
  22.7 0.8 shard_map.88
  23.6 4.4 %collective-permute-start.7 = (f32[72,256]{1,0:T(8,128)S(1)}, f32[72,256]{1,0:T(8,128)S(1)}, u32[]{:S(2)}, u32[]{:S(2)}) collective-permute-start(f32[72,256]{1,0:T(8,128)S(1)} %shard_map.89.refs_2_.refs_0_), channel_id=1, source_target_pairs={{0,8},{8,0},{16,24},{24,16},{1,9},{9,1},{17,25},{25,17},{2,10},{10... | collective-permute-start | bytes 221192 | tf_op jit(solution)/shard_map/ppermute | solution.py:463
  28.0 2.6 %shard_map.90 = (f32[8,256,256]{2,1,0:T(8,128)S(1)}, f32[8,128]{1,0:T(8,128)S(1)}) custom-call(bf16[3,8,256,256]{3,2,1,0:T(8,128)(2,1)S(1)} %get-tuple-element.36.refs_0_.refs_1_, bf16[9,256,256]{2,1,0:T(8,128)(2,1)S(1)} %get-tuple-element.37.refs_1_.refs_6_, f32[72,256]{1,0:T(8,128)S(1)} %shard_map.89.refs_2_.refs_0_), custom_call_target="tpu_custom_call" | custom-call | tf_op jit(solution)/shard_map/pallas_call | solution.py:31
  30.6 0.6 shard_map.91
  31.2 0.6 collective-permute-start.8
  31.9 0.8 collective-permute-start.6
  32.6 3.3 %collective-permute-done.6.refs_4_ = bf16[12,8,256]{2,1,0:T(8,128)(2,1)S(1)} collective-permute-done((bf16[12,8,256]{2,1,0:T(8,128)(2,1)S(1)}, bf16[12,8,256]{2,1,0:T(8,128)(2,1)S(1)}, u32[]{:S(2)}, u32[]{:S(2)}) %collective-permute-start.6) | collective-permute-done | bytes 49184 | tf_op jit(solution)/shard_map/ppermute | solution.py:430
  36.0 0.0 copy-start.6
  36.0 3.5 %shard_map.93 = (bf16[3,12,256,256]{3,2,1,0:T(8,128)(2,1)S(1)}, f32[8,256,256]{2,1,0:T(8,128)S(1)}, f32[8,128]{1,0:T(8,128)S(1)}) custom-call(f32[8,256]{1,0:T(8,128)S(1)} %broadcast_in_dim.27.refs_1_.refs_2_.refs_0_, f32[8,256]{1,0:T(8,128)S(1)} %broadcast_in_dim.28.refs_2_.refs_3_.refs_1_, bf16[6,256,256]{2,1,0:T(8,128)(2,1)S(1)} %collective-permute-done.refs_0_.refs_2_, ...), custom_call_target="tpu_custom_call" | custom-call | tf_op jit(solution)/shard_map/pallas_call | solution.py:31
  39.6 3.3 %shard_map.95 = (bf16[256,2048]{1,0:T(8,128)(2,1)S(1)}, f32[8,256,256]{2,1,0:T(8,128)S(1)}, f32[5,3,32,256]{3,2,1,0:T(8,128)S(1)}, f32[8,256]{1,0:T(8,128)S(1)}) custom-call(bf16[8,256,256]{2,1,0:T(8,128)(2,1)S(1)} %bitcast.6, f32[72,256]{1,0:T(8,128)S(1)} %shard_map.94.refs_1_, f32[8,256]{1,0:T(8,128)S(1)} %broadcast_in_dim.32.refs_2_.refs_5_, ...), custom_call_target="tpu_custom_call" | custom-call | tf_op jit(solution)/shard_map/pallas_call | solution.py:31
  42.9 3.0 %shard_map.96 = (f32[144,256]{1,0:T(8,128)S(1)}, f32[144,256]{1,0:T(8,128)S(1)}) custom-call(bf16[256,2048]{1,0:T(8,128)(2,1)S(1)} %get-tuple-element.48.refs_0_, bf16[3,8,256,256]{3,2,1,0:T(8,128)(2,1)S(1)} %get-tuple-element.36.refs_0_.refs_1_, bf16[3,12,256,256]{3,2,1,0:T(8,128)(2,1)S(1)} %get-tuple-element.49.refs_2_, ...), custom_call_target="tpu_custom_call" | custom-call | tf_op jit(solution)/shard_map/pallas_call | solution.py:31
  45.9 0.1 collective-permute-start.9
  46.0 1.4 %collective-permute-done.9 = f32[144,256]{1,0:T(8,128)S(1)} collective-permute-done((f32[144,256]{1,0:T(8,128)S(1)}, f32[144,256]{1,0:T(8,128)S(1)}, u32[]{:S(2)}, u32[]{:S(2)}) %collective-permute-start.9) | collective-permute-done | bytes 147488 | tf_op jit(solution)/shard_map/ppermute | solution.py:505
  47.4 1.0 %collective-permute-start.15 = (f32[144,256]{1,0:T(8,128)S(1)}, f32[144,256]{1,0:T(8,128)S(1)}, u32[]{:S(2)}, u32[]{:S(2)}) collective-permute-start(f32[144,256]{1,0:T(8,128)S(1)} %add.28.refs_6_.refs_0_), channel_id=1, source_target_pairs={{0,8},{8,0},{16,24},{24,16},{1,9},{9,1},{17,25},{25,17},{2,10},{10... | collective-permute-start | bytes 442376 | tf_op jit(solution)/shard_map/ppermute | solution.py:515
  48.4 3.3 %shard_map.97 = (f32[8,256,256]{2,1,0:T(8,128)S(1)}, f32[40,256]{1,0:T(8,128)S(1)}) custom-call(bf16[8,256,256]{2,1,0:T(8,128)(2,1)S(1)} %bitcast.7, f32[8,256,256]{2,1,0:T(8,128)S(1)} %get-tuple-element.43.refs_1_, f32[8,256,256]{2,1,0:T(8,128)S(1)} %get-tuple-element.45.refs_2_, f32[5,3,32,256]{3,2,1,0:T(8,128)S(1)} %get-tuple-element.46.refs_3_.refs_0_, ...), custom_call_target="tpu_custom_call" | custom-call | tf_op jit(solution)/shard_map/pallas_call | solution.py:31
  51.8 1.6 %collective-permute-done.15.refs_1_ = f32[144,256]{1,0:T(8,128)S(1)} collective-permute-done((f32[144,256]{1,0:T(8,128)S(1)}, f32[144,256]{1,0:T(8,128)S(1)}, u32[]{:S(2)}, u32[]{:S(2)}) %collective-permute-start.15) | collective-permute-done | bytes 147488 | tf_op jit(solution)/shard_map/ppermute | solution.py:515
  53.4 2.4 %collective-permute-start.16 = (f32[144,256]{1,0:T(8,128)S(1)}, f32[144,256]{1,0:T(8,128)S(1)}, u32[]{:S(2)}, u32[]{:S(2)}) collective-permute-start(f32[144,256]{1,0:T(8,128)S(1)} %shard_map.100.refs_0_), channel_id=1, source_target_pairs={{0,16},{8,24},{16,0},{24,8},{1,17},{9,25},{17,1},{25,9},{2,18},{10... | collective-permute-start | bytes 442376 | tf_op jit(solution)/shard_map/ppermute | solution.py:528
  55.8 1.2 %collective-permute-done.10 = f32[40,256]{1,0:T(8,128)S(1)} collective-permute-done((f32[40,256]{1,0:T(8,128)S(1)}, f32[40,256]{1,0:T(8,128)S(1)}, u32[]{:S(2)}, u32[]{:S(2)}) %collective-permute-start.10) | collective-permute-done | bytes 40992 | tf_op jit(solution)/shard_map/ppermute | solution.py:517
  57.0 1.5 %collective-permute-start.11 = (f32[40,256]{1,0:T(8,128)S(1)}, f32[40,256]{1,0:T(8,128)S(1)}, u32[]{:S(2)}, u32[]{:S(2)}) collective-permute-start(f32[40,256]{1,0:T(8,128)S(1)} %add.29), channel_id=1, source_target_pairs={{0,2},{1,3},{2,0},{3,1},{4,6},{5,7},{6,4},{7,5},{8,10},{9,11},{10,... | collective-permute-start | bytes 122888 | tf_op jit(solution)/shard_map/ppermute | solution.py:517
  58.5 2.5 %collective-permute-done.11 = f32[40,256]{1,0:T(8,128)S(1)} collective-permute-done((f32[40,256]{1,0:T(8,128)S(1)}, f32[40,256]{1,0:T(8,128)S(1)}, u32[]{:S(2)}, u32[]{:S(2)}) %collective-permute-start.11) | collective-permute-done | bytes 40992 | tf_op jit(solution)/shard_map/ppermute | solution.py:517
  61.0 0.8 collective-permute-start.12
  61.8 3.2 %collective-permute-done.12 = f32[40,256]{1,0:T(8,128)S(1)} collective-permute-done((f32[40,256]{1,0:T(8,128)S(1)}, f32[40,256]{1,0:T(8,128)S(1)}, u32[]{:S(2)}, u32[]{:S(2)}) %collective-permute-start.12) | collective-permute-done | bytes 40992 | tf_op jit(solution)/shard_map/ppermute | solution.py:517
  65.1 1.6 %collective-permute-start.17 = (f32[144,256]{1,0:T(8,128)S(1)}, f32[144,256]{1,0:T(8,128)S(1)}, u32[]{:S(2)}, u32[]{:S(2)}) collective-permute-start(f32[144,256]{1,0:T(8,128)S(1)} %shard_map.101.refs_0_), channel_id=1, source_target_pairs={{0,2},{1,3},{2,0},{3,1},{4,6},{5,7},{6,4},{7,5},{8,10},{9,11},{10,... | collective-permute-start | bytes 442376 | tf_op jit(solution)/shard_map/ppermute | solution.py:528
  66.6 1.4 %collective-permute-start.13 = (f32[40,256]{1,0:T(8,128)S(1)}, f32[40,256]{1,0:T(8,128)S(1)}, u32[]{:S(2)}, u32[]{:S(2)}) collective-permute-start(f32[40,256]{1,0:T(8,128)S(1)} %add.31.refs_2_), channel_id=1, source_target_pairs={{0,8},{8,0},{16,24},{24,16},{1,9},{9,1},{17,25},{25,17},{2,10},{10... | collective-permute-start | bytes 122888 | tf_op jit(solution)/shard_map/ppermute | solution.py:517
  68.1 2.6 %collective-permute-done.13 = f32[40,256]{1,0:T(8,128)S(1)} collective-permute-done((f32[40,256]{1,0:T(8,128)S(1)}, f32[40,256]{1,0:T(8,128)S(1)}, u32[]{:S(2)}, u32[]{:S(2)}) %collective-permute-start.13) | collective-permute-done | bytes 40992 | tf_op jit(solution)/shard_map/ppermute | solution.py:517
  70.7 0.9 %collective-permute-start.18 = (f32[144,256]{1,0:T(8,128)S(1)}, f32[144,256]{1,0:T(8,128)S(1)}, u32[]{:S(2)}, u32[]{:S(2)}) collective-permute-start(f32[144,256]{1,0:T(8,128)S(1)} %shard_map.102.refs_0_), channel_id=1, source_target_pairs={{0,4},{4,0},{1,5},{5,1},{2,6},{6,2},{3,7},{7,3},{8,12},{12,8},{9,1... | collective-permute-start | bytes 442376 | tf_op jit(solution)/shard_map/ppermute | solution.py:528
  71.5 0.6 collective-permute-start.14
  72.1 0.8 shard_map.98
  72.9 3.6 %collective-permute-done.14.refs_1_ = f32[40,256]{1,0:T(8,128)S(1)} collective-permute-done((f32[40,256]{1,0:T(8,128)S(1)}, f32[40,256]{1,0:T(8,128)S(1)}, u32[]{:S(2)}, u32[]{:S(2)}) %collective-permute-start.14) | collective-permute-done | bytes 40992 | tf_op jit(solution)/shard_map/ppermute | solution.py:517
  76.5 0.1 collective-permute-start.19
  76.6 4.3 %shard_map.104 = (bf16[8,256,256]{2,1,0:T(8,128)(2,1)}, f32[256]{0:T(256)}, f32[256]{0:T(256)}) custom-call(bf16[8,256,256]{2,1,0:T(8,128)(2,1)S(1)} %bitcast.8, f32[8,256,256]{2,1,0:T(8,128)S(1)} %get-tuple-element.52.refs_1_, f32[40,256]{1,0:T(8,128)S(1)} %shard_map.99.refs_2_, bf16[9,2,256,256]{3,2,1,0:T(8,128)(2,1)S(1)} %get-tuple-element.55.refs_3_, ...), custom_call_target="tpu_custom_call" | custom-call | tf_op jit(solution)/shard_map/pallas_call | solution.py:31
  80.9 0.8 shard_map.105
  (40 shorter events, 0.3 us)
Async XLA Ops:
  0.7 1.2 %copy-start.2 = (bf16[1,8,256,256]{3,2,1,0:T(8,128)(2,1)S(1)}, bf16[1,8,256,256]{3,2,1,0:T(8,128)(2,1)}, u32[]{:S(2)}) copy-start(bf16[1,8,256,256]{3,2,1,0:T(8,128)(2,1)} %param.6) | copy-start | bytes 3145732
  1.9 19.9 %copy-start.3 = (bf16[1,8,256,256]{3,2,1,0:T(8,128)(2,1)S(1)}, bf16[1,8,256,256]{3,2,1,0:T(8,128)(2,1)}, u32[]{:S(2)}) copy-start(bf16[1,8,256,256]{3,2,1,0:T(8,128)(2,1)} %param.6) | copy-start | bytes 3145732
  2.6 28.0 %collective-permute-start = (bf16[6,256,256]{2,1,0:T(8,128)(2,1)S(1)}, bf16[6,256,256]{2,1,0:T(8,128)(2,1)S(1)}, u32[]{:S(2)}, u32[]{:S(2)}) collective-permute-start(bf16[6,256,256]{2,1,0:T(8,128)(2,1)S(1)} %get-tuple-element.32), channel_id=1, source_target_pairs={{0,8},{16,24},{8,0},{24,16},{1,9},{17,25},{9,1},{25,17},{2,10},{18... | collective-permute-start | bytes 2359304 | tf_op jit(solution)/shard_map/ppermute | solution.py:430
  5.6 25.0 %collective-permute-start.1 = (bf16[6,256,256]{2,1,0:T(8,128)(2,1)S(1)}, bf16[6,256,256]{2,1,0:T(8,128)(2,1)S(1)}, u32[]{:S(2)}, u32[]{:S(2)}) collective-permute-start(bf16[6,256,256]{2,1,0:T(8,128)(2,1)S(1)} %get-tuple-element.33), channel_id=1, source_target_pairs={{8,16},{16,8},{9,17},{17,9},{10,18},{18,10},{11,19},{19,11},{12,20... | collective-permute-start | bytes 2359304 | tf_op jit(solution)/shard_map/ppermute | solution.py:430
  6.3 1.2 %copy-start = (bf16[1,8,256,256]{3,2,1,0:T(8,128)(2,1)S(1)}, bf16[1,8,256,256]{3,2,1,0:T(8,128)(2,1)}, u32[]{:S(2)}) copy-start(bf16[1,8,256,256]{3,2,1,0:T(8,128)(2,1)} %param.5) | copy-start | bytes 3145732
  10.5 1.3 %collective-permute-start.3 = (f32[72,256]{1,0:T(8,128)S(1)}, f32[72,256]{1,0:T(8,128)S(1)}, u32[]{:S(2)}, u32[]{:S(2)}) collective-permute-start(f32[72,256]{1,0:T(8,128)S(1)} %shard_map.85.refs_0_), channel_id=1, source_target_pairs={{0,1},{1,0},{2,3},{3,2},{4,5},{5,4},{6,7},{7,6},{8,9},{9,8},{10,11... | collective-permute-start | bytes 221192 | tf_op jit(solution)/shard_map/ppermute | solution.py:463
  11.9 4.4 %collective-permute-start.4 = (f32[72,256]{1,0:T(8,128)S(1)}, f32[72,256]{1,0:T(8,128)S(1)}, u32[]{:S(2)}, u32[]{:S(2)}) collective-permute-start(f32[72,256]{1,0:T(8,128)S(1)} %shard_map.86.refs_0_), channel_id=1, source_target_pairs={{0,2},{1,3},{2,0},{3,1},{4,6},{5,7},{6,4},{7,5},{8,10},{9,11},{10,... | collective-permute-start | bytes 221192 | tf_op jit(solution)/shard_map/ppermute | solution.py:463
  16.3 7.2 %collective-permute-start.5 = (f32[72,256]{1,0:T(8,128)S(1)}, f32[72,256]{1,0:T(8,128)S(1)}, u32[]{:S(2)}, u32[]{:S(2)}) collective-permute-start(f32[72,256]{1,0:T(8,128)S(1)} %shard_map.87.refs_5_.refs_0_), channel_id=1, source_target_pairs={{0,4},{4,0},{1,5},{5,1},{2,6},{6,2},{3,7},{7,3},{8,12},{12,8},{9,1... | collective-permute-start | bytes 221192 | tf_op jit(solution)/shard_map/ppermute | solution.py:463
  17.9 3.9 %collective-permute-start.2 = (bf16[8,8,256]{2,1,0:T(8,128)(2,1)S(1)}, bf16[8,8,256]{2,1,0:T(8,128)(2,1)S(1)}, u32[]{:S(2)}, u32[]{:S(2)}) collective-permute-start(bf16[8,8,256]{2,1,0:T(8,128)(2,1)S(1)} %get-tuple-element.34), channel_id=1, source_target_pairs={{0,4},{4,0},{1,5},{5,1},{2,6},{6,2},{3,7},{7,3},{8,12},{12,8},{9,1... | collective-permute-start | bytes 98312 | tf_op jit(solution)/shard_map/ppermute | solution.py:430
  21.8 0.9 %copy-start.4 = (bf16[3,3,32,256]{3,2,1,0:T(8,128)(2,1)S(1)}, bf16[3,3,32,256]{3,2,1,0:T(8,128)(2,1)}, u32[]{:S(2)}) copy-start(bf16[3,3,32,256]{3,2,1,0:T(8,128)(2,1)} %param.7) | copy-start | bytes 442372
  23.6 7.7 %collective-permute-start.7 = (f32[72,256]{1,0:T(8,128)S(1)}, f32[72,256]{1,0:T(8,128)S(1)}, u32[]{:S(2)}, u32[]{:S(2)}) collective-permute-start(f32[72,256]{1,0:T(8,128)S(1)} %shard_map.89.refs_2_.refs_0_), channel_id=1, source_target_pairs={{0,8},{8,0},{16,24},{24,16},{1,9},{9,1},{17,25},{25,17},{2,10},{10... | collective-permute-start | bytes 221192 | tf_op jit(solution)/shard_map/ppermute | solution.py:463
  31.2 8.3 %collective-permute-start.8 = (f32[72,256]{1,0:T(8,128)S(1)}, f32[72,256]{1,0:T(8,128)S(1)}, u32[]{:S(2)}, u32[]{:S(2)}) collective-permute-start(f32[72,256]{1,0:T(8,128)S(1)} %shard_map.92.refs_8_.refs_0_), channel_id=1, source_target_pairs={{0,16},{8,24},{16,0},{24,8},{1,17},{9,25},{17,1},{25,9},{2,18},{10... | collective-permute-start | bytes 221192 | tf_op jit(solution)/shard_map/ppermute | solution.py:463
  31.9 4.1 %collective-permute-start.6 = (bf16[12,8,256]{2,1,0:T(8,128)(2,1)S(1)}, bf16[12,8,256]{2,1,0:T(8,128)(2,1)S(1)}, u32[]{:S(2)}, u32[]{:S(2)}) collective-permute-start(bf16[12,8,256]{2,1,0:T(8,128)(2,1)S(1)} %get-tuple-element.40), channel_id=1, source_target_pairs={{0,4},{4,0},{1,5},{5,1},{2,6},{6,2},{3,7},{7,3},{8,12},{12,8},{9,1... | collective-permute-start | bytes 147464 | tf_op jit(solution)/shard_map/ppermute | solution.py:430
  36.0 3.6 %copy-start.5 = (f32[256]{0:T(256)S(1)}, f32[256]{0:T(256)}, u32[]{:S(2)}) copy-start(f32[256]{0:T(256)} %param.8) | copy-start | bytes 3076
  36.0 3.6 %copy-start.6 = (f32[256]{0:T(256)S(1)}, f32[256]{0:T(256)}, u32[]{:S(2)}) copy-start(f32[256]{0:T(256)} %param.9) | copy-start | bytes 3076
  36.0 3.6 %copy-start.1 = (bf16[1,8,256,256]{3,2,1,0:T(8,128)(2,1)S(1)}, bf16[1,8,256,256]{3,2,1,0:T(8,128)(2,1)}, u32[]{:S(2)}) copy-start(bf16[1,8,256,256]{3,2,1,0:T(8,128)(2,1)} %param.5) | copy-start | bytes 3145732
  45.9 1.4 %collective-permute-start.9 = (f32[144,256]{1,0:T(8,128)S(1)}, f32[144,256]{1,0:T(8,128)S(1)}, u32[]{:S(2)}, u32[]{:S(2)}) collective-permute-start(f32[144,256]{1,0:T(8,128)S(1)} %get-tuple-element.51), channel_id=1, source_target_pairs={{0,1},{1,0},{2,3},{3,2},{4,5},{5,4},{6,7},{7,6},{8,9},{9,8},{10,11... | collective-permute-start | bytes 442376 | tf_op jit(solution)/shard_map/ppermute | solution.py:505
  47.4 6.0 %collective-permute-start.15 = (f32[144,256]{1,0:T(8,128)S(1)}, f32[144,256]{1,0:T(8,128)S(1)}, u32[]{:S(2)}, u32[]{:S(2)}) collective-permute-start(f32[144,256]{1,0:T(8,128)S(1)} %add.28.refs_6_.refs_0_), channel_id=1, source_target_pairs={{0,8},{8,0},{16,24},{24,16},{1,9},{9,1},{17,25},{25,17},{2,10},{10... | collective-permute-start | bytes 442376 | tf_op jit(solution)/shard_map/ppermute | solution.py:515
  53.4 11.7 %collective-permute-start.16 = (f32[144,256]{1,0:T(8,128)S(1)}, f32[144,256]{1,0:T(8,128)S(1)}, u32[]{:S(2)}, u32[]{:S(2)}) collective-permute-start(f32[144,256]{1,0:T(8,128)S(1)} %shard_map.100.refs_0_), channel_id=1, source_target_pairs={{0,16},{8,24},{16,0},{24,8},{1,17},{9,25},{17,1},{25,9},{2,18},{10... | collective-permute-start | bytes 442376 | tf_op jit(solution)/shard_map/ppermute | solution.py:528
  55.8 1.2 %collective-permute-start.10 = (f32[40,256]{1,0:T(8,128)S(1)}, f32[40,256]{1,0:T(8,128)S(1)}, u32[]{:S(2)}, u32[]{:S(2)}) collective-permute-start(f32[40,256]{1,0:T(8,128)S(1)} %get-tuple-element.53.refs_2_), channel_id=1, source_target_pairs={{0,1},{1,0},{2,3},{3,2},{4,5},{5,4},{6,7},{7,6},{8,9},{9,8},{10,11... | collective-permute-start | bytes 122888 | tf_op jit(solution)/shard_map/ppermute | solution.py:517
  57.0 4.0 %collective-permute-start.11 = (f32[40,256]{1,0:T(8,128)S(1)}, f32[40,256]{1,0:T(8,128)S(1)}, u32[]{:S(2)}, u32[]{:S(2)}) collective-permute-start(f32[40,256]{1,0:T(8,128)S(1)} %add.29), channel_id=1, source_target_pairs={{0,2},{1,3},{2,0},{3,1},{4,6},{5,7},{6,4},{7,5},{8,10},{9,11},{10,... | collective-permute-start | bytes 122888 | tf_op jit(solution)/shard_map/ppermute | solution.py:517
  61.0 4.0 %collective-permute-start.12 = (f32[40,256]{1,0:T(8,128)S(1)}, f32[40,256]{1,0:T(8,128)S(1)}, u32[]{:S(2)}, u32[]{:S(2)}) collective-permute-start(f32[40,256]{1,0:T(8,128)S(1)} %add.30), channel_id=1, source_target_pairs={{0,4},{4,0},{1,5},{5,1},{2,6},{6,2},{3,7},{7,3},{8,12},{12,8},{9,1... | collective-permute-start | bytes 122888 | tf_op jit(solution)/shard_map/ppermute | solution.py:517
  65.1 5.6 %collective-permute-start.17 = (f32[144,256]{1,0:T(8,128)S(1)}, f32[144,256]{1,0:T(8,128)S(1)}, u32[]{:S(2)}, u32[]{:S(2)}) collective-permute-start(f32[144,256]{1,0:T(8,128)S(1)} %shard_map.101.refs_0_), channel_id=1, source_target_pairs={{0,2},{1,3},{2,0},{3,1},{4,6},{5,7},{6,4},{7,5},{8,10},{9,11},{10,... | collective-permute-start | bytes 442376 | tf_op jit(solution)/shard_map/ppermute | solution.py:528
  66.6 4.0 %collective-permute-start.13 = (f32[40,256]{1,0:T(8,128)S(1)}, f32[40,256]{1,0:T(8,128)S(1)}, u32[]{:S(2)}, u32[]{:S(2)}) collective-permute-start(f32[40,256]{1,0:T(8,128)S(1)} %add.31.refs_2_), channel_id=1, source_target_pairs={{0,8},{8,0},{16,24},{24,16},{1,9},{9,1},{17,25},{25,17},{2,10},{10... | collective-permute-start | bytes 122888 | tf_op jit(solution)/shard_map/ppermute | solution.py:517
  70.7 5.8 %collective-permute-start.18 = (f32[144,256]{1,0:T(8,128)S(1)}, f32[144,256]{1,0:T(8,128)S(1)}, u32[]{:S(2)}, u32[]{:S(2)}) collective-permute-start(f32[144,256]{1,0:T(8,128)S(1)} %shard_map.102.refs_0_), channel_id=1, source_target_pairs={{0,4},{4,0},{1,5},{5,1},{2,6},{6,2},{3,7},{7,3},{8,12},{12,8},{9,1... | collective-permute-start | bytes 442376 | tf_op jit(solution)/shard_map/ppermute | solution.py:528
  71.5 4.9 %collective-permute-start.14 = (f32[40,256]{1,0:T(8,128)S(1)}, f32[40,256]{1,0:T(8,128)S(1)}, u32[]{:S(2)}, u32[]{:S(2)}) collective-permute-start(f32[40,256]{1,0:T(8,128)S(1)} %add.32.refs_3_.refs_0_.refs_2_), channel_id=1, source_target_pairs={{0,16},{8,24},{16,0},{24,8},{1,17},{9,25},{17,1},{25,9},{2,18},{10... | collective-permute-start | bytes 122888 | tf_op jit(solution)/shard_map/ppermute | solution.py:517
  76.5 4.4 %collective-permute-start.19 = (f32[144,256]{1,0:T(8,128)S(1)}, f32[144,256]{1,0:T(8,128)S(1)}, u32[]{:S(2)}, u32[]{:S(2)}) collective-permute-start(f32[144,256]{1,0:T(8,128)S(1)} %shard_map.103.refs_5_.refs_0_), channel_id=1, source_target_pairs={{0,1},{1,0},{2,3},{3,2},{4,5},{5,4},{6,7},{7,6},{8,9},{9,8},{10,11... | collective-permute-start | bytes 442376 | tf_op jit(solution)/shard_map/ppermute | solution.py:535

commit v7 on v4

--- a/solution.py
+++ b/solution.py
@@ -488,7 +488,7 @@
     )
     row_stages = [stage for stage in stage_pairs[1:] if stage[0] == "rows"]
     tap_stages = row_stages + [stage for stage in stage_pairs[1:] if stage[0] != "rows"]
-    half = add(half, lax.ppermute(half, *tap_stages[0]), after=(sums,))
+    in_flight = lax.ppermute(half, *tap_stages[0])
     for number, stage in enumerate(stage_pairs):
         other = lax.ppermute(sums, *stage)
         token = ()
@@ -500,6 +500,8 @@
                 after=(sums,),
             )
         sums = add(sums, other, after=token)
+        if number == 0:
+            half = add(half, in_flight, after=(sums,))
         if 2 <= number < count:
             half = add(half, lax.ppermute(half, *tap_stages[number - 1]), after=(sums,))
     input_grad, gain_grad, bias_grad = run(

time: 78.6 us -> 78.9 us (level)
  waiting for transfers between devices: 21.8 us -> 23.6 us
  starting transfers between devices: 27.5 us -> 26.1 us
    ppermute x5, waiting for transfers between devices: 11.1 us -> 13 us  [shards(): other = lax.ppermute(sums, *stage)]
    ppermute x5, starting transfers between devices: 6.24 us -> 4.84 us  [shards(): other = lax.ppermute(sums, *stage)]
    ppermute x1, waiting for transfers between devices: 0.83 us -> 0.01 us  [shards(): in_flight = lax.ppermute(half, *tap_stages[0])]
  transfers between devices with their start and end apart: 19 -> 19, of which waited for: 12 -> 13; matrix products, arithmetic and copies ran while one was open for 0% -> 0% of each run, Pallas kernels for 23% -> 23%
where the time goes in v7:
time: 78.9 us; the launch traced here: 78.6 us
  starting transfers between devices  26.1 us (33%)
  Pallas kernels  25.9 us (33%)
  waiting for transfers between devices  23.6 us (30%)
  local copies, waits for them, and re-layouts  1.25 us (2%)
  other arithmetic  0.93 us (1%)
  between operations  0.9 us (1%)
    pallas_call x21, Pallas kernels, run(): pl.pallas_call(kernel, out_shape=out_shapes, in_specs=[VMEM_SPEC] * count...  25.9 us
    ppermute x5, waiting for transfers between devices, shards(): other = lax.ppermute(sums, *stage)  13 us
    ppermute x5, starting transfers between devices, shards(): other = lax.ppermute(stats, axis, pairs)  8.87 us
    ppermute x5, waiting for transfers between devices, shards(): other = lax.ppermute(stats, axis, pairs)  6.65 us
    ppermute x3, starting transfers between devices, swap(): lax.ppermute(part, axis, pairs)  5.81 us
    ppermute x5, starting transfers between devices, shards(): other = lax.ppermute(sums, *stage)  4.84 us
    ppermute x3, starting transfers between devices, shards(): half = add(half, lax.ppermute(half, *tap_stages[number - 1]), after=(sums,))  4.65 us
    ppermute x3, waiting for transfers between devices, swap(): lax.ppermute(part, axis, pairs)  1.9 us
  transfers between devices with their start and end apart: 19, of which 13 were waited for; matrix products, arithmetic and copies ran while one was open for 0% of the time, Pallas kernels for 23%

profile of v7, /device:TPU:0, one launch (start us, length us, event | category | flops | bytes accessed | tf_op | source)
XLA Modules:
  0.0 78.6 jit_solution(6658288075055966757)
XLA Ops:
  0.7 0.9 %slice_select_fusion = bf16[8,8,256]{2,1,0:T(8,128)(2,1)S(1)} fusion(bf16[8,256,256]{2,1,0:T(8,128)(2,1)} %bitcast.9, pred[]{:T(512)S(6)} %eq.14), kind=kLoop, calls=%fused_computation | loop fusion | flops 16384 | bytes 98305 | tf_op jit(solution)/shard_map/jit(_where)/select_n | solution.py:429
  1.5 3.0 %collective-permute-start = (bf16[8,8,256]{2,1,0:T(8,128)(2,1)S(1)}, bf16[8,8,256]{2,1,0:T(8,128)(2,1)S(1)}, u32[]{:S(2)}, u32[]{:S(2)}) collective-permute-start(bf16[8,8,256]{2,1,0:T(8,128)(2,1)S(1)} %slice_select_fusion), channel_id=1, source_target_pairs={{0,4},{4,0},{1,5},{5,1},{2,6},{6,2},{3,7},{7,3},{8,12},{12,8},{9,1... | collective-permute-start | bytes 98312 | tf_op jit(solution)/shard_map/ppermute | solution.py:406
  4.5 1.9 %collective-permute-done = bf16[8,8,256]{2,1,0:T(8,128)(2,1)S(1)} collective-permute-done((bf16[8,8,256]{2,1,0:T(8,128)(2,1)S(1)}, bf16[8,8,256]{2,1,0:T(8,128)(2,1)S(1)}, u32[]{:S(2)}, u32[]{:S(2)}) %collective-permute-start) | collective-permute-done | bytes 32800 | tf_op jit(solution)/shard_map/ppermute | solution.py:406
  6.4 0.0 copy-start.1
  6.4 1.2 %copy-done.1 = bf16[1,8,256,256]{3,2,1,0:T(8,128)(2,1)S(1)} copy-done((bf16[1,8,256,256]{3,2,1,0:T(8,128)(2,1)S(1)}, bf16[1,8,256,256]{3,2,1,0:T(8,128)(2,1)}, u32[]{:S(2)}) %copy-start.1) | copy-done | bytes 1048600
  7.6 0.4 shard_map.84
  8.0 2.1 %collective-permute-start.1 = (bf16[6,272,256]{2,1,0:T(8,128)(2,1)S(1)}, bf16[6,272,256]{2,1,0:T(8,128)(2,1)S(1)}, u32[]{:S(2)}, u32[]{:S(2)}) collective-permute-start(bf16[6,272,256]{2,1,0:T(8,128)(2,1)S(1)} %get-tuple-element.29), channel_id=1, source_target_pairs={{0,8},{16,24},{8,0},{24,16},{1,9},{17,25},{9,1},{25,17},{2,10},{18... | collective-permute-start | bytes 2506760 | tf_op jit(solution)/shard_map/ppermute | solution.py:406
  10.2 0.7 collective-permute-start.2
  10.9 3.0 %shard_map.85.refs_0_ = f32[72,256]{1,0:T(8,128)S(1)} custom-call(bf16[8,256,256]{2,1,0:T(8,128)(2,1)S(1)} %bitcast.5, f32[8,128]{1,0:T(8,128)S(1)} %get-tuple-element.31.refs_1_), custom_call_target="tpu_custom_call" | custom-call | tf_op jit(solution)/shard_map/pallas_call | solution.py:31
  13.9 0.1 collective-permute-start.3
  14.0 1.3 %collective-permute-done.3.refs_1_ = f32[72,256]{1,0:T(8,128)S(1)} collective-permute-done((f32[72,256]{1,0:T(8,128)S(1)}, f32[72,256]{1,0:T(8,128)S(1)}, u32[]{:S(2)}, u32[]{:S(2)}) %collective-permute-start.3) | collective-permute-done | bytes 73760 | tf_op jit(solution)/shard_map/ppermute | solution.py:440
  15.3 1.6 %collective-permute-start.4 = (f32[72,256]{1,0:T(8,128)S(1)}, f32[72,256]{1,0:T(8,128)S(1)}, u32[]{:S(2)}, u32[]{:S(2)}) collective-permute-start(f32[72,256]{1,0:T(8,128)S(1)} %shard_map.86.refs_0_), channel_id=1, source_target_pairs={{0,2},{1,3},{2,0},{3,1},{4,6},{5,7},{6,4},{7,5},{8,10},{9,11},{10,... | collective-permute-start | bytes 221192 | tf_op jit(solution)/shard_map/ppermute | solution.py:440
  16.8 2.9 %collective-permute-done.4.refs_1_ = f32[72,256]{1,0:T(8,128)S(1)} collective-permute-done((f32[72,256]{1,0:T(8,128)S(1)}, f32[72,256]{1,0:T(8,128)S(1)}, u32[]{:S(2)}, u32[]{:S(2)}) %collective-permute-start.4) | collective-permute-done | bytes 73760 | tf_op jit(solution)/shard_map/ppermute | solution.py:440
  19.7 1.6 %collective-permute-start.5 = (f32[72,256]{1,0:T(8,128)S(1)}, f32[72,256]{1,0:T(8,128)S(1)}, u32[]{:S(2)}, u32[]{:S(2)}) collective-permute-start(f32[72,256]{1,0:T(8,128)S(1)} %shard_map.87.refs_4_.refs_0_), channel_id=1, source_target_pairs={{0,4},{4,0},{1,5},{5,1},{2,6},{6,2},{3,7},{7,3},{8,12},{12,8},{9,1... | collective-permute-start | bytes 221192 | tf_op jit(solution)/shard_map/ppermute | solution.py:440
  21.3 0.8 shard_map.88
  22.1 2.0 %collective-permute-done.5.refs_1_ = f32[72,256]{1,0:T(8,128)S(1)} collective-permute-done((f32[72,256]{1,0:T(8,128)S(1)}, f32[72,256]{1,0:T(8,128)S(1)}, u32[]{:S(2)}, u32[]{:S(2)}) %collective-permute-start.5) | collective-permute-done | bytes 73760 | tf_op jit(solution)/shard_map/ppermute | solution.py:440
  24.1 4.4 %collective-permute-start.6 = (f32[72,256]{1,0:T(8,128)S(1)}, f32[72,256]{1,0:T(8,128)S(1)}, u32[]{:S(2)}, u32[]{:S(2)}) collective-permute-start(f32[72,256]{1,0:T(8,128)S(1)} %shard_map.89.refs_2_.refs_0_), channel_id=1, source_target_pairs={{0,8},{8,0},{16,24},{24,16},{1,9},{9,1},{17,25},{25,17},{2,10},{10... | collective-permute-start | bytes 221192 | tf_op jit(solution)/shard_map/ppermute | solution.py:440
  28.5 2.6 %shard_map.90 = (f32[8,256,256]{2,1,0:T(8,128)S(1)}, f32[8,128]{1,0:T(8,128)S(1)}) custom-call(bf16[3,8,256,256]{3,2,1,0:T(8,128)(2,1)S(1)} %get-tuple-element.33.refs_0_.refs_1_, bf16[9,256,256]{2,1,0:T(8,128)(2,1)S(1)} %get-tuple-element.32.refs_1_.refs_3_, f32[72,256]{1,0:T(8,128)S(1)} %shard_map.89.refs_2_.refs_0_), custom_call_target="tpu_custom_call" | custom-call | tf_op jit(solution)/shard_map/pallas_call | solution.py:31
  31.1 0.0 collective-permute-done.6.refs_1_
  31.2 1.2 %collective-permute-start.7 = (f32[72,256]{1,0:T(8,128)S(1)}, f32[72,256]{1,0:T(8,128)S(1)}, u32[]{:S(2)}, u32[]{:S(2)}) collective-permute-start(f32[72,256]{1,0:T(8,128)S(1)} %shard_map.91.refs_5_.refs_0_), channel_id=1, source_target_pairs={{0,16},{8,24},{16,0},{24,8},{1,17},{9,25},{17,1},{25,9},{2,18},{10... | collective-permute-start | bytes 221192 | tf_op jit(solution)/shard_map/ppermute | solution.py:440
  32.4 0.0 copy-start.5
  32.4 3.5 %shard_map.92 = (bf16[3,12,256,256]{3,2,1,0:T(8,128)(2,1)S(1)}, f32[8,256,256]{2,1,0:T(8,128)S(1)}, f32[8,128]{1,0:T(8,128)S(1)}) custom-call(f32[8,256]{1,0:T(8,128)S(1)} %broadcast_in_dim.10.refs_3_.refs_0_, bf16[6,272,256]{2,1,0:T(8,128)(2,1)S(1)} %collective-permute-done.1.refs_1_, bf16[6,272,256]{2,1,0:T(8,128)(2,1)S(1)} %collective-permute-done.2.refs_2_, ...), custom_call_target="tpu_custom_call" | custom-call | tf_op jit(solution)/shard_map/pallas_call | solution.py:31
  36.0 0.5 collective-permute-done.7.refs_1_
  36.6 3.3 %shard_map.94 = (bf16[256,2048]{1,0:T(8,128)(2,1)S(1)}, f32[8,256,256]{2,1,0:T(8,128)S(1)}, f32[5,3,32,256]{3,2,1,0:T(8,128)S(1)}, f32[8,256]{1,0:T(8,128)S(1)}) custom-call(bf16[8,256,256]{2,1,0:T(8,128)(2,1)S(1)} %bitcast.6, f32[72,256]{1,0:T(8,128)S(1)} %shard_map.93.refs_1_, f32[8,256]{1,0:T(8,128)S(1)} %broadcast_in_dim.24.refs_2_.refs_5_, ...), custom_call_target="tpu_custom_call" | custom-call | tf_op jit(solution)/shard_map/pallas_call | solution.py:31
  39.8 3.0 %shard_map.95 = (f32[144,256]{1,0:T(8,128)S(1)}, f32[144,256]{1,0:T(8,128)S(1)}) custom-call(bf16[256,2048]{1,0:T(8,128)(2,1)S(1)} %get-tuple-element.42.refs_0_, bf16[3,8,256,256]{3,2,1,0:T(8,128)(2,1)S(1)} %get-tuple-element.33.refs_0_.refs_1_, bf16[3,12,256,256]{3,2,1,0:T(8,128)(2,1)S(1)} %get-tuple-element.43.refs_2_, ...), custom_call_target="tpu_custom_call" | custom-call | tf_op jit(solution)/shard_map/pallas_call | solution.py:31
  42.8 0.1 collective-permute-start.8
  42.9 1.4 %collective-permute-done.8 = f32[144,256]{1,0:T(8,128)S(1)} collective-permute-done((f32[144,256]{1,0:T(8,128)S(1)}, f32[144,256]{1,0:T(8,128)S(1)}, u32[]{:S(2)}, u32[]{:S(2)}) %collective-permute-start.8) | collective-permute-done | bytes 147488 | tf_op jit(solution)/shard_map/ppermute | solution.py:481
  44.3 1.8 %collective-permute-start.14 = (f32[144,256]{1,0:T(8,128)S(1)}, f32[144,256]{1,0:T(8,128)S(1)}, u32[]{:S(2)}, u32[]{:S(2)}) collective-permute-start(f32[144,256]{1,0:T(8,128)S(1)} %add.28.refs_6_.refs_0_), channel_id=1, source_target_pairs={{0,8},{8,0},{16,24},{24,16},{1,9},{9,1},{17,25},{25,17},{2,10},{10... | collective-permute-start | bytes 442376 | tf_op jit(solution)/shard_map/ppermute | solution.py:491
  46.1 3.3 %shard_map.96 = (f32[8,256,256]{2,1,0:T(8,128)S(1)}, f32[40,256]{1,0:T(8,128)S(1)}) custom-call(bf16[8,256,256]{2,1,0:T(8,128)(2,1)S(1)} %bitcast.7, f32[8,256,256]{2,1,0:T(8,128)S(1)} %get-tuple-element.37.refs_1_, f32[8,256,256]{2,1,0:T(8,128)S(1)} %get-tuple-element.39.refs_2_, f32[5,3,32,256]{3,2,1,0:T(8,128)S(1)} %get-tuple-element.40.refs_3_.refs_0_, ...), custom_call_target="tpu_custom_call" | custom-call | tf_op jit(solution)/shard_map/pallas_call | solution.py:31
  49.4 0.1 collective-permute-start.9
  49.5 1.2 %collective-permute-done.9 = f32[40,256]{1,0:T(8,128)S(1)} collective-permute-done((f32[40,256]{1,0:T(8,128)S(1)}, f32[40,256]{1,0:T(8,128)S(1)}, u32[]{:S(2)}, u32[]{:S(2)}) %collective-permute-start.9) | collective-permute-done | bytes 40992 | tf_op jit(solution)/shard_map/ppermute | solution.py:493
  50.8 1.5 %collective-permute-start.15 = (f32[144,256]{1,0:T(8,128)S(1)}, f32[144,256]{1,0:T(8,128)S(1)}, u32[]{:S(2)}, u32[]{:S(2)}) collective-permute-start(f32[144,256]{1,0:T(8,128)S(1)} %shard_map.99.refs_0_), channel_id=1, source_target_pairs={{0,16},{8,24},{16,0},{24,8},{1,17},{9,25},{17,1},{25,9},{2,18},{10... | collective-permute-start | bytes 442376 | tf_op jit(solution)/shard_map/ppermute | solution.py:506
  52.3 1.5 %collective-permute-start.10 = (f32[40,256]{1,0:T(8,128)S(1)}, f32[40,256]{1,0:T(8,128)S(1)}, u32[]{:S(2)}, u32[]{:S(2)}) collective-permute-start(f32[40,256]{1,0:T(8,128)S(1)} %add.29.refs_2_), channel_id=1, source_target_pairs={{0,2},{1,3},{2,0},{3,1},{4,6},{5,7},{6,4},{7,5},{8,10},{9,11},{10,... | collective-permute-start | bytes 122888 | tf_op jit(solution)/shard_map/ppermute | solution.py:493
  53.8 2.5 %collective-permute-done.10 = f32[40,256]{1,0:T(8,128)S(1)} collective-permute-done((f32[40,256]{1,0:T(8,128)S(1)}, f32[40,256]{1,0:T(8,128)S(1)}, u32[]{:S(2)}, u32[]{:S(2)}) %collective-permute-start.10) | collective-permute-done | bytes 40992 | tf_op jit(solution)/shard_map/ppermute | solution.py:493
  56.3 1.5 %collective-permute-start.11 = (f32[40,256]{1,0:T(8,128)S(1)}, f32[40,256]{1,0:T(8,128)S(1)}, u32[]{:S(2)}, u32[]{:S(2)}) collective-permute-start(f32[40,256]{1,0:T(8,128)S(1)} %add.30), channel_id=1, source_target_pairs={{0,4},{4,0},{1,5},{5,1},{2,6},{6,2},{3,7},{7,3},{8,12},{12,8},{9,1... | collective-permute-start | bytes 122888 | tf_op jit(solution)/shard_map/ppermute | solution.py:493
  57.8 2.5 %collective-permute-done.11 = f32[40,256]{1,0:T(8,128)S(1)} collective-permute-done((f32[40,256]{1,0:T(8,128)S(1)}, f32[40,256]{1,0:T(8,128)S(1)}, u32[]{:S(2)}, u32[]{:S(2)}) %collective-permute-start.11) | collective-permute-done | bytes 40992 | tf_op jit(solution)/shard_map/ppermute | solution.py:493
  60.3 0.4 collective-permute-done.15.refs_1_
  60.7 1.6 %collective-permute-start.16 = (f32[144,256]{1,0:T(8,128)S(1)}, f32[144,256]{1,0:T(8,128)S(1)}, u32[]{:S(2)}, u32[]{:S(2)}) collective-permute-start(f32[144,256]{1,0:T(8,128)S(1)} %shard_map.100.refs_0_), channel_id=1, source_target_pairs={{0,2},{1,3},{2,0},{3,1},{4,6},{5,7},{6,4},{7,5},{8,10},{9,11},{10,... | collective-permute-start | bytes 442376 | tf_op jit(solution)/shard_map/ppermute | solution.py:506
  62.2 0.9 %collective-permute-start.12 = (f32[40,256]{1,0:T(8,128)S(1)}, f32[40,256]{1,0:T(8,128)S(1)}, u32[]{:S(2)}, u32[]{:S(2)}) collective-permute-start(f32[40,256]{1,0:T(8,128)S(1)} %add.31.refs_2_), channel_id=1, source_target_pairs={{0,8},{8,0},{16,24},{24,16},{1,9},{9,1},{17,25},{25,17},{2,10},{10... | collective-permute-start | bytes 122888 | tf_op jit(solution)/shard_map/ppermute | solution.py:493
  63.1 3.1 %collective-permute-done.12 = f32[40,256]{1,0:T(8,128)S(1)} collective-permute-done((f32[40,256]{1,0:T(8,128)S(1)}, f32[40,256]{1,0:T(8,128)S(1)}, u32[]{:S(2)}, u32[]{:S(2)}) %collective-permute-start.12) | collective-permute-done | bytes 40992 | tf_op jit(solution)/shard_map/ppermute | solution.py:493
  66.2 0.3 collective-permute-done.16.refs_1_
  66.6 1.6 %collective-permute-start.17 = (f32[144,256]{1,0:T(8,128)S(1)}, f32[144,256]{1,0:T(8,128)S(1)}, u32[]{:S(2)}, u32[]{:S(2)}) collective-permute-start(f32[144,256]{1,0:T(8,128)S(1)} %shard_map.101.refs_0_), channel_id=1, source_target_pairs={{0,4},{4,0},{1,5},{5,1},{2,6},{6,2},{3,7},{7,3},{8,12},{12,8},{9,1... | collective-permute-start | bytes 442376 | tf_op jit(solution)/shard_map/ppermute | solution.py:506
  68.1 0.9 %collective-permute-start.13 = (f32[40,256]{1,0:T(8,128)S(1)}, f32[40,256]{1,0:T(8,128)S(1)}, u32[]{:S(2)}, u32[]{:S(2)}) collective-permute-start(f32[40,256]{1,0:T(8,128)S(1)} %add.32.refs_3_.refs_0_.refs_2_), channel_id=1, source_target_pairs={{0,16},{8,24},{16,0},{24,8},{1,17},{9,25},{17,1},{25,9},{2,18},{10... | collective-permute-start | bytes 122888 | tf_op jit(solution)/shard_map/ppermute | solution.py:493
  69.0 0.8 shard_map.97
  69.8 3.7 %collective-permute-done.13.refs_1_ = f32[40,256]{1,0:T(8,128)S(1)} collective-permute-done((f32[40,256]{1,0:T(8,128)S(1)}, f32[40,256]{1,0:T(8,128)S(1)}, u32[]{:S(2)}, u32[]{:S(2)}) %collective-permute-start.13) | collective-permute-done | bytes 40992 | tf_op jit(solution)/shard_map/ppermute | solution.py:493
  73.5 0.1 collective-permute-start.18
  73.6 4.3 %shard_map.103 = (bf16[8,256,256]{2,1,0:T(8,128)(2,1)}, f32[256]{0:T(256)}, f32[256]{0:T(256)}) custom-call(bf16[8,256,256]{2,1,0:T(8,128)(2,1)S(1)} %bitcast.8, f32[8,256,256]{2,1,0:T(8,128)S(1)} %get-tuple-element.46.refs_1_, f32[40,256]{1,0:T(8,128)S(1)} %shard_map.98.refs_2_, bf16[9,2,256,256]{3,2,1,0:T(8,128)(2,1)S(1)} %get-tuple-element.49.refs_3_, ...), custom_call_target="tpu_custom_call" | custom-call | tf_op jit(solution)/shard_map/pallas_call | solution.py:31
  77.9 0.8 shard_map.104
  (34 shorter events, 0.3 us)
Async XLA Ops:
  0.6 10.3 %copy-start = (bf16[1,8,256,256]{3,2,1,0:T(8,128)(2,1)S(1)}, bf16[1,8,256,256]{3,2,1,0:T(8,128)(2,1)}, u32[]{:S(2)}) copy-start(bf16[1,8,256,256]{3,2,1,0:T(8,128)(2,1)} %param.5) | copy-start | bytes 3145732
  1.5 4.9 %collective-permute-start = (bf16[8,8,256]{2,1,0:T(8,128)(2,1)S(1)}, bf16[8,8,256]{2,1,0:T(8,128)(2,1)S(1)}, u32[]{:S(2)}, u32[]{:S(2)}) collective-permute-start(bf16[8,8,256]{2,1,0:T(8,128)(2,1)S(1)} %slice_select_fusion), channel_id=1, source_target_pairs={{0,4},{4,0},{1,5},{5,1},{2,6},{6,2},{3,7},{7,3},{8,12},{12,8},{9,1... | collective-permute-start | bytes 98312 | tf_op jit(solution)/shard_map/ppermute | solution.py:406
  6.4 1.2 %copy-start.1 = (bf16[1,8,256,256]{3,2,1,0:T(8,128)(2,1)S(1)}, bf16[1,8,256,256]{3,2,1,0:T(8,128)(2,1)}, u32[]{:S(2)}) copy-start(bf16[1,8,256,256]{3,2,1,0:T(8,128)(2,1)} %param.6) | copy-start | bytes 3145732
  7.6 13.6 %copy-start.2 = (bf16[1,8,256,256]{3,2,1,0:T(8,128)(2,1)S(1)}, bf16[1,8,256,256]{3,2,1,0:T(8,128)(2,1)}, u32[]{:S(2)}) copy-start(bf16[1,8,256,256]{3,2,1,0:T(8,128)(2,1)} %param.6) | copy-start | bytes 3145732
  7.6 13.6 %copy-start.3 = (bf16[3,3,32,256]{3,2,1,0:T(8,128)(2,1)S(1)}, bf16[3,3,32,256]{3,2,1,0:T(8,128)(2,1)}, u32[]{:S(2)}) copy-start(bf16[3,3,32,256]{3,2,1,0:T(8,128)(2,1)} %param.7) | copy-start | bytes 442372
  8.0 24.4 %collective-permute-start.1 = (bf16[6,272,256]{2,1,0:T(8,128)(2,1)S(1)}, bf16[6,272,256]{2,1,0:T(8,128)(2,1)S(1)}, u32[]{:S(2)}, u32[]{:S(2)}) collective-permute-start(bf16[6,272,256]{2,1,0:T(8,128)(2,1)S(1)} %get-tuple-element.29), channel_id=1, source_target_pairs={{0,8},{16,24},{8,0},{24,16},{1,9},{17,25},{9,1},{25,17},{2,10},{18... | collective-permute-start | bytes 2506760 | tf_op jit(solution)/shard_map/ppermute | solution.py:406
  10.2 22.2 %collective-permute-start.2 = (bf16[6,272,256]{2,1,0:T(8,128)(2,1)S(1)}, bf16[6,272,256]{2,1,0:T(8,128)(2,1)S(1)}, u32[]{:S(2)}, u32[]{:S(2)}) collective-permute-start(bf16[6,272,256]{2,1,0:T(8,128)(2,1)S(1)} %get-tuple-element.30), channel_id=1, source_target_pairs={{8,16},{16,8},{9,17},{17,9},{10,18},{18,10},{11,19},{19,11},{12,20... | collective-permute-start | bytes 2506760 | tf_op jit(solution)/shard_map/ppermute | solution.py:406
  13.9 1.3 %collective-permute-start.3 = (f32[72,256]{1,0:T(8,128)S(1)}, f32[72,256]{1,0:T(8,128)S(1)}, u32[]{:S(2)}, u32[]{:S(2)}) collective-permute-start(f32[72,256]{1,0:T(8,128)S(1)} %shard_map.85.refs_0_), channel_id=1, source_target_pairs={{0,1},{1,0},{2,3},{3,2},{4,5},{5,4},{6,7},{7,6},{8,9},{9,8},{10,11... | collective-permute-start | bytes 221192 | tf_op jit(solution)/shard_map/ppermute | solution.py:440
  15.3 4.4 %collective-permute-start.4 = (f32[72,256]{1,0:T(8,128)S(1)}, f32[72,256]{1,0:T(8,128)S(1)}, u32[]{:S(2)}, u32[]{:S(2)}) collective-permute-start(f32[72,256]{1,0:T(8,128)S(1)} %shard_map.86.refs_0_), channel_id=1, source_target_pairs={{0,2},{1,3},{2,0},{3,1},{4,6},{5,7},{6,4},{7,5},{8,10},{9,11},{10,... | collective-permute-start | bytes 221192 | tf_op jit(solution)/shard_map/ppermute | solution.py:440
  19.7 4.4 %collective-permute-start.5 = (f32[72,256]{1,0:T(8,128)S(1)}, f32[72,256]{1,0:T(8,128)S(1)}, u32[]{:S(2)}, u32[]{:S(2)}) collective-permute-start(f32[72,256]{1,0:T(8,128)S(1)} %shard_map.87.refs_4_.refs_0_), channel_id=1, source_target_pairs={{0,4},{4,0},{1,5},{5,1},{2,6},{6,2},{3,7},{7,3},{8,12},{12,8},{9,1... | collective-permute-start | bytes 221192 | tf_op jit(solution)/shard_map/ppermute | solution.py:440
  24.1 7.0 %collective-permute-start.6 = (f32[72,256]{1,0:T(8,128)S(1)}, f32[72,256]{1,0:T(8,128)S(1)}, u32[]{:S(2)}, u32[]{:S(2)}) collective-permute-start(f32[72,256]{1,0:T(8,128)S(1)} %shard_map.89.refs_2_.refs_0_), channel_id=1, source_target_pairs={{0,8},{8,0},{16,24},{24,16},{1,9},{9,1},{17,25},{25,17},{2,10},{10... | collective-permute-start | bytes 221192 | tf_op jit(solution)/shard_map/ppermute | solution.py:440
  31.2 5.3 %collective-permute-start.7 = (f32[72,256]{1,0:T(8,128)S(1)}, f32[72,256]{1,0:T(8,128)S(1)}, u32[]{:S(2)}, u32[]{:S(2)}) collective-permute-start(f32[72,256]{1,0:T(8,128)S(1)} %shard_map.91.refs_5_.refs_0_), channel_id=1, source_target_pairs={{0,16},{8,24},{16,0},{24,8},{1,17},{9,25},{17,1},{25,9},{2,18},{10... | collective-permute-start | bytes 221192 | tf_op jit(solution)/shard_map/ppermute | solution.py:440
  32.4 4.1 %copy-start.4 = (f32[256]{0:T(256)S(1)}, f32[256]{0:T(256)}, u32[]{:S(2)}) copy-start(f32[256]{0:T(256)} %param.8) | copy-start | bytes 3076
  32.4 4.1 %copy-start.5 = (f32[256]{0:T(256)S(1)}, f32[256]{0:T(256)}, u32[]{:S(2)}) copy-start(f32[256]{0:T(256)} %param.9) | copy-start | bytes 3076
  42.8 1.4 %collective-permute-start.8 = (f32[144,256]{1,0:T(8,128)S(1)}, f32[144,256]{1,0:T(8,128)S(1)}, u32[]{:S(2)}, u32[]{:S(2)}) collective-permute-start(f32[144,256]{1,0:T(8,128)S(1)} %get-tuple-element.45), channel_id=1, source_target_pairs={{0,1},{1,0},{2,3},{3,2},{4,5},{5,4},{6,7},{7,6},{8,9},{9,8},{10,11... | collective-permute-start | bytes 442376 | tf_op jit(solution)/shard_map/ppermute | solution.py:481
  44.3 6.4 %collective-permute-start.14 = (f32[144,256]{1,0:T(8,128)S(1)}, f32[144,256]{1,0:T(8,128)S(1)}, u32[]{:S(2)}, u32[]{:S(2)}) collective-permute-start(f32[144,256]{1,0:T(8,128)S(1)} %add.28.refs_6_.refs_0_), channel_id=1, source_target_pairs={{0,8},{8,0},{16,24},{24,16},{1,9},{9,1},{17,25},{25,17},{2,10},{10... | collective-permute-start | bytes 442376 | tf_op jit(solution)/shard_map/ppermute | solution.py:491
  49.4 1.3 %collective-permute-start.9 = (f32[40,256]{1,0:T(8,128)S(1)}, f32[40,256]{1,0:T(8,128)S(1)}, u32[]{:S(2)}, u32[]{:S(2)}) collective-permute-start(f32[40,256]{1,0:T(8,128)S(1)} %get-tuple-element.47), channel_id=1, source_target_pairs={{0,1},{1,0},{2,3},{3,2},{4,5},{5,4},{6,7},{7,6},{8,9},{9,8},{10,11... | collective-permute-start | bytes 122888 | tf_op jit(solution)/shard_map/ppermute | solution.py:493
  50.8 9.9 %collective-permute-start.15 = (f32[144,256]{1,0:T(8,128)S(1)}, f32[144,256]{1,0:T(8,128)S(1)}, u32[]{:S(2)}, u32[]{:S(2)}) collective-permute-start(f32[144,256]{1,0:T(8,128)S(1)} %shard_map.99.refs_0_), channel_id=1, source_target_pairs={{0,16},{8,24},{16,0},{24,8},{1,17},{9,25},{17,1},{25,9},{2,18},{10... | collective-permute-start | bytes 442376 | tf_op jit(solution)/shard_map/ppermute | solution.py:506
  52.3 4.0 %collective-permute-start.10 = (f32[40,256]{1,0:T(8,128)S(1)}, f32[40,256]{1,0:T(8,128)S(1)}, u32[]{:S(2)}, u32[]{:S(2)}) collective-permute-start(f32[40,256]{1,0:T(8,128)S(1)} %add.29.refs_2_), channel_id=1, source_target_pairs={{0,2},{1,3},{2,0},{3,1},{4,6},{5,7},{6,4},{7,5},{8,10},{9,11},{10,... | collective-permute-start | bytes 122888 | tf_op jit(solution)/shard_map/ppermute | solution.py:493
  56.3 4.0 %collective-permute-start.11 = (f32[40,256]{1,0:T(8,128)S(1)}, f32[40,256]{1,0:T(8,128)S(1)}, u32[]{:S(2)}, u32[]{:S(2)}) collective-permute-start(f32[40,256]{1,0:T(8,128)S(1)} %add.30), channel_id=1, source_target_pairs={{0,4},{4,0},{1,5},{5,1},{2,6},{6,2},{3,7},{7,3},{8,12},{12,8},{9,1... | collective-permute-start | bytes 122888 | tf_op jit(solution)/shard_map/ppermute | solution.py:493
  60.7 5.9 %collective-permute-start.16 = (f32[144,256]{1,0:T(8,128)S(1)}, f32[144,256]{1,0:T(8,128)S(1)}, u32[]{:S(2)}, u32[]{:S(2)}) collective-permute-start(f32[144,256]{1,0:T(8,128)S(1)} %shard_map.100.refs_0_), channel_id=1, source_target_pairs={{0,2},{1,3},{2,0},{3,1},{4,6},{5,7},{6,4},{7,5},{8,10},{9,11},{10,... | collective-permute-start | bytes 442376 | tf_op jit(solution)/shard_map/ppermute | solution.py:506
  62.2 4.0 %collective-permute-start.12 = (f32[40,256]{1,0:T(8,128)S(1)}, f32[40,256]{1,0:T(8,128)S(1)}, u32[]{:S(2)}, u32[]{:S(2)}) collective-permute-start(f32[40,256]{1,0:T(8,128)S(1)} %add.31.refs_2_), channel_id=1, source_target_pairs={{0,8},{8,0},{16,24},{24,16},{1,9},{9,1},{17,25},{25,17},{2,10},{10... | collective-permute-start | bytes 122888 | tf_op jit(solution)/shard_map/ppermute | solution.py:493
  66.6 6.9 %collective-permute-start.17 = (f32[144,256]{1,0:T(8,128)S(1)}, f32[144,256]{1,0:T(8,128)S(1)}, u32[]{:S(2)}, u32[]{:S(2)}) collective-permute-start(f32[144,256]{1,0:T(8,128)S(1)} %shard_map.101.refs_0_), channel_id=1, source_target_pairs={{0,4},{4,0},{1,5},{5,1},{2,6},{6,2},{3,7},{7,3},{8,12},{12,8},{9,1... | collective-permute-start | bytes 442376 | tf_op jit(solution)/shard_map/ppermute | solution.py:506
  68.1 5.3 %collective-permute-start.13 = (f32[40,256]{1,0:T(8,128)S(1)}, f32[40,256]{1,0:T(8,128)S(1)}, u32[]{:S(2)}, u32[]{:S(2)}) collective-permute-start(f32[40,256]{1,0:T(8,128)S(1)} %add.32.refs_3_.refs_0_.refs_2_), channel_id=1, source_target_pairs={{0,16},{8,24},{16,0},{24,8},{1,17},{9,25},{17,1},{25,9},{2,18},{10... | collective-permute-start | bytes 122888 | tf_op jit(solution)/shard_map/ppermute | solution.py:493
  73.5 4.4 %collective-permute-start.18 = (f32[144,256]{1,0:T(8,128)S(1)}, f32[144,256]{1,0:T(8,128)S(1)}, u32[]{:S(2)}, u32[]{:S(2)}) collective-permute-start(f32[144,256]{1,0:T(8,128)S(1)} %shard_map.102.refs_5_.refs_0_), channel_id=1, source_target_pairs={{0,1},{1,0},{2,3},{3,2},{4,5},{5,4},{6,7},{7,6},{8,9},{9,8},{10,11... | collective-permute-start | bytes 442376 | tf_op jit(solution)/shard_map/ppermute | solution.py:513
